TPU v7x, 32 devices: a whole 2x2x4 slice. The times are simulated.
32 devices in a mesh: dp: 8 (over z, y), row: 2 (over x), col: 2 (over core).
Axes of the slice: x: 2, y: 2, z: 4, core: 2. Of those that a mesh axis runs over, the one named last changes fastest.
Arguments:
- tokens: bfloat16 [4096, 2048], P('dp', ('row', 'col')), may hold values from -6 to 6
- norm_first: float32 [2048], P(('row', 'col')), may hold values from 0.5 to 1.5
- mixer_in: bfloat16 [2048, 6144], P('row', 'col'), may hold values from -0.125 to 0.125
- query_weight: bfloat16 [2048, 1024], P('row', 'col'), may hold values from -0.125 to 0.125
- bc_weight: bfloat16 [2048, 512], P('row'), may hold values from -0.125 to 0.125
- step_weight: bfloat16 [2048, 48], P('row'), may hold values from -0.125 to 0.125
- kv_weight: bfloat16 [2048, 2, 256], P('row', 'col'), may hold values from -0.125 to 0.125
- conv_inner: float32 [4, 3072], P(None, ('col', 'row')), may hold values from -3 to 3
- conv_shared: float32 [4, 512], replicated, may hold values from -3 to 3
- log_rate: float32 [48], P(('col', 'row')), may hold values from -1 to 2.5
- step_bias: float32 [48], P(('col', 'row')), may hold values from -4 to -1
- skip_gain: float32 [48], P(('col', 'row')), may hold values from 0.5 to 1.5
- group_gain: float32 [3072], P(('col', 'row')), may hold values from 0.5 to 1.5
- out_weight: bfloat16 [4096, 2048], P('col', 'row'), may hold values from -1 to 1
- norm_second: float32 [2048], P(('row', 'col')), may hold values from 0.5 to 1.5
- gate_weight: bfloat16 [2048, 4096], P('row', 'col'), may hold values from -0.125 to 0.125
- up_weight: bfloat16 [2048, 4096], P('row', 'col'), may hold values from -0.125 to 0.125
- down_weight: bfloat16 [4096, 2048], P('col', 'row'), may hold values from -0.09375 to 0.09375
- cotangent: bfloat16 [4096, 2048], P('dp', ('row', 'col')), may hold values from -6 to 6
Outputs:
- layer_out: bfloat16 [4096, 2048], P('dp', ('row', 'col'))
- tokens_grad: float32 [4096, 2048], P('dp', ('row', 'col'))
- norm_first_grad: float32 [2048], P(('row', 'col', 'dp'))
- mixer_in_grad: float32 [2048, 6144], P(('row', 'dp'), 'col')
- query_weight_grad: float32 [2048, 1024], P(('row', 'dp'), 'col')
- bc_weight_grad: float32 [2048, 512], P(('row', 'dp'))
- step_weight_grad: float32 [2048, 48], P(('row', 'dp'))
- kv_weight_grad: float32 [2048, 2, 256], P(('row', 'dp'), 'col')
- conv_inner_grad: float32 [4, 3072], P(None, ('col', 'row', 'dp'))
- conv_shared_grad: float32 [4, 512], P(None, 'dp')
- log_rate_grad: float32 [48], P(('col', 'row'))
- step_bias_grad: float32 [48], P(('col', 'row'))
- skip_gain_grad: float32 [48], P(('col', 'row'))
- group_gain_grad: float32 [3072], P(('col', 'row', 'dp'))
- out_weight_grad: float32 [4096, 2048], P(('col', 'dp'), 'row')
- norm_second_grad: float32 [2048], P(('row', 'col', 'dp'))
- gate_weight_grad: float32 [2048, 4096], P(('row', 'dp'), 'col')
- up_weight_grad: float32 [2048, 4096], P(('row', 'dp'), 'col')
- down_weight_grad: float32 [4096, 2048], P(('col', 'dp'), 'row')
All inputs are finite; a program needn't handle non-finite values.
Results may differ from a plain program's by a relative error of at most 0.023.
Values may be sent and summed in bfloat16 or wider, within the bound.
No kernel may reach another device: no remote copies, remote signals or barrier semaphores. Data moves between devices by JAX's collectives and lax.ppermute only.
A program may use at most 256 MiB of HBM per device.

v0:
```python
from functools import partial
import math

import jax
import jax.numpy as jnp
from jax import lax
from jax.sharding import PartitionSpec as P

D = 2048
HM = 48
PM = 64
KV = 2
HD = 128
SCAN_BLOCK = 256


norm_epsilon = 1e-05
rope_base = 10000.0
highest = lax.Precision.HIGHEST


def round_keep(values_in):
    rounded = values_in.astype(jnp.bfloat16).astype(jnp.float32)
    return values_in + lax.stop_gradient(rounded - values_in)


def causal_conv(signal, tap_weights):
    tap_count = tap_weights.shape[0]
    length = signal.shape[0]
    padded = jnp.pad(signal, ((tap_count - 1, 0), (0, 0)))
    running_sum = jnp.zeros_like(signal)
    for offset in range(tap_count):
        running_sum = running_sum + tap_weights[offset] * padded[offset : offset + length]
    return running_sum


def rotate(rotated_in):
    length = rotated_in.shape[0]
    half_width = rotated_in.shape[2] // 2
    inverse = rope_base ** (-jnp.arange(half_width, dtype=jnp.float32) * 2.0 / rotated_in.shape[2])
    angles = jnp.arange(length, dtype=jnp.float32)[:, None] * inverse[None, :]
    cosine = jnp.cos(angles)[:, None, :]
    sine_part = jnp.sin(angles)[:, None, :]
    front_part = rotated_in[..., :half_width]
    back_part = rotated_in[..., half_width:]
    return jnp.concatenate(
        [front_part * cosine - back_part * sine_part, back_part * cosine + front_part * sine_part],
        axis=-1,
    )


def mixer_core(
    mix_sum,
    query_sum,
    shared_sum,
    step_raw,
    pair_sum,
    conv_inner,
    conv_shared,
    log_rate,
    step_bias,
    skip_gain,
    quantize,
):
    length = mix_sum.shape[0]
    head_count = log_rate.shape[0]
    state_dim = shared_sum.shape[1] // 2
    head_width = mix_sum.shape[1] // (2 * head_count)
    head_pairs = mix_sum.reshape(length, head_count, 2, head_width)
    gate_part = head_pairs[:, :, 0, :]
    inner_seq = jax.nn.silu(
        causal_conv(head_pairs[:, :, 1, :].reshape(length, head_count * head_width), conv_inner)
    )
    inner_seq = inner_seq.reshape(length, head_count, head_width)
    shared = jax.nn.silu(causal_conv(shared_sum, conv_shared))
    bmatrix = shared[:, :state_dim]
    cmatrix = shared[:, state_dim:]
    step_size = jax.nn.softplus(step_raw + step_bias)
    log_decay = -jnp.exp(log_rate) * step_size
    block_count = length // SCAN_BLOCK
    lower_mask = jnp.tril(jnp.ones((SCAN_BLOCK, SCAN_BLOCK), jnp.float32))[:, :, None]

    def state_block(carry_state, block_inputs):
        inner_block, basis_block, read_block, step_block, decay_block = block_inputs
        running = jnp.cumsum(decay_block, axis=0)
        gram_block = jnp.dot(read_block, basis_block.T, precision=highest)
        spread = jnp.exp(jnp.minimum(running[:, None, :] - running[None, :, :], 0.0)) * lower_mask
        mixing = gram_block[:, :, None] * spread * step_block[None, :, :]
        within = jnp.einsum("tsh,shp->thp", mixing, inner_block, precision=highest)
        carried = (
            jnp.einsum("hpn,tn->thp", carry_state, read_block, precision=highest)
            * jnp.exp(running)[:, :, None]
        )
        tail_weight = jnp.exp(running[-1][None, :] - running) * step_block
        fresh_state = jnp.einsum(
            "sh,shp,sn->hpn", tail_weight, inner_block, basis_block, precision=highest
        )
        return (jnp.exp(running[-1])[:, None, None] * carry_state + fresh_state, within + carried)

    block_inputs = (
        inner_seq.reshape(block_count, SCAN_BLOCK, head_count, head_width),
        bmatrix.reshape(block_count, SCAN_BLOCK, state_dim),
        cmatrix.reshape(block_count, SCAN_BLOCK, state_dim),
        step_size.reshape(block_count, SCAN_BLOCK, head_count),
        log_decay.reshape(block_count, SCAN_BLOCK, head_count),
    )
    initial = jnp.zeros((head_count, head_width, state_dim), jnp.float32)
    final_state, outputs = lax.scan(jax.checkpoint(state_block), initial, block_inputs)
    ssm_out = outputs.reshape(length, head_count, head_width) + skip_gain[None, :, None] * inner_seq
    gated_out = (ssm_out * jax.nn.silu(gate_part)).reshape(length, head_count * head_width)
    query_heads = query_sum.shape[1] // HD
    pair_heads = pair_sum.shape[1]
    queries = quantize(rotate(query_sum.reshape(length, query_heads, HD)))
    key_heads = quantize(rotate(pair_sum[:, :, :HD]))
    value_heads = quantize(pair_sum[:, :, HD:])
    key_heads = jnp.repeat(key_heads, query_heads // pair_heads, axis=1)
    value_heads = jnp.repeat(value_heads, query_heads // pair_heads, axis=1)
    block_rows = min(512, length)
    score_scale = 1.0 / math.sqrt(HD)
    positions = jnp.arange(length, dtype=jnp.int32)

    def attend(first_row):
        scores = jnp.einsum("qhd,khd->hqk", queries, key_heads, precision=highest) * score_scale
        query_rows = first_row + jnp.arange(block_rows, dtype=jnp.int32)
        visible = positions[None, :] <= query_rows[:, None]
        scores = jnp.where(visible[None, :, :], scores, -1e30)
        exponent = jnp.exp(scores - jnp.max(scores, axis=2, keepdims=True))
        softmax_weights = quantize(exponent / jnp.sum(exponent, axis=2, keepdims=True))
        return jnp.einsum("hqk,khd->qhd", softmax_weights, value_heads, precision=highest)

    starts = jnp.arange(length // block_rows, dtype=jnp.int32) * block_rows
    attended = lax.map(jax.checkpoint(attend), starts).reshape(length, query_heads * HD)
    return (gated_out, attended)


def product(left_side, right_side):
    return jnp.dot(left_side, right_side, preferred_element_type=jnp.float32)


def product_back(left_side, right_side):
    return lax.dot_general(
        left_side, right_side, (((1,), (1,)), ((), ())), preferred_element_type=jnp.float32
    )


def outer_sum(left_side, right_side):
    return lax.dot_general(
        left_side, right_side, (((0,), (0,)), ((), ())), preferred_element_type=jnp.float32
    )


def feature_total(partial_total):
    return lax.psum(partial_total, ("row", "col"))


def gather_inputs(values_in):
    return lax.all_gather(values_in, "col", axis=1, tiled=True)


def sum_projections(first_term, second_term):
    return (
        lax.psum_scatter(first_term, "row", scatter_dimension=1, tiled=True),
        lax.psum_scatter(second_term, "row", scatter_dimension=1, tiled=True),
    )


def gather_mixed(values_in):
    return lax.all_gather(values_in, "row", axis=1, tiled=True)


def sum_outputs(values_in):
    return lax.psum_scatter(values_in, "col", scatter_dimension=1, tiled=True)


def gather_output_grads(values_in):
    return lax.all_gather(values_in, "col", axis=1, tiled=True)


def sum_mixed_grads(values_in):
    return lax.psum_scatter(
        values_in.astype(jnp.bfloat16), "row", scatter_dimension=1, tiled=True
    ).astype(jnp.float32)


def gather_projection_grads(first_term, second_term):
    return (
        lax.all_gather(first_term, "row", axis=1, tiled=True),
        lax.all_gather(second_term, "row", axis=1, tiled=True),
    )


def sum_input_grads(values_in):
    return lax.psum_scatter(
        values_in.astype(jnp.bfloat16), "col", scatter_dimension=1, tiled=True
    ).astype(jnp.float32)


def reduce_ffn(gate_grad, up_grad, down_grad, gain_grad):
    return (
        lax.psum_scatter(
            gate_grad.astype(jnp.bfloat16), "dp", scatter_dimension=0, tiled=True
        ).astype(jnp.float32),
        lax.psum_scatter(
            up_grad.astype(jnp.bfloat16), "dp", scatter_dimension=0, tiled=True
        ).astype(jnp.float32),
        lax.psum_scatter(
            down_grad.astype(jnp.bfloat16), "dp", scatter_dimension=0, tiled=True
        ).astype(jnp.float32),
        lax.psum_scatter(
            gain_grad.astype(jnp.bfloat16), "dp", scatter_dimension=0, tiled=True
        ).astype(jnp.float32),
    )


def norm_forward(residual, gain_vec, feature_count):
    square_total = feature_total(jnp.sum(residual * residual, axis=1))
    factor = lax.rsqrt(square_total / feature_count + norm_epsilon)
    return (residual * factor[:, None] * gain_vec, factor)


def norm_backward(residual, gain_vec, factor, incoming, feature_count):
    inner_total = feature_total(jnp.sum(incoming * gain_vec * residual, axis=1))
    result = (
        factor[:, None] * gain_vec * incoming
        - residual * (factor**3 * inner_total / feature_count)[:, None]
    )
    gain_grad = jnp.sum(incoming * residual * factor[:, None], axis=0)
    return (result, gain_grad)


def local(
    tokens,
    norm_first,
    mixer_in,
    query_weight,
    bc_weight,
    step_weight,
    kv_weight,
    conv_inner,
    conv_shared,
    log_rate,
    step_bias,
    skip_gain,
    group_gain,
    out_weight,
    norm_second,
    gate_weight,
    up_weight,
    down_weight,
    cotangent,
):
    seq_len = tokens.shape[0]
    row_count = lax.axis_size("row")
    col_count = lax.axis_size("col")
    col_place = lax.axis_index("col")
    quarter = col_place * row_count + lax.axis_index("row")
    head_count = log_rate.shape[0]
    kv_flat = kv_weight.reshape(kv_weight.shape[0], -1)
    residual = tokens.astype(jnp.float32)
    first_norm, first_factor = norm_forward(residual, norm_first, D)
    first_in = first_norm.astype(jnp.bfloat16)
    first_half = gather_inputs(first_in)
    mix_sum, query_sum = sum_projections(
        product(first_half, mixer_in), product(first_half, query_weight)
    )
    shared_sum, step_sum, pair_sum = lax.psum(
        (
            product(first_half, bc_weight),
            product(first_half, step_weight),
            product(first_half, kv_flat),
        ),
        "row",
    )
    step_own = lax.dynamic_slice_in_dim(step_sum, quarter * head_count, head_count, 1)
    core_local = partial(mixer_core, quantize=round_keep)
    (gated_out, attended), core_back = jax.vjp(
        core_local,
        mix_sum,
        query_sum,
        shared_sum,
        step_own,
        pair_sum.reshape(seq_len, 1, -1),
        conv_inner,
        conv_shared,
        log_rate,
        step_bias,
        skip_gain,
    )
    normed, gated_factor = norm_forward(gated_out, group_gain, HM * PM)
    group_count = attended.shape[1] // HD
    mixed_vec = jnp.concatenate(
        [normed.reshape(seq_len, group_count, -1), attended.reshape(seq_len, group_count, HD)],
        axis=2,
    )
    mixed_vec = mixed_vec.reshape(seq_len, -1).astype(jnp.bfloat16)
    mixed_half = gather_mixed(mixed_vec)
    second = residual + sum_outputs(product(mixed_half, out_weight))
    second_norm, second_factor = norm_forward(second, norm_second, D)
    second_in = second_norm.astype(jnp.bfloat16)
    second_half = gather_inputs(second_in)
    gate_sum, up_sum = sum_projections(
        product(second_half, gate_weight), product(second_half, up_weight)
    )
    gate_act = jax.nn.silu(gate_sum)
    hidden = (gate_act * up_sum).astype(jnp.bfloat16)
    hidden_half = gather_mixed(hidden)
    output = second + sum_outputs(product(hidden_half, down_weight))
    grad_half = gather_output_grads(cotangent)
    down_weight_grad = outer_sum(hidden_half, grad_half)
    hidden_grad = sum_mixed_grads(product_back(grad_half, down_weight))
    sigmoid_gate = jax.nn.sigmoid(gate_sum)
    gate_grad = (
        hidden_grad * up_sum * sigmoid_gate * (1.0 + gate_sum * (1.0 - sigmoid_gate))
    ).astype(jnp.bfloat16)
    up_grad = (hidden_grad * gate_act).astype(jnp.bfloat16)
    gate_grad_half, up_grad_half = gather_projection_grads(gate_grad, up_grad)
    gate_weight_grad = outer_sum(second_half, gate_grad_half)
    up_weight_grad = outer_sum(second_half, up_grad_half)
    second_in_grad = sum_input_grads(
        product_back(gate_grad_half, gate_weight) + product_back(up_grad_half, up_weight)
    )
    second_back, norm_second_grad = norm_backward(
        second, norm_second, second_factor, second_in_grad, D
    )
    second_grad = cotangent.astype(jnp.float32) + second_back
    branch_half = gather_output_grads(second_grad.astype(jnp.bfloat16))
    out_weight_grad = outer_sum(mixed_half, branch_half)
    mixed_grad = sum_mixed_grads(product_back(branch_half, out_weight)).reshape(
        seq_len, group_count, -1
    )
    mamba_width = normed.shape[1] // group_count
    normed_grad = mixed_grad[:, :, :mamba_width].reshape(seq_len, -1)
    attended_grad = mixed_grad[:, :, mamba_width:].reshape(seq_len, -1)
    gated_grad, group_gain_grad = norm_backward(
        gated_out, group_gain, gated_factor, normed_grad, HM * PM
    )
    (
        mix_grad,
        query_grad,
        shared_grad,
        step_grad,
        pair_grad,
        conv_inner_grad,
        conv_shared_part,
        log_rate_grad,
        step_bias_grad,
        skip_gain_grad,
    ) = core_back((gated_grad, attended_grad))
    step_padded = lax.dynamic_update_slice(
        jnp.zeros(step_sum.shape, jnp.float32), step_grad, (0, quarter * head_count)
    )
    pair_padded = lax.dynamic_update_slice(
        jnp.zeros((seq_len, KV, pair_sum.shape[1]), jnp.float32), pair_grad, (0, col_place, 0)
    )
    shared_total, step_total, pair_total, conv_shared_grad = (
        lax.psum(shared_grad.astype(jnp.bfloat16), ("row", "col")).astype(jnp.float32),
        lax.psum(step_padded.astype(jnp.bfloat16), ("row", "col")).astype(jnp.float32),
        lax.psum(pair_padded.astype(jnp.bfloat16), ("row", "col")).astype(jnp.float32),
        lax.psum(conv_shared_part.astype(jnp.bfloat16), ("row", "col")).astype(jnp.float32),
    )
    shared_low = shared_total.astype(jnp.bfloat16)
    step_low = step_total.astype(jnp.bfloat16)
    pair_low = lax.dynamic_index_in_dim(pair_total, col_place, 1, keepdims=False).astype(
        jnp.bfloat16
    )
    mix_grad_half, query_grad_half = gather_projection_grads(
        mix_grad.astype(jnp.bfloat16), query_grad.astype(jnp.bfloat16)
    )
    mixer_in_grad = outer_sum(first_half, mix_grad_half)
    query_weight_grad = outer_sum(first_half, query_grad_half)
    bc_weight_grad = outer_sum(first_half, shared_low)
    step_weight_grad = outer_sum(first_half, step_low)
    kv_weight_grad = outer_sum(first_half, pair_low).reshape(kv_weight.shape)
    repeated = (product_back(shared_low, bc_weight) + product_back(step_low, step_weight)) * (
        1.0 / col_count
    )
    first_in_grad = sum_input_grads(
        product_back(mix_grad_half, mixer_in)
        + product_back(query_grad_half, query_weight)
        + product_back(pair_low, kv_flat)
        + repeated
    )
    first_back, norm_first_grad = norm_backward(
        residual, norm_first, first_factor, first_in_grad, D
    )
    input_grad = second_grad + first_back
    ffn_sums = reduce_ffn(gate_weight_grad, up_weight_grad, down_weight_grad, norm_second_grad)
    mixer_sums = (
        lax.psum_scatter(
            norm_first_grad.astype(jnp.bfloat16), "dp", scatter_dimension=0, tiled=True
        ).astype(jnp.float32),
        lax.psum_scatter(
            mixer_in_grad.astype(jnp.bfloat16), "dp", scatter_dimension=0, tiled=True
        ).astype(jnp.float32),
        lax.psum_scatter(
            query_weight_grad.astype(jnp.bfloat16), "dp", scatter_dimension=0, tiled=True
        ).astype(jnp.float32),
        lax.psum_scatter(
            bc_weight_grad.astype(jnp.bfloat16), "dp", scatter_dimension=0, tiled=True
        ).astype(jnp.float32),
        lax.psum_scatter(
            step_weight_grad.astype(jnp.bfloat16), "dp", scatter_dimension=0, tiled=True
        ).astype(jnp.float32),
        lax.psum_scatter(
            kv_weight_grad.astype(jnp.bfloat16), "dp", scatter_dimension=0, tiled=True
        ).astype(jnp.float32),
        lax.psum_scatter(
            conv_inner_grad.astype(jnp.bfloat16), "dp", scatter_dimension=1, tiled=True
        ).astype(jnp.float32),
        lax.psum_scatter(
            conv_shared_grad.astype(jnp.bfloat16), "dp", scatter_dimension=1, tiled=True
        ).astype(jnp.float32),
        lax.psum_scatter(
            group_gain_grad.astype(jnp.bfloat16), "dp", scatter_dimension=0, tiled=True
        ).astype(jnp.float32),
        lax.psum_scatter(
            out_weight_grad.astype(jnp.bfloat16), "dp", scatter_dimension=0, tiled=True
        ).astype(jnp.float32),
    )
    head_sums = lax.psum((log_rate_grad, step_bias_grad, skip_gain_grad), "dp")
    return (
        output.astype(jnp.bfloat16),
        input_grad,
        mixer_sums[0],
        mixer_sums[1],
        mixer_sums[2],
        mixer_sums[3],
        mixer_sums[4],
        mixer_sums[5],
        mixer_sums[6],
        mixer_sums[7],
        head_sums[0],
        head_sums[1],
        head_sums[2],
        mixer_sums[8],
        mixer_sums[9],
        ffn_sums[3],
        ffn_sums[0],
        ffn_sums[1],
        ffn_sums[2],
    )


def solution(mesh):
    in_specs = (
        P("dp", ("row", "col")),
        P(("row", "col")),
        P("row", "col"),
        P("row", "col"),
        P("row", None),
        P("row", None),
        P("row", "col", None),
        P(None, ("col", "row")),
        P(),
        P(("col", "row")),
        P(("col", "row")),
        P(("col", "row")),
        P(("col", "row")),
        P("col", "row"),
        P(("row", "col")),
        P("row", "col"),
        P("row", "col"),
        P("col", "row"),
        P("dp", ("row", "col")),
    )
    out_specs = (
        P("dp", ("row", "col")),
        P("dp", ("row", "col")),
        P(("row", "col", "dp")),
        P(("row", "dp"), "col"),
        P(("row", "dp"), "col"),
        P(("row", "dp"), None),
        P(("row", "dp"), None),
        P(("row", "dp"), "col", None),
        P(None, ("col", "row", "dp")),
        P(None, "dp"),
        P(("col", "row")),
        P(("col", "row")),
        P(("col", "row")),
        P(("col", "row", "dp")),
        P(("col", "dp"), "row"),
        P(("row", "col", "dp")),
        P(("row", "dp"), "col"),
        P(("row", "dp"), "col"),
        P(("col", "dp"), "row"),
    )
    return jax.shard_map(local, mesh=mesh, in_specs=in_specs, out_specs=out_specs, check_vma=False)
```

profile of v0, /device:TPU:0, one launch (start us, length us, event | category | flops | bytes accessed | tf_op | source)
XLA Modules:
  0.0 1850.0 jit_solution(365628367020615453)
XLA Ops:
  50.9 41.3 %all-reduce.41.cloned.1.call-done = (f32[512,1,256]{2,0,1:T(8,128)}, f32[512,48]{0,1:T(8,128)}, f32[512,512]{1,0:T(8,128)}) async-done(((f32[512,1,256]{2,0,1:T(8,128)}, f32[512,48]{0,1:T(8,128)}, f32[512,512]{1,0:T(8,128)}), (f32[512,1,256]{2,0,1:T(8,128)}, f32[512,48]{0,1:T(8,128)}, f32[512,512]{1,0:T(8,128)})) %all-reduce.41.cloned.1.call-update) | async-done | bytes 1671184 | tf_op jit(solution)/shard_map/psum | solution.py:266
  101.8 13.5 reduce-scatter.30.cloned.1.call-done
  123.1 71.7 %reduce-scatter.28.cloned.1.call-done = f32[512,1536]{1,0:T(8,128)} async-done(((f32[512,3072]{1,0:T(8,128)}), f32[512,1536]{1,0:T(8,128)}) %reduce-scatter.28.cloned.1.call-update) | async-done | bytes 3145744 | tf_op jit(solution)/shard_map/reduce_scatter | solution.py:162
  212.4 59.2 %while.50 = (s32[]{:T(128)}, f32[12,64,256]{2,1,0:T(8,128)S(1)}, f32[2,256,12,64]{1,0,3,2:T(2,128)}, f32[2,12,64,256]{3,2,1,0:T(8,128)}, f32[2,256,12]{1,2,0:T(8...) while((s32[]{:T(128)}, f32[12,64,256]{2,1,0:T(8,128)S(1)}, ...), condition=%wide.region_8.9_spmd.clone, body=%wide.region_5.8_spmd.clone.sunk | while | flops 2019301376 | bytes 13459100 | solution.py:108
  222.1 16.7 dynamic_update_slice.85
  251.5 16.7 dynamic_update_slice.85
  284.5 34.3 %all-gather.12.cloned.1.call-done = bf16[512,2048]{0,1:T(8,128)(2,1)} async-done(((bf16[512,1024]{0,1:T(8,128)(2,1)}), bf16[512,2048]{0,1:T(8,128)(2,1)}) %all-gather.12.cloned.1.call-update) | async-done | bytes 2097168 | tf_op jit(solution)/shard_map/all_gather | solution.py:168
  373.2 21.6 %reduce-scatter.40.cloned.1.call-done = bf16[512,1024]{1,0:T(8,128)(2,1)} async-done(((bf16[512,2048]{1,0:T(8,128)(2,1)}), bf16[512,1024]{1,0:T(8,128)(2,1)}) %reduce-scatter.40.cloned.1.call-update) | async-done | bytes 1048592 | tf_op jit(solution)/shard_map/reduce_scatter | solution.py:180
  394.8 56.5 %reduce-scatter.36.cloned.1.call-done = f32[512,1024]{1,0:T(8,128)} async-done(((f32[512,2048]{1,0:T(8,128)}), f32[512,1024]{1,0:T(8,128)}) %reduce-scatter.36.cloned.1.call-update) | async-done | bytes 2097168 | tf_op jit(solution)/shard_map/reduce_scatter | solution.py:163
  451.2 56.7 %reduce-scatter.34.cloned.1.call-done = f32[512,1024]{1,0:T(8,128)} async-done(((f32[512,2048]{1,0:T(8,128)}), f32[512,1024]{1,0:T(8,128)}) %reduce-scatter.34.cloned.1.call-update) | async-done | bytes 2097168 | tf_op jit(solution)/shard_map/reduce_scatter | solution.py:162
  514.2 32.5 %all-gather.20.cloned.1.call-done = bf16[512,2048]{1,0:T(8,128)(2,1)} async-done(((bf16[512,1024]{1,0:T(8,128)(2,1)}), bf16[512,2048]{1,0:T(8,128)(2,1)}) %all-gather.20.cloned.1.call-update) | async-done | bytes 2097168 | tf_op jit(solution)/shard_map/all_gather | solution.py:187
  553.2 28.7 %all-gather.22.cloned.1.call-done = bf16[512,2048]{1,0:T(8,128)(2,1)} async-done(((bf16[512,1024]{1,0:T(8,128)(2,1)}), bf16[512,2048]{1,0:T(8,128)(2,1)}) %all-gather.22.cloned.1.call-update) | async-done | bytes 2097168 | tf_op jit(solution)/shard_map/all_gather | solution.py:188
  627.5 30.9 %reduce-scatter.44.cloned.1.call-done = bf16[512,1024]{1,0:T(8,128)(2,1)} async-done(((bf16[512,2048]{1,0:T(8,128)(2,1)}), bf16[512,1024]{1,0:T(8,128)(2,1)}) %reduce-scatter.44.cloned.1.call-update) | async-done | bytes 1048592 | tf_op jit(solution)/shard_map/reduce_scatter | solution.py:180
  694.6 115.4 %while.51 = (s32[]{:T(128)}, f32[12,64,256]{2,1,0:T(8,128)}, f32[2,256,12,64]{1,0,3,2:T(2,128)}, f32[2,256,256]{2,1,0:T(8,128)}, f32[2,256,256]{2,1,0:T(8,128)},...) while((s32[]{:T(128)}, f32[12,64,256]{2,1,0:T(8,128)}, ...), condition=%wide.region_40.41_spmd.clone, body=%wide.region_28.40_spmd.clone.sunk | while | flops 4854478848 | bytes 63372344 | solution.py:108
  735.1 16.7 dynamic_update_slice.88
  793.1 16.7 dynamic_update_slice.88
  855.4 22.8 %reduce-scatter.68.cloned.1.call-done = bf16[64,4]{1,0:T(8,128)(2,1)} async-done(((bf16[512,4]{1,0:T(8,128)(2,1)}), bf16[64,4]{1,0:T(8,128)(2,1)}) %reduce-scatter.68.cloned.1.call-update) | async-done | bytes 528
  890.8 21.6 %all-gather.16.cloned.1.call-done = bf16[512,2048]{1,0:T(8,128)(2,1)} async-done(((bf16[512,1024]{1,0:T(8,128)(2,1)}), bf16[512,2048]{1,0:T(8,128)(2,1)}) %all-gather.16.cloned.1.call-update) | async-done | bytes 2097168 | tf_op jit(solution)/shard_map/all_gather | solution.py:168
  932.5 19.6 %all-reduce.43.cloned.1.call-done = (bf16[512,2,256]{2,0,1:T(8,128)(2,1)}, bf16[512,512]{1,0:T(8,128)(2,1)}) async-done(((bf16[512,2,256]{2,0,1:T(8,128)(2,1)}, bf16[512,512]{1,0:T(8,128)(2,1)}), (bf16[512,2,256]{2,0,1:T(8,128)(2,1)}, bf16[512,512]{1,0:T(8,128)(2,1)})) %all-reduce.43.cloned.1.call-update) | async-done | bytes 1048592 | tf_op jit(solution)/shard_map/psum | solution.py:358
  984.9 15.8 all-gather.26.cloned.1.call-done
  1025.7 21.7 %all-reduce.33 = (f32[12]{0:T(128)}, f32[12]{0:T(128)}, f32[12]{0:T(128)}) all-reduce(f32[12]{0:T(128)S(1)} %negate_multiply_fusion, f32[12]{0:T(128)S(1)} %get-tuple-element.830, f32[12]{0:T(128)S(1)} %reduce_sum.458), channel_id=1, replica_groups=mesh['dp'=8,'row'=2,'col'=2] {'dp'}, use_global_device_ids=true, to_apply=%region_71.72 | all-reduce | flops 36 | bytes 288 | tf_op jit(solution)/shard_map/psum | solution.py:420
  1048.0 18.4 reduce-scatter.66.cloned.1.call-done
  1067.8 63.1 %reduce-scatter.64.cloned.1.call-done = bf16[128,48]{1,0:T(8,128)(2,1)} async-done(((bf16[1024,48]{1,0:T(8,128)(2,1)}), bf16[128,48]{1,0:T(8,128)(2,1)}) %reduce-scatter.64.cloned.1.call-update) | async-done | bytes 12304
  1132.4 89.6 %reduce-scatter.62.cloned.1.call-done = bf16[256,1024]{1,0:T(8,128)(2,1)} async-done(((bf16[2048,1024]{1,0:T(8,128)(2,1)}), bf16[256,1024]{1,0:T(8,128)(2,1)}) %reduce-scatter.62.cloned.1.call-update) | async-done | bytes 524304 | tf_op jit(solution)/shard_map/reduce_scatter | solution.py:206
  1224.1 89.2 %reduce-scatter.60.cloned.1.call-done = bf16[128,2048]{1,0:T(8,128)(2,1)} async-done(((bf16[1024,2048]{1,0:T(8,128)(2,1)}), bf16[128,2048]{1,0:T(8,128)(2,1)}) %reduce-scatter.60.cloned.1.call-update) | async-done | bytes 524304 | tf_op jit(solution)/shard_map/reduce_scatter | solution.py:203
  1315.4 89.6 %reduce-scatter.58.cloned.1.call-done = bf16[128,2048]{1,0:T(8,128)(2,1)} async-done(((bf16[1024,2048]{1,0:T(8,128)(2,1)}), bf16[128,2048]{1,0:T(8,128)(2,1)}) %reduce-scatter.58.cloned.1.call-update) | async-done | bytes 524304 | tf_op jit(solution)/shard_map/reduce_scatter | solution.py:200
  1407.2 63.3 %reduce-scatter.54.cloned.1.call-done = bf16[128,1,256]{2,0,1:T(8,128)(2,1)} async-done(((bf16[1024,1,256]{2,0,1:T(8,128)(2,1)}), bf16[128,1,256]{2,0,1:T(8,128)(2,1)}) %reduce-scatter.54.cloned.1.call-update) | async-done | bytes 65552 | tf_op jit(solution)/shard_map/reduce_scatter | solution.py:404
  1472.1 65.0 %reduce-scatter.50.cloned.1.call-done = bf16[128,512]{1,0:T(8,128)(2,1)} async-done(((bf16[1024,512]{1,0:T(8,128)(2,1)}), bf16[128,512]{1,0:T(8,128)(2,1)}) %reduce-scatter.50.cloned.1.call-update) | async-done | bytes 131088 | tf_op jit(solution)/shard_map/reduce_scatter | solution.py:395
  1538.8 64.2 %reduce-scatter.52.cloned.1.call-done = bf16[128,512]{1,0:T(8,128)(2,1)} async-done(((bf16[1024,512]{1,0:T(8,128)(2,1)}), bf16[128,512]{1,0:T(8,128)(2,1)}) %reduce-scatter.52.cloned.1.call-update) | async-done | bytes 131088 | tf_op jit(solution)/shard_map/reduce_scatter | solution.py:398
  1604.6 89.4 %reduce-scatter.56.cloned.1.call-done = bf16[256,1024]{1,0:T(8,128)(2,1)} async-done(((bf16[2048,1024]{1,0:T(8,128)(2,1)}), bf16[256,1024]{1,0:T(8,128)(2,1)}) %reduce-scatter.56.cloned.1.call-update) | async-done | bytes 524304 | tf_op jit(solution)/shard_map/reduce_scatter | solution.py:416
  1706.5 21.6 %all-reduce.35 = (bf16[512]{0:T(512)(128)(2,1)S(1)}, bf16[768]{0:T(1024)(128)(2,1)S(1)}, bf16[512]{0:T(512)(128)(2,1)S(1)}) all-reduce(bf16[512]{0:T(512)(128)(2,1)S(1)} %get-tuple-element.759, bf16[768]{0:T(1024)(128)(2,1)S(1)} %copy-done.101, bf16[512]{0:T(512)(128)(2,1)S(1)} %copy-done.104), channel_id=12, replica_groups=mesh['dp'=8,'row'=2,'col'=2] {'dp'}, use_global_device_ids=true, to_apply=%region_53.54.clone | all-reduce | flops 1792 | bytes 7168
  1738.4 102.5 %reduce-scatter.48.cloned.1.call-done = bf16[128,3072]{1,0:T(8,128)(2,1)} async-done(((bf16[1024,3072]{1,0:T(8,128)(2,1)}), bf16[128,3072]{1,0:T(8,128)(2,1)}) %reduce-scatter.48.cloned.1.call-update) | async-done | bytes 786448 | tf_op jit(solution)/shard_map/reduce_scatter | solution.py:392
  (649 shorter events, 519.0 us)
Async XLA Ops:
  7.2 21.9 %all-gather.10.cloned.1.call-start = ((), (), s32[]{:S(2)}) async-start(), calls=%async_computation.21 | async-start | bytes 1572864 | tf_op jit(solution)/shard_map/all_gather | solution.py:157
  19.6 72.6 %all-reduce.41.cloned.1.call-start = ((), (), s32[]{:S(2)}) async-start(), calls=%async_computation.51 | async-start | bytes 3342336 | tf_op jit(solution)/shard_map/psum | solution.py:266
  36.9 78.5 %reduce-scatter.30.cloned.1.call-start = ((), (), s32[]{:S(2)}) async-start(), calls=%async_computation.23 | async-start | bytes 1572864 | tf_op jit(solution)/shard_map/reduce_scatter | solution.py:163
  38.7 156.0 %reduce-scatter.28.cloned.1.call-start = ((), (), s32[]{:S(2)}) async-start(), calls=%async_computation.22 | async-start | bytes 9437184 | tf_op jit(solution)/shard_map/reduce_scatter | solution.py:162
  46.8 272.0 %all-gather.12.cloned.1.call-start = ((), (), s32[]{:S(2)}) async-start(), calls=%async_computation.24 | async-start | bytes 3145728 | tf_op jit(solution)/shard_map/all_gather | solution.py:168
  284.5 50.7 %reduce-scatter.32.cloned.1.call-start = ((), (), s32[]{:S(2)}) async-start(), calls=%async_computation.25 | async-start | bytes 3145728 | tf_op jit(solution)/shard_map/reduce_scatter | solution.py:172
  325.4 21.8 %all-gather.18.cloned.1.call-start = ((), (), s32[]{:S(2)}) async-start(), calls=%async_computation.31 | async-start | bytes 1572864 | tf_op jit(solution)/shard_map/all_gather | solution.py:176
  326.1 33.3 %all-gather.14.cloned.1.call-start = ((), (), s32[]{:S(2)}) async-start(), calls=%async_computation.26 | async-start | bytes 1572864 | tf_op jit(solution)/shard_map/all_gather | solution.py:157
  347.1 47.7 %reduce-scatter.40.cloned.1.call-start = ((), (), s32[]{:S(2)}) async-start(), calls=%async_computation.32 | async-start | bytes 3145728 | tf_op jit(solution)/shard_map/reduce_scatter | solution.py:180
  353.3 97.9 %reduce-scatter.36.cloned.1.call-start = ((), (), s32[]{:S(2)}) async-start(), calls=%async_computation.28 | async-start | bytes 6291456 | tf_op jit(solution)/shard_map/reduce_scatter | solution.py:163
  366.2 141.8 %reduce-scatter.34.cloned.1.call-start = ((), (), s32[]{:S(2)}) async-start(), calls=%async_computation.27 | async-start | bytes 6291456 | tf_op jit(solution)/shard_map/reduce_scatter | solution.py:162
  373.1 173.6 %all-gather.20.cloned.1.call-start = ((), (), s32[]{:S(2)}) async-start(), calls=%async_computation.33 | async-start | bytes 3145728 | tf_op jit(solution)/shard_map/all_gather | solution.py:187
  513.4 68.5 %all-gather.22.cloned.1.call-start = ((), (), s32[]{:S(2)}) async-start(), calls=%async_computation.34 | async-start | bytes 3145728 | tf_op jit(solution)/shard_map/all_gather | solution.py:188
  514.2 83.3 %reduce-scatter.42.cloned.1.call-start = ((), (), s32[]{:S(2)}) async-start(), calls=%async_computation.35 | async-start | bytes 1572864 | tf_op jit(solution)/shard_map/reduce_scatter | solution.py:193
  588.8 30.2 %all-gather.24.cloned.1.call-start = ((), (), s32[]{:S(2)}) async-start(), calls=%async_computation.36 | async-start | bytes 1572864 | tf_op jit(solution)/shard_map/all_gather | solution.py:176
  609.8 48.6 %reduce-scatter.44.cloned.1.call-start = ((), (), s32[]{:S(2)}) async-start(), calls=%async_computation.37 | async-start | bytes 3145728 | tf_op jit(solution)/shard_map/reduce_scatter | solution.py:180
  625.3 252.8 %reduce-scatter.68.cloned.1.call-start = ((), (), s32[]{:S(2)}) async-start(), calls=%async_computation.50 | async-start | bytes 147456
  816.0 96.3 %all-gather.16.cloned.1.call-start = ((), (), s32[]{:S(2)}) async-start(), calls=%async_computation.29 | async-start | bytes 3145728 | tf_op jit(solution)/shard_map/all_gather | solution.py:168
  819.4 132.7 %all-reduce.43.cloned.1.call-start = ((), (), s32[]{:S(2)}) async-start(), calls=%async_computation.52 | async-start | bytes 2097152 | tf_op jit(solution)/shard_map/psum | solution.py:358
  845.8 154.8 %all-gather.26.cloned.1.call-start = ((), (), s32[]{:S(2)}) async-start(), calls=%async_computation.38 | async-start | bytes 4718592 | tf_op jit(solution)/shard_map/all_gather | solution.py:187
  853.0 213.4 %reduce-scatter.66.cloned.1.call-start = ((), (), s32[]{:S(2)}) async-start(), calls=%async_computation.49 | async-start | bytes 221184
  855.3 275.6 %reduce-scatter.64.cloned.1.call-start = ((), (), s32[]{:S(2)}) async-start(), calls=%async_computation.48 | async-start | bytes 294912
  890.8 331.2 %reduce-scatter.62.cloned.1.call-start = ((), (), s32[]{:S(2)}) async-start(), calls=%async_computation.47 | async-start | bytes 4718592 | tf_op jit(solution)/shard_map/reduce_scatter | solution.py:206
  918.7 394.6 %reduce-scatter.60.cloned.1.call-start = ((), (), s32[]{:S(2)}) async-start(), calls=%async_computation.46 | async-start | bytes 4718592 | tf_op jit(solution)/shard_map/reduce_scatter | solution.py:203
  926.0 479.0 %reduce-scatter.58.cloned.1.call-start = ((), (), s32[]{:S(2)}) async-start(), calls=%async_computation.45 | async-start | bytes 4718592 | tf_op jit(solution)/shard_map/reduce_scatter | solution.py:200
  932.5 538.1 %reduce-scatter.54.cloned.1.call-start = ((), (), s32[]{:S(2)}) async-start(), calls=%async_computation.43 | async-start | bytes 589824 | tf_op jit(solution)/shard_map/reduce_scatter | solution.py:404
  954.4 582.7 %reduce-scatter.50.cloned.1.call-start = ((), (), s32[]{:S(2)}) async-start(), calls=%async_computation.41 | async-start | bytes 1179648 | tf_op jit(solution)/shard_map/reduce_scatter | solution.py:395
  970.5 632.4 %reduce-scatter.52.cloned.1.call-start = ((), (), s32[]{:S(2)}) async-start(), calls=%async_computation.42 | async-start | bytes 1179648 | tf_op jit(solution)/shard_map/reduce_scatter | solution.py:398
  972.4 721.6 %reduce-scatter.56.cloned.1.call-start = ((), (), s32[]{:S(2)}) async-start(), calls=%async_computation.44 | async-start | bytes 4718592 | tf_op jit(solution)/shard_map/reduce_scatter | solution.py:416
  978.7 726.3 %reduce-scatter.46.cloned.1.call-start = ((), (), s32[]{:S(2)}) async-start(), calls=%async_computation.39 | async-start | bytes 1572864 | tf_op jit(solution)/shard_map/reduce_scatter | solution.py:193
  1009.0 726.0 %reduce-scatter.38.cloned.1.call-start = ((), (), s32[]{:S(2)}) async-start(), calls=%async_computation.30 | async-start | bytes 3145728 | tf_op jit(solution)/shard_map/reduce_scatter | solution.py:172
  1015.5 825.3 %reduce-scatter.48.cloned.1.call-start = ((), (), s32[]{:S(2)}) async-start(), calls=%async_computation.40 | async-start | bytes 7077888 | tf_op jit(solution)/shard_map/reduce_scatter | solution.py:392
  (134 other events, 5513.5 us)
Sparse Core Ops, SparseCore 0:
  19.7 9.3 all-gather.9
  37.0 55.1 all-reduce.40
  95.0 20.3 reduce-scatter.29
  117.6 77.0 reduce-scatter.27
  284.6 34.1 all-gather.11
  325.5 9.6 reduce-scatter.31
  336.7 10.2 all-gather.17
  349.2 10.1 all-gather.13
  361.7 32.9 reduce-scatter.39
  396.9 54.2 reduce-scatter.35
  453.6 54.3 reduce-scatter.33
  513.5 33.1 all-gather.19
  548.8 33.1 all-gather.21
  588.9 8.5 reduce-scatter.41
  609.9 9.0 all-gather.23
  625.4 32.9 reduce-scatter.43
  816.2 61.9 reduce-scatter.67
  880.1 32.2 all-gather.15
  916.0 36.1 all-reduce.42
  954.2 46.4 all-gather.25
  1004.8 61.4 reduce-scatter.65
  1070.6 60.2 reduce-scatter.63
  1135.0 86.9 reduce-scatter.61
  1225.4 87.7 reduce-scatter.59
  1317.3 87.6 reduce-scatter.57
  1408.8 61.6 reduce-scatter.53
  1474.7 62.3 reduce-scatter.49
  1540.5 62.3 reduce-scatter.51
  1607.1 86.9 reduce-scatter.55
  1696.7 8.2 reduce-scatter.45
  1707.3 10.7 reduce-scatter.37
  1721.7 119.1 reduce-scatter.47
where the time goes:
time: 1860 us; the launch traced here: 1850 us
  waiting for transfers between devices  1250 us (67%)
  matrix products  206 us (11%)
  local copies, waits for them, and re-layouts  147 us (8%)
  other arithmetic  116 us (6%)
  blocking collectives  105 us (6%)
    reduce_scatter x2, waiting for transfers between devices, sum_projections(): lax.psum_scatter(first_term, 'row', scatter_dimension=1, tiled=True)  128 us
    unnamed x35, waiting for transfers between devices  106 us
    reduce_scatter x1, waiting for transfers between devices, local(): lax.psum_scatter(mixer_in_grad.astype(jnp.bfloat16), 'dp', scatter_dimens...  103 us
    reduce_scatter x1, waiting for transfers between devices, reduce_ffn(): lax.psum_scatter(gate_grad.astype(jnp.bfloat16), 'dp', scatter_dimension=...  89.6 us
    reduce_scatter x1, waiting for transfers between devices, reduce_ffn(): lax.psum_scatter(down_grad.astype(jnp.bfloat16), 'dp', scatter_dimension=...  89.6 us
    reduce_scatter x1, waiting for transfers between devices, local(): lax.psum_scatter(out_weight_grad.astype(jnp.bfloat16), 'dp', scatter_dime...  89.4 us
    reduce_scatter x1, waiting for transfers between devices, reduce_ffn(): lax.psum_scatter(up_grad.astype(jnp.bfloat16), 'dp', scatter_dimension=0,...  89.2 us
    dynamic_update_slice x16, local copies, waits for them, and re-layouts, mixer_core(): lax.scan(jax.checkpoint(state_block), initial, block_inputs)  72.2 us
  transfers between devices with their start and end apart: 32, of which 30 were waited for; matrix products, arithmetic and copies ran while one was open for 10% of the time, Pallas kernels for 0%

commit v1 on v0

v1 whole, which is shorter than its diff:
```python
from functools import partial
import math

import jax
import jax.numpy as jnp
from jax import lax
from jax.experimental import pallas as pl
from jax.experimental.pallas import tpu as pltpu
from jax.sharding import PartitionSpec as P

D = 2048
HM = 48
PM = 64
NS = 256
HD = 128
LANES = 128
CHUNK = 128

norm_epsilon = 1e-05
rope_base = 10000.0
highest = lax.Precision.HIGHEST
f32 = jnp.float32
bf16 = jnp.bfloat16
VMEM_LIMIT = 56 * 1024 * 1024


def product(left_side, right_side):
    return jnp.dot(left_side, right_side, preferred_element_type=f32)


def product_back(left_side, right_side):
    return lax.dot_general(
        left_side, right_side, (((1,), (1,)), ((), ())), preferred_element_type=f32
    )


def outer_sum(left_side, right_side):
    return lax.dot_general(
        left_side, right_side, (((0,), (0,)), ((), ())), preferred_element_type=f32
    )


def swap(values_in, axis):
    return lax.ppermute(values_in, axis, [(0, 1), (1, 0)])


def in_order(own, other, place, axis):
    return jnp.concatenate(
        [jnp.where(place == 0, own, other), jnp.where(place == 0, other, own)], axis=axis
    )


def part_of(values_in, place, axis):
    size = values_in.shape[axis] // 2
    return lax.dynamic_slice_in_dim(values_in, place * size, size, axis)


def rows_total(values_in):
    values_in = values_in + swap(values_in, "col")
    return values_in + swap(values_in, "row")


def dp_bits():
    bits, bit = [], 1
    while bit < lax.axis_size("dp"):
        bits.append(bit)
        bit *= 2
    return bits


def swap_dp(values_in, bit):
    return lax.ppermute(values_in, "dp", [(i, i ^ bit) for i in range(lax.axis_size("dp"))])


def scatter_dp(grads, last_first=False):
    bits = dp_bits()
    count = lax.axis_size("dp")
    me = lax.axis_index("dp")
    rest = (grads.shape[0] // count,) + grads.shape[1:]
    parts = grads.reshape((2,) * len(bits) + rest)
    left = bits[::-1]
    order = bits[1:] + bits[:1] if last_first else bits
    for bit in order:
        axis = left.index(bit)
        mine = (me // bit) % 2
        send = lax.dynamic_index_in_dim(parts, 1 - mine, axis, keepdims=False)
        keep = lax.dynamic_index_in_dim(parts, mine, axis, keepdims=False)
        parts = keep.astype(f32) + swap_dp(send, bit).astype(f32)
        left.pop(axis)
        if left:
            parts = parts.astype(bf16)
    return parts


def sigmoid(values_in):
    return 1.0 / (1.0 + jnp.exp(-values_in))


def softplus(values_in):
    return jnp.maximum(values_in, 0.0) + jnp.log1p(jnp.exp(-jnp.abs(values_in)))


def low_lanes():
    return lax.broadcasted_iota(jnp.int32, (1, LANES), 1) < PM


def pair_columns(values_in, pair):
    return jnp.where(
        low_lanes(), values_in[:, 2 * pair : 2 * pair + 1], values_in[:, 2 * pair + 1 : 2 * pair + 2]
    )


def shift_down(values_in, count):
    if count == 0:
        return values_in
    rows = lax.broadcasted_iota(jnp.int32, values_in.shape, 0)
    return jnp.where(rows >= count, pltpu.roll(values_in, count, 0), 0.0)


def shift_up(values_in, count):
    if count == 0:
        return values_in
    length = values_in.shape[0]
    rows = lax.broadcasted_iota(jnp.int32, values_in.shape, 0)
    return jnp.where(rows < length - count, pltpu.roll(values_in, length - count, 0), 0.0)


def conv(values_in, taps):
    count = taps.shape[0]
    total = values_in * taps[count - 1 : count, :]
    for tap in range(count - 1):
        total = total + taps[tap : tap + 1, :] * shift_down(values_in, count - 1 - tap)
    return total


def conv_back(grad, values_in, taps):
    count = taps.shape[0]
    total = grad * taps[count - 1 : count, :]
    for tap in range(count - 1):
        total = total + taps[tap : tap + 1, :] * shift_up(grad, count - 1 - tap)
    tap_grads = [
        jnp.sum(grad * shift_down(values_in, count - 1 - tap), axis=0, keepdims=True)
        for tap in range(count)
    ]
    return total, tap_grads


def stacked_pair(values_in):
    low = low_lanes()
    return jnp.concatenate(
        [jnp.where(low, values_in, 0.0), jnp.where(low, 0.0, values_in)], axis=0
    ).astype(bf16)


def lower_mask():
    rows = lax.broadcasted_iota(jnp.int32, (CHUNK, CHUNK), 0)
    columns = lax.broadcasted_iota(jnp.int32, (CHUNK, CHUNK), 1)
    return (rows >= columns).astype(f32)


def mixer_forward_kernel(
    own_ref,
    other_ref,
    factor_ref,
    shared_ref,
    step_ref,
    conv_inner_ref,
    conv_shared_ref,
    head_ref,
    skip_ref,
    gain_ref,
    gained_ref,
    square_ref,
    mix_ref,
    ssm_ref,
    states_ref,
    inner_buf,
    gate_buf,
    maps_buf,
    step_buf,
    decay_buf,
    weighted_buf,
    state_buf,
):
    pairs = gained_ref.shape[1] // LANES
    length = own_ref.shape[0]
    low = low_lanes()
    factor = factor_ref[...]
    for pair in range(pairs):
        first = slice(2 * pair * LANES, (2 * pair + 1) * LANES)
        second = slice((2 * pair + 1) * LANES, (2 * pair + 2) * LANES)
        own = slice(pair * LANES, (pair + 1) * LANES)
        head_a = (own_ref[:, first] + other_ref[:, first].astype(f32)) * factor
        head_b = (own_ref[:, second] + other_ref[:, second].astype(f32)) * factor
        mix_ref[:, first] = head_a
        mix_ref[:, second] = head_b
        taken = jnp.where(low, pltpu.roll(head_a, PM, 1), head_b)
        gate_buf[:, own] = jnp.where(low, head_a, pltpu.roll(head_b, PM, 1))
        taken = conv(taken, conv_inner_ref[:, own])
        inner_buf[:, own] = taken * sigmoid(taken)
    for block in range(shared_ref.shape[1] // LANES):
        own = slice(block * LANES, (block + 1) * LANES)
        taken = conv(shared_ref[:, own], conv_shared_ref[:, own])
        maps_buf[:, own] = (taken * sigmoid(taken)).astype(bf16)
    steps = softplus(step_ref[...] + head_ref[1:2, :])
    step_buf[...] = steps
    decay_buf[...] = -jnp.exp(head_ref[0:1, :]) * steps
    state_buf[...] = jnp.zeros_like(state_buf)
    mask = lower_mask()

    def chunk(index, carry):
        rows = pl.ds(pl.multiple_of(index * CHUNK, CHUNK), CHUNK)
        running = jnp.dot(mask, decay_buf[rows, :], precision=highest, preferred_element_type=f32)
        running_t = running.T
        step = step_buf[rows, :]
        step_t = step.T
        last = running[CHUNK - 1 : CHUNK, :]
        grown = jnp.exp(running)
        tail = jnp.exp(last - running) * step
        grown_last = jnp.exp(last)
        basis = maps_buf[rows, 0:NS]
        read = maps_buf[rows, NS : 2 * NS]
        gram = product_back(read, basis)
        state_low = state_buf[...].astype(bf16)
        states_ref[pl.ds(pl.multiple_of(index * NS, NS), NS), :] = state_low
        carried = product(read, state_low)
        square = jnp.zeros((CHUNK, 1), f32)
        for pair in range(pairs):
            own = slice(pair * LANES, (pair + 1) * LANES)
            inner = inner_buf[rows, own]
            mixing = []
            for head in (2 * pair, 2 * pair + 1):
                spread = jnp.exp(
                    jnp.minimum(running[:, head : head + 1] - running_t[head : head + 1, :], 0.0)
                )
                mixing.append(
                    (gram * spread * mask * step_t[head : head + 1, :]).astype(bf16)
                )
            ssm = product(jnp.concatenate(mixing, axis=1), stacked_pair(inner))
            ssm = ssm + pair_columns(grown, pair) * carried[:, own] + skip_ref[:, own] * inner
            ssm_ref[rows, own] = ssm
            weighted_buf[:, own] = (pair_columns(tail, pair) * inner).astype(bf16)
            gate = gate_buf[rows, own]
            gated = ssm * gate * sigmoid(gate)
            square = square + jnp.sum(gated * gated, axis=1, keepdims=True)
            gained_ref[rows, own] = (gated * gain_ref[:, own]).astype(bf16)
        square_ref[rows, :] = square
        fresh = outer_sum(basis, weighted_buf[...])
        for pair in range(pairs):
            own = slice(pair * LANES, (pair + 1) * LANES)
            state_buf[:, own] = (
                pair_columns(grown_last, pair) * state_buf[:, own] + fresh[:, own]
            )
        return carry

    lax.fori_loop(0, length // CHUNK, chunk, 0)


def mixer_backward_kernel(
    mix_ref,
    ssm_ref,
    states_ref,
    shared_ref,
    step_ref,
    conv_inner_ref,
    conv_shared_ref,
    head_ref,
    skip_ref,
    gain_ref,
    lanes_ref,
    grad_ref,
    group_factor_ref,
    group_scale_ref,
    factor_ref,
    mix_grad_ref,
    shared_grad_ref,
    step_grad_ref,
    inner_taps_ref,
    shared_taps_ref,
    head_grad_ref,
    wide_grad_ref,
    total_ref,
    taken_buf,
    inner_buf,
    maps_buf,
    step_buf,
    decay_buf,
    weighted_buf,
    grown_buf,
    inner_grad_buf,
    maps_grad_buf,
    sums_buf,
    state_grad_buf,
):
    pairs = ssm_ref.shape[1] // LANES
    length = ssm_ref.shape[0]
    group_pairs = pairs // (grad_ref.shape[1] // (pairs * LANES // 2 + HD))
    low = low_lanes()
    for pair in range(pairs):
        first = slice(2 * pair * LANES, (2 * pair + 1) * LANES)
        second = slice((2 * pair + 1) * LANES, (2 * pair + 2) * LANES)
        own = slice(pair * LANES, (pair + 1) * LANES)
        taken = jnp.where(low, pltpu.roll(mix_ref[:, first], PM, 1), mix_ref[:, second])
        taken_buf[:, own] = taken
        taken = conv(taken, conv_inner_ref[:, own])
        inner_buf[:, own] = taken * sigmoid(taken)
    for block in range(shared_ref.shape[1] // LANES):
        own = slice(block * LANES, (block + 1) * LANES)
        taken = conv(shared_ref[:, own], conv_shared_ref[:, own])
        maps_buf[:, own] = (taken * sigmoid(taken)).astype(bf16)
    shifted = step_ref[...] + head_ref[1:2, :]
    steps = softplus(shifted)
    rate = -jnp.exp(head_ref[0:1, :])
    step_buf[...] = steps
    decay_buf[...] = rate * steps
    state_grad_buf[...] = jnp.zeros_like(state_grad_buf)
    head_grad_ref[...] = jnp.zeros_like(head_grad_ref)
    wide_grad_ref[...] = jnp.zeros_like(wide_grad_ref)
    mask = lower_mask()
    chunks = length // CHUNK
    lane_index = lax.broadcasted_iota(jnp.int32, (1, LANES), 1)

    def chunk(turn, carry):
        index = chunks - 1 - turn
        rows = pl.ds(pl.multiple_of(index * CHUNK, CHUNK), CHUNK)
        running = jnp.dot(mask, decay_buf[rows, :], precision=highest, preferred_element_type=f32)
        running_t = running.T
        step = step_buf[rows, :]
        step_t = step.T
        last = running[CHUNK - 1 : CHUNK, :]
        grown = jnp.exp(running)
        fading = jnp.exp(last - running)
        grown_last = jnp.exp(last)
        basis = maps_buf[rows, 0:NS]
        read = maps_buf[rows, NS : 2 * NS]
        gram = product_back(read, basis)
        state_low = states_ref[pl.ds(pl.multiple_of(index * NS, NS), NS), :]
        carried = product(read, state_low)
        state_grad_low = state_grad_buf[...].astype(bf16)
        weighted_grad = product(basis, state_grad_low)
        gram_grad = jnp.zeros((CHUNK, CHUNK), f32)
        decay_grad = jnp.zeros((CHUNK, LANES), f32)
        column_grads = []
        total = jnp.zeros((CHUNK, 1), f32)
        group_factor = group_factor_ref[rows, :]
        group_scale = group_scale_ref[rows, :]
        factor = factor_ref[rows, :]
        for pair in range(pairs):
            first = slice(2 * pair * LANES, (2 * pair + 1) * LANES)
            second = slice((2 * pair + 1) * LANES, (2 * pair + 2) * LANES)
            own = slice(pair * LANES, (pair + 1) * LANES)
            place = pair * LANES + (pair // group_pairs) * HD
            incoming = grad_ref[rows, place : place + LANES]
            head_a = mix_ref[rows, first]
            head_b = mix_ref[rows, second]
            gate = jnp.where(low, head_a, pltpu.roll(head_b, PM, 1))
            gate_sigmoid = sigmoid(gate)
            gate_act = gate * gate_sigmoid
            ssm = ssm_ref[rows, own]
            gated = ssm * gate_act
            wide_grad_ref[0:1, own] += jnp.sum(
                incoming * gated * group_factor, axis=0, keepdims=True
            )
            gated_grad = group_factor * gain_ref[:, own] * incoming - gated * group_scale
            gate_grad = gated_grad * ssm * gate_sigmoid * (1.0 + gate * (1.0 - gate_sigmoid))
            ssm_grad = gated_grad * gate_act
            inner = inner_buf[rows, own]
            wide_grad_ref[1:2, own] += jnp.sum(ssm_grad * inner, axis=0, keepdims=True)
            gate_b = pltpu.roll(gate_grad, PM, 1)
            total = total + jnp.sum(gate_grad * gate, axis=1, keepdims=True)
            mix_grad_ref[rows, first] = jnp.where(low, gate_grad * factor, 0.0).astype(bf16)
            mix_grad_ref[rows, second] = jnp.where(low, gate_b * factor, 0.0).astype(bf16)
            grad_low = ssm_grad.astype(bf16)
            mixing_grad = product_back(grad_low, stacked_pair(inner))
            spreads = []
            for side, head in enumerate((2 * pair, 2 * pair + 1)):
                spread = mask * jnp.exp(
                    jnp.minimum(running[:, head : head + 1] - running_t[head : head + 1, :], 0.0)
                )
                step_row = step_t[head : head + 1, :]
                spread_gram = gram * spread
                spreads.append(spread_gram.astype(bf16))
                own_grad = mixing_grad[:, side * CHUNK : (side + 1) * CHUNK] * step_row
                gram_grad = gram_grad + own_grad * spread
                moved = own_grad * spread_gram
                decay_grad = decay_grad + jnp.where(
                    lane_index == head, jnp.sum(moved, axis=1, keepdims=True), 0.0
                )
                column_grads.append(jnp.sum(moved, axis=0, keepdims=True))
            within = outer_sum(jnp.concatenate(spreads, axis=0), stacked_pair(ssm_grad))
            fading_grad = pair_columns(fading, pair) * weighted_grad[:, own]
            spread_grad = within + fading_grad
            step_wide = pair_columns(step, pair)
            inner_grad_buf[rows, own] = step_wide * spread_grad + skip_ref[:, own] * ssm_grad
            grown_grad = pair_columns(grown, pair) * ssm_grad
            grown_buf[:, own] = grown_grad.astype(bf16)
            weighted_buf[:, own] = (pair_columns(fading, pair) * step_wide * inner).astype(bf16)
            sums_buf[0:CHUNK, own] = (inner * spread_grad).astype(bf16)
            sums_buf[CHUNK : 2 * CHUNK, own] = (inner * fading_grad * step_wide).astype(bf16)
            sums_buf[2 * CHUNK : 3 * CHUNK, own] = (grown_grad * carried[:, own]).astype(bf16)
        head_sums = product(sums_buf[...], lanes_ref[...])
        step_part = head_sums[0:CHUNK, :]
        fading_part = head_sums[CHUNK : 2 * CHUNK, :]
        grown_part = head_sums[2 * CHUNK : 3 * CHUNK, :]
        fill = jnp.zeros((CHUNK - len(column_grads), CHUNK), f32)
        column_grad = jnp.concatenate(column_grads + [fill], axis=0).T
        decay_grad = decay_grad - column_grad + grown_part - fading_part
        state_part = jnp.zeros((1, LANES), f32)
        grown_low = grown_buf[...]
        fresh = outer_sum(read, grown_low)
        for pair in range(pairs):
            own = slice(pair * LANES, (pair + 1) * LANES)
            state_grad = state_grad_buf[:, own]
            held = jnp.sum(state_grad * state_low[:, own].astype(f32), axis=0, keepdims=True)
            for side, head in enumerate((2 * pair, 2 * pair + 1)):
                kept = jnp.where(low if side == 0 else jnp.logical_not(low), held, 0.0)
                state_part = state_part + jnp.where(
                    lane_index == head, jnp.sum(kept, axis=1, keepdims=True), 0.0
                )
            state_grad_buf[:, own] = pair_columns(grown_last, pair) * state_grad + fresh[:, own]
        last_grad = jnp.sum(fading_part, axis=0, keepdims=True) + grown_last * state_part
        decay_sum = (
            lax.dot_general(
                mask,
                decay_grad,
                (((0,), (0,)), ((), ())),
                precision=highest,
                preferred_element_type=f32,
            )
            + last_grad
        )
        raw_shift = step_ref[rows, :] + head_ref[1:2, :]
        raw_grad = (step_part + decay_sum * rate) * sigmoid(raw_shift)
        head_grad_ref[0:1, :] += jnp.sum(decay_sum * decay_buf[rows, :], axis=0, keepdims=True)
        head_grad_ref[1:2, :] += jnp.sum(raw_grad, axis=0, keepdims=True)
        step_grad_ref[rows, :] = (raw_grad * factor).astype(bf16)
        total = total + jnp.sum(raw_grad * step_ref[rows, :], axis=1, keepdims=True)
        total_ref[rows, :] = total
        gram_low = gram_grad.astype(bf16)
        maps_grad_buf[rows, 0:NS] = outer_sum(gram_low, read) + product_back(
            weighted_buf[...], state_grad_low
        )
        maps_grad_buf[rows, NS : 2 * NS] = product(gram_low, basis) + product_back(
            grown_low, state_low
        )
        return carry

    lax.fori_loop(0, chunks, chunk, 0)
    factor = factor_ref[...]
    total = total_ref[...]
    for pair in range(pairs):
        first = slice(2 * pair * LANES, (2 * pair + 1) * LANES)
        second = slice((2 * pair + 1) * LANES, (2 * pair + 2) * LANES)
        own = slice(pair * LANES, (pair + 1) * LANES)
        taken = taken_buf[:, own]
        taps = conv_inner_ref[:, own]
        before = conv(taken, taps)
        before_sigmoid = sigmoid(before)
        grad = inner_grad_buf[:, own] * before_sigmoid * (1.0 + before * (1.0 - before_sigmoid))
        grad, tap_grads = conv_back(grad, taken, taps)
        for tap, tap_grad in enumerate(tap_grads):
            inner_taps_ref[tap : tap + 1, own] = tap_grad
        total = total + jnp.sum(grad * taken, axis=1, keepdims=True)
        grad = grad * factor
        low_a = mix_grad_ref[:, first].astype(f32)
        low_b = mix_grad_ref[:, second].astype(f32)
        mix_grad_ref[:, first] = jnp.where(low, low_a, pltpu.roll(grad, PM, 1)).astype(bf16)
        mix_grad_ref[:, second] = jnp.where(low, low_b, grad).astype(bf16)
    for block in range(shared_ref.shape[1] // LANES):
        own = slice(block * LANES, (block + 1) * LANES)
        taken = shared_ref[:, own]
        taps = conv_shared_ref[:, own]
        before = conv(taken, taps)
        before_sigmoid = sigmoid(before)
        grad = maps_grad_buf[:, own] * before_sigmoid * (1.0 + before * (1.0 - before_sigmoid))
        grad, tap_grads = conv_back(grad, taken, taps)
        for tap, tap_grad in enumerate(tap_grads):
            shared_taps_ref[tap : tap + 1, own] = tap_grad
        total = total + jnp.sum(grad * taken, axis=1, keepdims=True)
        shared_grad_ref[:, own] = (grad * factor).astype(bf16)
    total_ref[...] = total


def call(kernel, outs, scratch, flops, *operands):
    moved = sum(math.prod(item.shape) * item.dtype.itemsize for item in operands)
    moved += sum(math.prod(item.shape) * item.dtype.itemsize for item in outs)
    return pl.pallas_call(
        kernel,
        out_shape=outs,
        in_specs=[pl.BlockSpec(memory_space=pltpu.VMEM)] * len(operands),
        out_specs=[pl.BlockSpec(memory_space=pltpu.VMEM)] * len(outs),
        scratch_shapes=scratch,
        compiler_params=pltpu.CompilerParams(vmem_limit_bytes=VMEM_LIMIT),
        cost_estimate=pl.CostEstimate(flops=flops, bytes_accessed=moved, transcendentals=0),
    )(*operands)


def shape(dims, dtype=f32):
    return jax.ShapeDtypeStruct(dims, dtype)


def mixer_forward(own, other, factor, shared, step, taps, shared_taps, heads, skip, gain):
    length, width = own.shape
    channels = width // 2
    chunks = length // CHUNK
    return call(
        mixer_forward_kernel,
        [
            shape((length, channels), bf16),
            shape((length, 1)),
            shape((length, width)),
            shape((length, channels)),
            shape((chunks * NS, channels), bf16),
        ],
        [
            pltpu.VMEM((length, channels), f32),
            pltpu.VMEM((length, channels), f32),
            pltpu.VMEM((length, 2 * NS), bf16),
            pltpu.VMEM((length, LANES), f32),
            pltpu.VMEM((length, LANES), f32),
            pltpu.VMEM((CHUNK, channels), bf16),
            pltpu.VMEM((NS, channels), f32),
        ],
        8 * 10**9,
        own, other, factor, shared, step, taps, shared_taps, heads, skip, gain,
    )


def mixer_backward(
    mix, ssm, states, shared, step, taps, shared_taps, heads, skip, gain, lanes, grad,
    group_factor, group_scale, factor,
):
    length, width = mix.shape
    channels = width // 2
    return call(
        mixer_backward_kernel,
        [
            shape((length, width), bf16),
            shape((length, 2 * NS), bf16),
            shape((length, LANES), bf16),
            shape((taps.shape[0], channels)),
            shape((taps.shape[0], 2 * NS)),
            shape((8, LANES)),
            shape((8, channels)),
            shape((length, 1)),
        ],
        [
            pltpu.VMEM((length, channels), f32),
            pltpu.VMEM((length, channels), f32),
            pltpu.VMEM((length, 2 * NS), bf16),
            pltpu.VMEM((length, LANES), f32),
            pltpu.VMEM((length, LANES), f32),
            pltpu.VMEM((CHUNK, channels), bf16),
            pltpu.VMEM((CHUNK, channels), bf16),
            pltpu.VMEM((length, channels), f32),
            pltpu.VMEM((length, 2 * NS), f32),
            pltpu.VMEM((3 * CHUNK, channels), bf16),
            pltpu.VMEM((NS, channels), f32),
        ],
        16 * 10**9,
        mix, ssm, states, shared, step, taps, shared_taps, heads, skip, gain, lanes, grad,
        group_factor, group_scale, factor,
    )


def rotated(values_in, cosine, sine):
    return values_in * cosine + pltpu.roll(values_in, HD // 2, 1) * sine


def rotated_back(grad, cosine, sine):
    return grad * cosine + pltpu.roll(grad * sine, HD // 2, 1)


def attention_forward_kernel(query_ref, pair_ref, cosine_ref, sine_ref, out_ref):
    length = query_ref.shape[0]
    scale = 1.0 / math.sqrt(HD)
    block = min(256, length)
    keys = rotated(pair_ref[:, :HD], cosine_ref[...], sine_ref[...]).astype(bf16)
    vals = pair_ref[:, HD:].astype(bf16)
    for head in range(query_ref.shape[1] // HD):
        lanes = slice(head * HD, (head + 1) * HD)
        queries = rotated(query_ref[:, lanes], cosine_ref[...], sine_ref[...]).astype(bf16)
        for start in range(0, length, block):
            end = start + block
            scores = product_back(queries[start:end], keys[:end]) * scale
            rows = start + lax.broadcasted_iota(jnp.int32, (block, end), 0)
            columns = lax.broadcasted_iota(jnp.int32, (block, end), 1)
            scores = jnp.where(columns <= rows, scores, -1e30)
            exponent = jnp.exp(scores - jnp.max(scores, axis=1, keepdims=True))
            probs = exponent * (1.0 / jnp.sum(exponent, axis=1, keepdims=True))
            out_ref[start:end, lanes] = product(probs.astype(bf16), vals[:end]).astype(bf16)


def attention_backward_kernel(
    query_ref, pair_ref, cosine_ref, sine_ref, grad_ref, factor_ref,
    query_grad_ref, pair_grad_ref, total_ref, key_buf, val_buf,
):
    length = query_ref.shape[0]
    scale = 1.0 / math.sqrt(HD)
    block = min(256, length)
    cosine, sine = cosine_ref[...], sine_ref[...]
    keys = rotated(pair_ref[:, :HD], cosine, sine).astype(bf16)
    vals = pair_ref[:, HD:].astype(bf16)
    heads = query_ref.shape[1] // HD
    group = grad_ref.shape[1] // heads
    key_buf[...] = jnp.zeros_like(key_buf)
    val_buf[...] = jnp.zeros_like(val_buf)
    for head in range(heads):
        lanes = slice(head * HD, (head + 1) * HD)
        queries = rotated(query_ref[:, lanes], cosine, sine).astype(bf16)
        incoming = grad_ref[:, (head + 1) * group - HD : (head + 1) * group].astype(bf16)
        for start in range(0, length, block):
            end = start + block
            scores = product_back(queries[start:end], keys[:end]) * scale
            rows = start + lax.broadcasted_iota(jnp.int32, (block, end), 0)
            columns = lax.broadcasted_iota(jnp.int32, (block, end), 1)
            scores = jnp.where(columns <= rows, scores, -1e30)
            exponent = jnp.exp(scores - jnp.max(scores, axis=1, keepdims=True))
            probs = exponent * (1.0 / jnp.sum(exponent, axis=1, keepdims=True))
            grad_low = incoming[start:end]
            val_buf[:end, :] += outer_sum(probs.astype(bf16), grad_low)
            probs_grad = product_back(grad_low, vals[:end])
            inner = jnp.sum(probs * probs_grad, axis=1, keepdims=True)
            scores_grad = (probs * (probs_grad - inner) * scale).astype(bf16)
            query_grad = rotated_back(
                product(scores_grad, keys[:end]), cosine[start:end], sine[start:end]
            )
            key_buf[:end, :] += outer_sum(scores_grad, queries[start:end])
            taken = query_ref[start:end, lanes]
            part = jnp.sum(query_grad * taken, axis=1, keepdims=True)
            if head == 0:
                total_ref[start:end, :] = part
            else:
                total_ref[start:end, :] += part
            query_grad_ref[start:end, lanes] = (query_grad * factor_ref[start:end, :]).astype(bf16)
    key_grad = rotated_back(key_buf[...], cosine, sine)
    val_grad = val_buf[...]
    total_ref[...] += jnp.sum(
        key_grad * pair_ref[:, :HD] + val_grad * pair_ref[:, HD:], axis=1, keepdims=True
    )
    pair_grad_ref[:, :HD] = (key_grad * factor_ref[...]).astype(bf16)
    pair_grad_ref[:, HD:] = (val_grad * factor_ref[...]).astype(bf16)


def attention_forward(query, pair, cosine, sine):
    return call(
        attention_forward_kernel, [shape(query.shape, bf16)], [], 4 * 10**9,
        query, pair, cosine, sine,
    )[0]


def attention_backward(query, pair, cosine, sine, grad, factor):
    length = query.shape[0]
    return call(
        attention_backward_kernel,
        [shape(query.shape, bf16), shape(pair.shape, bf16), shape((length, 1))],
        [pltpu.VMEM((length, HD), f32), pltpu.VMEM((length, HD), f32)],
        8 * 10**9,
        query, pair, cosine, sine, grad, factor,
    )


def rope_tables(length):
    half = HD // 2
    inverse = rope_base ** (-jnp.arange(half, dtype=f32) * 2.0 / HD)
    angles = jnp.arange(length, dtype=f32)[:, None] * inverse[None, :]
    cosine, sine = jnp.cos(angles), jnp.sin(angles)
    return jnp.concatenate([cosine, cosine], axis=1), jnp.concatenate([-sine, sine], axis=1)


def to_lanes(values_in):
    return jnp.pad(values_in, ((0, 0), (0, LANES - values_in.shape[1])))


def local(
    tokens,
    norm_first,
    mixer_in,
    query_weight,
    bc_weight,
    step_weight,
    kv_weight,
    conv_inner,
    conv_shared,
    log_rate,
    step_bias,
    skip_gain,
    group_gain,
    out_weight,
    norm_second,
    gate_weight,
    up_weight,
    down_weight,
    cotangent,
):
    length = tokens.shape[0]
    row = lax.axis_index("row")
    col = lax.axis_index("col")
    quarter = col * 2 + row
    head_count = log_rate.shape[0]
    channels = group_gain.shape[0]
    kv_flat = kv_weight.reshape(kv_weight.shape[0], -1)
    residual = tokens.astype(f32)

    first_own = (residual * norm_first).astype(bf16)
    first_half = in_order(first_own, swap(first_own, "col"), col, 1)
    first_factor = lax.rsqrt(rows_total(jnp.sum(residual * residual, axis=1)) / D + norm_epsilon)
    first_column = first_factor[:, None]

    query_own = product(first_half, part_of(query_weight, row, 1))
    query_out = product(first_half, part_of(query_weight, 1 - row, 1)).astype(bf16)
    pair_own = product(first_half, kv_flat)
    shared_own = product(first_half, bc_weight)
    step_own = product(first_half, step_weight)
    early = swap(
        jnp.concatenate(
            [query_out, pair_own.astype(bf16), shared_own.astype(bf16), to_lanes(step_own).astype(bf16)],
            axis=1,
        ),
        "row",
    )
    query_width = query_own.shape[1]
    pair_width = pair_own.shape[1]
    shared_width = shared_own.shape[1]
    mix_out = product(first_half, part_of(mixer_in, 1 - row, 1)).astype(bf16)
    mix_other = swap(mix_out, "row")
    mix_own = product(first_half, part_of(mixer_in, row, 1))
    query_sum = (query_own + early[:, :query_width].astype(f32)) * first_column
    place = query_width
    pair_sum = (pair_own + early[:, place : place + pair_width].astype(f32)) * first_column
    place += pair_width
    shared_sum = (shared_own + early[:, place : place + shared_width].astype(f32)) * first_column
    place += shared_width
    step_sum = (
        step_own + early[:, place : place + step_own.shape[1]].astype(f32)
    ) * first_column
    step_sum = to_lanes(lax.dynamic_slice_in_dim(step_sum, quarter * head_count, head_count, 1))

    cot_half = in_order(cotangent, swap(cotangent, "col"), col, 1)
    hidden_back = product_back(cot_half, part_of(down_weight, 1 - row, 0)).astype(bf16)
    hidden_back = swap(hidden_back, "row")
    hidden_back_own = product_back(cot_half, part_of(down_weight, row, 0))

    cosine, sine = rope_tables(length)
    attended = attention_forward(query_sum, pair_sum, cosine, sine)
    heads = to_lanes(jnp.stack([log_rate, step_bias] + [jnp.zeros_like(log_rate)] * 6))
    skip_wide = jnp.repeat(skip_gain, PM)[None, :]
    gain_wide = group_gain[None, :]
    gained, square, mix_sum, ssm, states = mixer_forward(
        mix_own, mix_other, first_column, shared_sum, step_sum, conv_inner, conv_shared,
        heads, skip_wide, gain_wide,
    )
    group_factor = lax.rsqrt(rows_total(square[:, 0]) / (HM * PM) + norm_epsilon)
    groups = attended.shape[1] // HD
    normed = (gained.astype(f32) * group_factor[:, None]).astype(bf16)
    mixed = jnp.concatenate(
        [normed.reshape(length, groups, -1), attended.reshape(length, groups, HD)], axis=2
    ).reshape(length, -1)
    mixed_half = in_order(mixed, swap(mixed, "row"), row, 1)

    out_partial = product(mixed_half, out_weight)
    second = (
        residual
        + part_of(out_partial, col, 1)
        + swap(part_of(out_partial, 1 - col, 1).astype(bf16), "col").astype(f32)
    )
    second_own = (second * norm_second).astype(bf16)
    second_half = in_order(second_own, swap(second_own, "col"), col, 1)
    second_factor = lax.rsqrt(rows_total(jnp.sum(second * second, axis=1)) / D + norm_epsilon)
    second_column = second_factor[:, None]
    gate_other = swap(product(second_half, part_of(gate_weight, 1 - row, 1)).astype(bf16), "row")
    up_other = swap(product(second_half, part_of(up_weight, 1 - row, 1)).astype(bf16), "row")
    gate_sum = (
        product(second_half, part_of(gate_weight, row, 1)) + gate_other.astype(f32)
    ) * second_column
    up_sum = (
        product(second_half, part_of(up_weight, row, 1)) + up_other.astype(f32)
    ) * second_column
    gate_sigmoid = jax.nn.sigmoid(gate_sum)
    gate_act = gate_sum * gate_sigmoid
    hidden_grad = hidden_back_own + hidden_back.astype(f32)
    gate_grad = hidden_grad * up_sum * gate_sigmoid * (1.0 + gate_sum * (1.0 - gate_sigmoid))
    up_grad = hidden_grad * gate_act
    second_total = rows_total(jnp.sum(gate_grad * gate_sum + up_grad * up_sum, axis=1))
    gate_low = (gate_grad * second_column).astype(bf16)
    up_low = (up_grad * second_column).astype(bf16)
    gate_half = in_order(gate_low, swap(gate_low, "row"), row, 1)
    up_half = in_order(up_low, swap(up_low, "row"), row, 1)
    second_in_partial = product_back(gate_half, gate_weight) + product_back(up_half, up_weight)
    second_in_grad = part_of(second_in_partial, col, 1) + swap(
        part_of(second_in_partial, 1 - col, 1).astype(bf16), "col"
    ).astype(f32)
    cot_own = cotangent.astype(f32)
    second_grad = (
        cot_own
        + norm_second * second_in_grad
        - second * (second_factor**2 * second_total / D)[:, None]
    )
    norm_second_grad = jnp.sum(second_in_grad * second, axis=0)

    branch_own = second_grad.astype(bf16)
    branch_half = in_order(branch_own, swap(branch_own, "col"), col, 1)
    mixed_back = swap(
        product_back(branch_half, part_of(out_weight, 1 - row, 0)).astype(bf16), "row"
    )
    mixed_grad = product_back(branch_half, part_of(out_weight, row, 0)) + mixed_back.astype(f32)

    hidden = (gate_act * up_sum).astype(bf16)
    hidden_half = in_order(hidden, swap(hidden, "row"), row, 1)
    layer_partial = product(hidden_half, down_weight)
    layer_out = (
        second
        + part_of(layer_partial, col, 1)
        + swap(part_of(layer_partial, 1 - col, 1).astype(bf16), "col").astype(f32)
    ).astype(bf16)

    gate_weight_grad = scatter_dp(outer_sum(second_half, gate_half).astype(bf16))
    up_weight_grad = scatter_dp(outer_sum(second_half, up_half).astype(bf16))
    down_weight_grad = scatter_dp(outer_sum(hidden_half, cot_half).astype(bf16))
    out_weight_grad = scatter_dp(outer_sum(mixed_half, branch_half).astype(bf16), True)

    normed_grad = mixed_grad.reshape(length, groups, -1)[:, :, : channels // groups]
    group_total = rows_total(
        jnp.sum(
            normed_grad * gained.astype(f32).reshape(length, groups, -1), axis=(1, 2)
        )
    )
    group_scale = group_factor**3 * group_total / (HM * PM)
    lanes = (
        jnp.arange(channels)[:, None] // PM == jnp.arange(LANES)[None, :]
    ).astype(bf16)
    query_grad, pair_grad, attention_total = attention_backward(
        query_sum, pair_sum, cosine, sine, mixed_grad, first_column
    )
    (
        mix_grad,
        shared_grad,
        step_grad,
        conv_inner_grad,
        conv_shared_part,
        head_grads,
        wide_grads,
        mixer_total,
    ) = mixer_backward(
        mix_sum, ssm, states, shared_sum, step_sum, conv_inner, conv_shared, heads, skip_wide,
        gain_wide, lanes, mixed_grad, group_factor[:, None], group_scale[:, None], first_column,
    )
    first_total = rows_total((attention_total + mixer_total)[:, 0])

    mix_half = in_order(mix_grad, swap(mix_grad, "row"), row, 1)
    query_half = in_order(query_grad, swap(query_grad, "row"), row, 1)
    shared_sums = shared_grad.astype(f32) + swap(shared_grad, "col").astype(f32)
    shared_low = shared_sums.astype(bf16)
    late = jnp.concatenate([shared_low, pair_grad], axis=1)
    late = (late.astype(f32) + swap(late, "row").astype(f32)).astype(bf16)
    shared_low, pair_low = late[:, :shared_width], late[:, shared_width:]
    step_two = in_order(
        step_grad[:, :head_count], swap(step_grad, "row")[:, :head_count], row, 1
    )
    step_all = in_order(step_two, swap(step_two, "col"), col, 1)

    first_in_partial = (
        product_back(mix_half, mixer_in)
        + product_back(query_half, query_weight)
        + product_back(pair_low, kv_flat)
        + 0.5 * (product_back(shared_low, bc_weight) + product_back(step_all, step_weight))
    )
    first_in_grad = part_of(first_in_partial, col, 1) + swap(
        part_of(first_in_partial, 1 - col, 1).astype(bf16), "col"
    ).astype(f32)
    input_grad = (
        second_grad
        + norm_first * first_in_grad
        - residual * (first_factor**2 * first_total / D)[:, None]
    )
    norm_first_grad = jnp.sum(first_in_grad * residual, axis=0)

    mixer_in_grad = scatter_dp(outer_sum(first_half, mix_half).astype(bf16))
    rest = jnp.concatenate(
        [query_half, pair_low, part_of(shared_low, col, 1), to_lanes(step_all)], axis=1
    )
    rest_grad = scatter_dp(outer_sum(first_half, rest).astype(bf16))
    place = query_half.shape[1]
    query_weight_grad = rest_grad[:, :place]
    kv_weight_grad = rest_grad[:, place : place + pair_width].reshape((-1,) + kv_weight.shape[1:])
    place += pair_width
    bc_own = rest_grad[:, place : place + shared_width // 2]
    bc_weight_grad = in_order(bc_own, swap(bc_own, "col"), col, 1)
    place += shared_width // 2
    step_weight_grad = rest_grad[:, place : place + step_weight.shape[1]]

    conv_shared_sum = conv_shared_part + swap(conv_shared_part, "col")
    conv_shared_sum = conv_shared_sum + swap(conv_shared_sum, "row")
    skip_grad = wide_grads[1].reshape(head_count, PM).sum(axis=1)
    pieces = [
        norm_first_grad,
        norm_second_grad,
        conv_inner_grad.reshape(-1),
        conv_shared_sum.reshape(-1),
        wide_grads[0],
        jnp.pad(head_grads[0, :head_count], (0, LANES - head_count)),
        jnp.pad(head_grads[1, :head_count], (0, LANES - head_count)),
        jnp.pad(skip_grad, (0, LANES - head_count)),
    ]
    small = jnp.concatenate(pieces).reshape(-1, LANES)
    for bit in dp_bits():
        small = small + swap_dp(small, bit)
    small = small.reshape(-1)
    sums, place = [], 0
    for piece in pieces:
        sums.append(small[place : place + piece.shape[0]])
        place += piece.shape[0]
    me, count = lax.axis_index("dp"), lax.axis_size("dp")

    def own_block(values_in, axis):
        size = values_in.shape[axis] // count
        return lax.dynamic_slice_in_dim(values_in, me * size, size, axis)

    return (
        layer_out,
        input_grad,
        own_block(sums[0], 0),
        mixer_in_grad,
        query_weight_grad,
        bc_weight_grad,
        step_weight_grad,
        kv_weight_grad,
        own_block(sums[2].reshape(conv_inner.shape), 1),
        own_block(sums[3].reshape(conv_shared.shape), 1),
        sums[5][:head_count],
        sums[6][:head_count],
        sums[7][:head_count],
        own_block(sums[4], 0),
        out_weight_grad,
        own_block(sums[1], 0),
        gate_weight_grad,
        up_weight_grad,
        down_weight_grad,
    )


def solution(mesh):
    in_specs = (
        P("dp", ("row", "col")),
        P(("row", "col")),
        P("row", "col"),
        P("row", "col"),
        P("row", None),
        P("row", None),
        P("row", "col", None),
        P(None, ("col", "row")),
        P(),
        P(("col", "row")),
        P(("col", "row")),
        P(("col", "row")),
        P(("col", "row")),
        P("col", "row"),
        P(("row", "col")),
        P("row", "col"),
        P("row", "col"),
        P("col", "row"),
        P("dp", ("row", "col")),
    )
    out_specs = (
        P("dp", ("row", "col")),
        P("dp", ("row", "col")),
        P(("row", "col", "dp")),
        P(("row", "dp"), "col"),
        P(("row", "dp"), "col"),
        P(("row", "dp"), None),
        P(("row", "dp"), None),
        P(("row", "dp"), "col", None),
        P(None, ("col", "row", "dp")),
        P(None, "dp"),
        P(("col", "row")),
        P(("col", "row")),
        P(("col", "row")),
        P(("col", "row", "dp")),
        P(("col", "dp"), "row"),
        P(("row", "col", "dp")),
        P(("row", "dp"), "col"),
        P(("row", "dp"), "col"),
        P(("col", "dp"), "row"),
    )
    return jax.shard_map(local, mesh=mesh, in_specs=in_specs, out_specs=out_specs, check_vma=False)
```

time: 1860 us -> 829 us (0.45)
  waiting for transfers between devices: 1250 us -> 507 us
  matrix products: 206 us -> 74 us
  blocking collectives: 105 us -> 0 us
  local copies, waits for them, and re-layouts: 147 us -> 60.3 us
  Pallas kernels: 0 us -> 56.8 us
  starting transfers between devices: 2.59 us -> 51.3 us
  other arithmetic: 116 us -> 68.1 us
    reduce_scatter x18 -> x0, waiting for transfers between devices: 930 us -> none  [the longest x2 128 us: sum_projections(): lax.psum_scatter(first_term, 'row', scatter_dimension=1, tiled=True)]
    ppermute x0 -> x60, waiting for transfers between devices: none -> 507 us  [the longest x21 307 us: swap_dp(): lax.ppermute(values_in, 'dp', [(i, i ^ bit) for i in range(lax.axis_size(...]
    all_gather x9 -> x0, waiting for transfers between devices: 157 us -> none  [the longest x2 55.9 us: gather_mixed(): return lax.all_gather(values_in, 'row', axis=1, tiled=True)]
    unnamed x35 -> x0, waiting for transfers between devices: 106 us -> none
    dot_general x44 -> x13, matrix products: 129 us -> 35.2 us  [product(): return jnp.dot(left_side, right_side, preferred_element_type=f32)]
    dynamic_update_slice x17 -> x0, local copies, waits for them, and re-layouts: 72.4 us -> none  [the longest x16 72.2 us: mixer_core(): lax.scan(jax.checkpoint(state_block), initial, block_inputs)]
    psum x8 -> x0, blocking collectives: 72.3 us -> none  [the longest x6 39.9 us: feature_total(): return lax.psum(partial_total, ('row', 'col'))]
    psum x2 -> x0, waiting for transfers between devices: 60.9 us -> none  [the longest x1 41.3 us: local(): lax.psum((product(first_half, bc_weight), product(first_half, step_weight...]
  transfers between devices with their start and end apart: 32 -> 60, of which waited for: 30 -> 25; matrix products, arithmetic and copies ran while one was open for 10% -> 22% of each run, Pallas kernels for 0% -> 5%
where the time goes in v1:
time: 829 us; the launch traced here: 820 us
  waiting for transfers between devices  507 us (61%)
  matrix products  74 us (9%)
  other arithmetic  68.1 us (8%)
  local copies, waits for them, and re-layouts  60.3 us (7%)
  Pallas kernels  56.8 us (7%)
  starting transfers between devices  51.3 us (6%)
    ppermute x21, waiting for transfers between devices, swap_dp(): lax.ppermute(values_in, 'dp', [(i, i ^ bit) for i in range(lax.axis_size(...  307 us
    ppermute x39, waiting for transfers between devices, swap(): return lax.ppermute(values_in, axis, [(0, 1), (1, 0)])  200 us
    pallas_call x4, Pallas kernels, call(): pl.pallas_call(kernel, out_shape=outs, in_specs=[pl.BlockSpec(memory_spac...  56.8 us
    dot_general x13, matrix products, product(): return jnp.dot(left_side, right_side, preferred_element_type=f32)  35.2 us
    ppermute x21, starting transfers between devices, swap_dp(): lax.ppermute(values_in, 'dp', [(i, i ^ bit) for i in range(lax.axis_size(...  27.3 us
    ppermute x39, starting transfers between devices, swap(): return lax.ppermute(values_in, axis, [(0, 1), (1, 0)])  23.9 us
    dot_general x11, matrix products, product_back(): lax.dot_general(left_side, right_side, (((1,), (1,)), ((), ())), preferre...  23.3 us
    convert_element_type x12, other arithmetic, scatter_dp(): parts = parts.astype(bf16)  19.5 us
  transfers between devices with their start and end apart: 60, of which 25 were waited for; matrix products, arithmetic and copies ran while one was open for 22% of the time, Pallas kernels for 5%

profile of v1, /device:TPU:0, one launch (start us, length us, event | category | flops | bytes accessed | tf_op | source)
XLA Modules:
  0.0 820.2 jit_solution(12819203989833382193)
XLA Ops:
  15.7 4.8 fusion.10
  26.9 48.8 %collective-permute-done.3 = f32[512]{0:T(512)S(1)} collective-permute-done((f32[512]{0:T(512)S(1)}, f32[512]{0:T(512)S(1)}, u32[]{:S(2)}, u32[]{:S(2)}) %collective-permute-start.3) | collective-permute-done | bytes 2080 | tf_op jit(solution)/shard_map/ppermute | solution.py:44
  78.9 5.7 fusion.8.own_ref
  90.6 16.2 %shard_map.330 = (bf16[512,768]{1,0:T(8,128)(2,1)}, f32[512,1]{1,0:T(8,128)}, f32[512,1536]{1,0:T(8,128)}, f32[512,768]{1,0:T(8,128)}, bf16[1024,768]{1,0:T(8,128)(2,1)}) custom-call(f32[512,1536]{1,0:T(8,128)} %fusion.8.own_ref, bf16[512,1536]{1,0:T(8,128)(2,1)} %collective-permute-done.1.other_ref, f32[512,1]{1,0:T(8,128)} %copy.114.factor_ref, ...), custom_call_target="tpu_custom_call" | custom-call | flops 8000000000 | bytes 13142016 | tf_op jit(solution)/shard_map/pallas_call | solution.py:487
  112.0 4.0 shard_map.331
  120.7 25.1 %collective-permute-done.7 = bf16[512,1024]{1,0:T(8,128)(2,1)} collective-permute-done((bf16[512,1024]{1,0:T(8,128)(2,1)S(1)}, bf16[512,1024]{1,0:T(8,128)(2,1)}, u32[]{:S(2)}, u32[]{:S(2)}) %collective-permute-start.7) | collective-permute-done | bytes 1048608 | tf_op jit(solution)/shard_map/ppermute | solution.py:44
  168.8 16.3 %collective-permute-done.17 = bf16[512,1024]{1,0:T(8,128)(2,1)} collective-permute-done((bf16[512,1024]{1,0:T(8,128)(2,1)}, bf16[512,1024]{1,0:T(8,128)(2,1)}, u32[]{:S(2)}, u32[]{:S(2)}) %collective-permute-start.17) | collective-permute-done | bytes 1048608 | tf_op jit(solution)/shard_map/ppermute | solution.py:44
  185.2 3.3 convert_add_fusion.12
  188.5 41.1 %collective-permute-done.12 = f32[512]{0:T(512)S(1)} collective-permute-done((f32[512]{0:T(512)S(1)}, f32[512]{0:T(512)S(1)}, u32[]{:S(2)}, u32[]{:S(2)}) %collective-permute-start.12) | collective-permute-done | bytes 2080 | tf_op jit(solution)/shard_map/ppermute | solution.py:44
  232.3 5.0 multiply_convert_fusion.1
  245.3 18.5 %collective-permute-done.19 = bf16[512,1024]{1,0:T(8,128)(2,1)} collective-permute-done((bf16[512,1024]{1,0:T(8,128)(2,1)}, bf16[512,1024]{1,0:T(8,128)(2,1)}, u32[]{:S(2)}, u32[]{:S(2)}) %collective-permute-start.19) | collective-permute-done | bytes 1048608 | tf_op jit(solution)/shard_map/ppermute | solution.py:44
  267.9 18.4 %collective-permute-done.18 = bf16[512,1024]{1,0:T(8,128)(2,1)} collective-permute-done((bf16[512,1024]{1,0:T(8,128)(2,1)}, bf16[512,1024]{1,0:T(8,128)(2,1)}, u32[]{:S(2)}, u32[]{:S(2)}) %collective-permute-start.18) | collective-permute-done | bytes 1048608 | tf_op jit(solution)/shard_map/ppermute | solution.py:44
  290.3 16.8 %collective-permute-done.14 = bf16[512,1024]{1,0:T(8,128)(2,1)S(1)} collective-permute-done((bf16[512,1024]{1,0:T(8,128)(2,1)}, bf16[512,1024]{1,0:T(8,128)(2,1)S(1)}, u32[]{:S(2)}, u32[]{:S(2)}) %collective-permute-start.14) | collective-permute-done | bytes 1048608 | tf_op jit(solution)/shard_map/ppermute | solution.py:44
  312.4 3.3 fusion.120
  342.5 6.3 collective-permute-done.24
  351.4 4.2 reshape.196
  355.5 3.4 fusion.37
  359.0 7.6 shard_map.333
  370.7 41.2 %collective-permute-done.54 = bf16[2,2,128,2048]{3,2,0,1:T(8,128)(2,1)} collective-permute-done((bf16[2,2,128,2048]{3,2,0,1:T(8,128)(2,1)}, bf16[2,2,128,2048]{3,2,0,1:T(8,128)(2,1)}, u32[]{:S(2)}, u32[]{:S(2)}) %collective-permute-start.54) | collective-permute-done | bytes 2097184 | tf_op jit(solution)/shard_map/ppermute | solution.py:72
  416.0 39.9 %collective-permute-done.57 = bf16[2,2,256,1024]{3,2,0,1:T(8,128)(2,1)} collective-permute-done((bf16[2,2,256,1024]{3,2,0,1:T(8,128)(2,1)}, bf16[2,2,256,1024]{3,2,0,1:T(8,128)(2,1)}, u32[]{:S(2)}, u32[]{:S(2)}) %collective-permute-start.57) | collective-permute-done | bytes 2097184 | tf_op jit(solution)/shard_map/ppermute | solution.py:72
  464.0 28.9 %shard_map.332 = (bf16[512,1536]{1,0:T(8,128)(2,1)}, bf16[512,512]{1,0:T(8,128)(2,1)}, bf16[512,128]{1,0:T(8,128)(2,1)}, f32[4,768]{1,0:T(4,128)}, f32[4,512]{1,...) custom-call(f32[512,1536]{1,0:T(8,128)} %get-tuple-element.37.mix_ref, ...), custom_call_target="tpu_custom_call" | custom-call | flops 16000000000 | bytes 12212224 | tf_op jit(solution)/shard_map/pallas_call | solution.py:487
  523.2 6.1 collective-permute-done.55
  533.6 28.8 %collective-permute-done.58 = bf16[2,256,1024]{2,1,0:T(8,128)(2,1)} collective-permute-done((bf16[2,256,1024]{2,1,0:T(8,128)(2,1)}, bf16[2,256,1024]{2,1,0:T(8,128)(2,1)}, u32[]{:S(2)}, u32[]{:S(2)}) %collective-permute-start.58) | collective-permute-done | bytes 1048608 | tf_op jit(solution)/shard_map/ppermute | solution.py:72
  583.0 39.6 %collective-permute-done.56 = bf16[128,2048]{1,0:T(8,128)(2,1)S(1)} collective-permute-done((bf16[128,2048]{1,0:T(8,128)(2,1)S(1)}, bf16[128,2048]{1,0:T(8,128)(2,1)S(1)}, u32[]{:S(2)}, u32[]{:S(2)}) %collective-permute-start.56) | collective-permute-done | bytes 524320 | tf_op jit(solution)/shard_map/ppermute | solution.py:72
  623.9 5.6 fusion.36
  630.5 4.0 convolution_convert_fusion
  643.6 66.6 %collective-permute-done.38 = f32[57,128]{1,0:T(8,128)S(1)} collective-permute-done((f32[57,128]{1,0:T(8,128)S(1)}, f32[57,128]{1,0:T(8,128)S(1)}, u32[]{:S(2)}, u32[]{:S(2)}) %collective-permute-start.38) | collective-permute-done | bytes 29216 | tf_op jit(solution)/shard_map/ppermute | solution.py:72
  710.6 3.5 collective-permute-done.39
  720.9 3.1 fusion
  728.7 42.0 %collective-permute-done.45 = bf16[2,128,1152]{2,1,0:T(8,128)(2,1)S(1)} collective-permute-done((bf16[2,128,1152]{2,1,0:T(8,128)(2,1)S(1)}, bf16[2,128,1152]{2,1,0:T(8,128)(2,1)S(1)}, u32[]{:S(2)}, u32[]{:S(2)}) %collective-permute-start.45) | collective-permute-done | bytes 589856 | tf_op jit(solution)/shard_map/ppermute | solution.py:72
  775.4 25.3 %collective-permute-done.46 = bf16[128,1152]{1,0:T(8,128)(2,1)S(1)} collective-permute-done((bf16[128,1152]{1,0:T(8,128)(2,1)S(1)}, bf16[128,1152]{1,0:T(8,128)(2,1)S(1)}, u32[]{:S(2)}, u32[]{:S(2)}) %collective-permute-start.46) | collective-permute-done | bytes 294944 | tf_op jit(solution)/shard_map/ppermute | solution.py:72
  806.0 11.5 %collective-permute-done.43 = bf16[128,3072]{1,0:T(8,128)(2,1)} collective-permute-done((bf16[128,3072]{1,0:T(8,128)(2,1)}, bf16[128,3072]{1,0:T(8,128)(2,1)}, u32[]{:S(2)}, u32[]{:S(2)}) %collective-permute-start.43) | collective-permute-done | bytes 786464 | tf_op jit(solution)/shard_map/ppermute | solution.py:72
  (452 shorter events, 222.4 us)
Async XLA Ops:
  12.7 72.0 %collective-permute-start.4 = (bf16[512,1152]{1,0:T(8,128)(2,1)S(1)}, bf16[512,1152]{1,0:T(8,128)(2,1)}, u32[]{:S(2)}, u32[]{:S(2)}) collective-permute-start(bf16[512,1152]{1,0:T(8,128)(2,1)S(1)} %fusion.62), channel_id=1, source_target_pairs={{0,2},{2,0},{1,3},{3,1},{4,6},{6,4},{5,7},{7,5},{8,10},{10,8},{9,1... | collective-permute-start | bytes 3538952 | tf_op jit(solution)/shard_map/ppermute | solution.py:44
  20.5 70.1 %collective-permute-start.1 = (bf16[512,1536]{1,0:T(8,128)(2,1)}, bf16[512,1536]{1,0:T(8,128)(2,1)}, u32[]{:S(2)}, u32[]{:S(2)}) collective-permute-start(bf16[512,1536]{1,0:T(8,128)(2,1)} %fusion.10), channel_id=1, source_target_pairs={{0,2},{2,0},{1,3},{3,1},{4,6},{6,4},{5,7},{7,5},{8,10},{10,8},{9,1... | collective-permute-start | bytes 4718600 | tf_op jit(solution)/shard_map/ppermute | solution.py:44
  21.7 54.1 %collective-permute-start.3 = (f32[512]{0:T(512)S(1)}, f32[512]{0:T(512)S(1)}, u32[]{:S(2)}, u32[]{:S(2)}) collective-permute-start(f32[512]{0:T(512)S(1)} %add.364), channel_id=1, source_target_pairs={{0,2},{2,0},{1,3},{3,1},{4,6},{6,4},{5,7},{7,5},{8,10},{10,8},{9,1... | collective-permute-start | bytes 6152 | tf_op jit(solution)/shard_map/ppermute | solution.py:44
  161.7 67.8 %collective-permute-start.13 = (bf16[512,1024]{1,0:T(8,128)(2,1)}, bf16[512,1024]{1,0:T(8,128)(2,1)}, u32[]{:S(2)}, u32[]{:S(2)}) collective-permute-start(bf16[512,1024]{1,0:T(8,128)(2,1)} %fusion.49), channel_id=1, source_target_pairs={{0,2},{2,0},{1,3},{3,1},{4,6},{6,4},{5,7},{7,5},{8,10},{10,8},{9,1... | collective-permute-start | bytes 3145736 | tf_op jit(solution)/shard_map/ppermute | solution.py:44
  165.5 66.7 %collective-permute-start.10 = (bf16[512,1024]{1,0:T(8,128)(2,1)}, bf16[512,1024]{1,0:T(8,128)(2,1)}, u32[]{:S(2)}, u32[]{:S(2)}) collective-permute-start(bf16[512,1024]{1,0:T(8,128)(2,1)} %fusion.46), channel_id=1, source_target_pairs={{0,2},{2,0},{1,3},{3,1},{4,6},{6,4},{5,7},{7,5},{8,10},{10,8},{9,1... | collective-permute-start | bytes 3145736 | tf_op jit(solution)/shard_map/ppermute | solution.py:44
  167.4 62.2 %collective-permute-start.12 = (f32[512]{0:T(512)S(1)}, f32[512]{0:T(512)S(1)}, u32[]{:S(2)}, u32[]{:S(2)}) collective-permute-start(f32[512]{0:T(512)S(1)} %add.385), channel_id=1, source_target_pairs={{0,2},{2,0},{1,3},{3,1},{4,6},{6,4},{5,7},{7,5},{8,10},{10,8},{9,1... | collective-permute-start | bytes 6152 | tf_op jit(solution)/shard_map/ppermute | solution.py:44
  237.3 26.5 %collective-permute-start.19 = (bf16[512,1024]{1,0:T(8,128)(2,1)}, bf16[512,1024]{1,0:T(8,128)(2,1)}, u32[]{:S(2)}, u32[]{:S(2)}) collective-permute-start(bf16[512,1024]{1,0:T(8,128)(2,1)} %get-tuple-element.141), channel_id=1, source_target_pairs={{0,2},{2,0},{1,3},{3,1},{4,6},{6,4},{5,7},{7,5},{8,10},{10,8},{9,1... | collective-permute-start | bytes 3145736 | tf_op jit(solution)/shard_map/ppermute | solution.py:44
  237.7 48.6 %collective-permute-start.18 = (bf16[512,1024]{1,0:T(8,128)(2,1)}, bf16[512,1024]{1,0:T(8,128)(2,1)}, u32[]{:S(2)}, u32[]{:S(2)}) collective-permute-start(bf16[512,1024]{1,0:T(8,128)(2,1)} %get-tuple-element.139), channel_id=1, source_target_pairs={{0,2},{2,0},{1,3},{3,1},{4,6},{6,4},{5,7},{7,5},{8,10},{10,8},{9,1... | collective-permute-start | bytes 3145736 | tf_op jit(solution)/shard_map/ppermute | solution.py:44
  243.2 64.0 %collective-permute-start.14 = (bf16[512,1024]{1,0:T(8,128)(2,1)}, bf16[512,1024]{1,0:T(8,128)(2,1)S(1)}, u32[]{:S(2)}, u32[]{:S(2)}) collective-permute-start(bf16[512,1024]{1,0:T(8,128)(2,1)} %get-tuple-element.148), channel_id=1, source_target_pairs={{0,2},{2,0},{1,3},{3,1},{4,6},{6,4},{5,7},{7,5},{8,10},{10,8},{9,1... | collective-permute-start | bytes 3145736 | tf_op jit(solution)/shard_map/ppermute | solution.py:44
  243.5 66.4 %collective-permute-start.22 = (f32[512]{0:T(512)S(1)}, f32[512]{0:T(512)S(1)}, u32[]{:S(2)}, u32[]{:S(2)}) collective-permute-start(f32[512]{0:T(512)S(1)} %add.398), channel_id=1, source_target_pairs={{0,2},{2,0},{1,3},{3,1},{4,6},{6,4},{5,7},{7,5},{8,10},{10,8},{9,1... | collective-permute-start | bytes 6152 | tf_op jit(solution)/shard_map/ppermute | solution.py:44
  318.1 48.8 %collective-permute-start.51 = (bf16[2,2,128,2048]{3,2,0,1:T(8,128)(2,1)}, bf16[2,2,128,2048]{3,2,0,1:T(8,128)(2,1)}, u32[]{:S(2)}, u32[]{:S(2)}) collective-permute-start(bf16[2,2,128,2048]{3,2,0,1:T(8,128)(2,1)} %bitcast.159), channel_id=1, source_target_pairs={{0,4},{4,0},{8,12},{12,8},{16,20},{20,16},{24,28},{28,24},{1,5},{5... | collective-permute-start | bytes 6291464 | tf_op jit(solution)/shard_map/ppermute | solution.py:72
  327.9 84.0 %collective-permute-start.54 = (bf16[2,2,128,2048]{3,2,0,1:T(8,128)(2,1)}, bf16[2,2,128,2048]{3,2,0,1:T(8,128)(2,1)}, u32[]{:S(2)}, u32[]{:S(2)}) collective-permute-start(bf16[2,2,128,2048]{3,2,0,1:T(8,128)(2,1)} %bitcast.158), channel_id=1, source_target_pairs={{0,4},{4,0},{8,12},{12,8},{16,20},{20,16},{24,28},{28,24},{1,5},{5... | collective-permute-start | bytes 6291464 | tf_op jit(solution)/shard_map/ppermute | solution.py:72
  334.1 121.8 %collective-permute-start.57 = (bf16[2,2,256,1024]{3,2,0,1:T(8,128)(2,1)}, bf16[2,2,256,1024]{3,2,0,1:T(8,128)(2,1)}, u32[]{:S(2)}, u32[]{:S(2)}) collective-permute-start(bf16[2,2,256,1024]{3,2,0,1:T(8,128)(2,1)} %bitcast.157), channel_id=1, source_target_pairs={{0,4},{4,0},{8,12},{12,8},{16,20},{20,16},{24,28},{28,24},{1,5},{5... | collective-permute-start | bytes 6291464 | tf_op jit(solution)/shard_map/ppermute | solution.py:72
  340.9 224.8 %collective-permute-start.48 = (bf16[2,2,256,1024]{3,2,1,0:T(8,128)(2,1)}, bf16[2,2,256,1024]{3,2,1,0:T(8,128)(2,1)}, u32[]{:S(2)}, u32[]{:S(2)}) collective-permute-start(bf16[2,2,256,1024]{3,2,1,0:T(8,128)(2,1)} %dynamic-slice_bitcast_fusion), channel_id=1, source_target_pairs={{0,8},{4,12},{8,0},{12,4},{16,24},{20,28},{24,16},{28,20},{1,9},{5... | collective-permute-start | bytes 6291464 | tf_op jit(solution)/shard_map/ppermute | solution.py:72
  358.9 100.6 %collective-permute-start.25 = (f32[512]{0:T(512)S(1)}, f32[512]{0:T(512)S(1)}, u32[]{:S(2)}, u32[]{:S(2)}) collective-permute-start(f32[512]{0:T(512)S(1)} %fusion.37), channel_id=1, source_target_pairs={{0,1},{1,0},{2,3},{3,2},{4,5},{5,4},{6,7},{7,6},{8,9},{9,8},{10,11... | collective-permute-start | bytes 6152 | tf_op jit(solution)/shard_map/ppermute | solution.py:44
  367.0 149.4 %collective-permute-start.28 = (bf16[512,256]{1,0:T(8,128)(2,1)}, bf16[512,256]{1,0:T(8,128)(2,1)}, u32[]{:S(2)}, u32[]{:S(2)}) collective-permute-start(bf16[512,256]{1,0:T(8,128)(2,1)} %get-tuple-element.41), channel_id=1, source_target_pairs={{0,2},{2,0},{1,3},{3,1},{4,6},{6,4},{5,7},{7,5},{8,10},{10,8},{9,1... | collective-permute-start | bytes 786440 | tf_op jit(solution)/shard_map/ppermute | solution.py:44
  411.9 109.0 %collective-permute-start.52 = (bf16[2,128,2048]{2,1,0:T(8,128)(2,1)}, bf16[2,128,2048]{2,1,0:T(8,128)(2,1)}, u32[]{:S(2)}, u32[]{:S(2)}) collective-permute-start(bf16[2,128,2048]{2,1,0:T(8,128)(2,1)} %dynamic-slice_bitcast_fusion.4), channel_id=1, source_target_pairs={{0,8},{4,12},{8,0},{12,4},{16,24},{20,28},{24,16},{28,20},{1,9},{5... | collective-permute-start | bytes 3145736 | tf_op jit(solution)/shard_map/ppermute | solution.py:72
  512.4 49.9 %collective-permute-start.58 = (bf16[2,256,1024]{2,1,0:T(8,128)(2,1)}, bf16[2,256,1024]{2,1,0:T(8,128)(2,1)}, u32[]{:S(2)}, u32[]{:S(2)}) collective-permute-start(bf16[2,256,1024]{2,1,0:T(8,128)(2,1)} %dynamic-slice_bitcast_fusion.2), channel_id=1, source_target_pairs={{0,8},{4,12},{8,0},{12,4},{16,24},{20,28},{24,16},{28,20},{1,9},{5... | collective-permute-start | bytes 3145736 | tf_op jit(solution)/shard_map/ppermute | solution.py:72
  519.0 104.8 %collective-permute-start.27 = (bf16[512,1536]{1,0:T(8,128)(2,1)S(1)}, bf16[512,1536]{1,0:T(8,128)(2,1)S(1)}, u32[]{:S(2)}, u32[]{:S(2)}) collective-permute-start(bf16[512,1536]{1,0:T(8,128)(2,1)S(1)} %copy-done.16), channel_id=1, source_target_pairs={{0,2},{2,0},{1,3},{3,1},{4,6},{6,4},{5,7},{7,5},{8,10},{10,8},{9,1... | collective-permute-start | bytes 4718600 | tf_op jit(solution)/shard_map/ppermute | solution.py:44
  520.9 51.7 %collective-permute-start.30 = (bf16[512,768]{1,0:T(8,128)(2,1)S(1)}, bf16[512,768]{1,0:T(8,128)(2,1)S(1)}, u32[]{:S(2)}, u32[]{:S(2)}) collective-permute-start(bf16[512,768]{1,0:T(8,128)(2,1)S(1)} %pad_maximum_fusion.20), channel_id=1, source_target_pairs={{0,2},{2,0},{1,3},{3,1},{4,6},{6,4},{5,7},{7,5},{8,10},{10,8},{9,1... | collective-permute-start | bytes 2359304 | tf_op jit(solution)/shard_map/ppermute | solution.py:44
  529.3 51.1 %collective-permute-start.53 = (bf16[128,2048]{1,0:T(8,128)(2,1)S(1)}, bf16[128,2048]{1,0:T(8,128)(2,1)S(1)}, u32[]{:S(2)}, u32[]{:S(2)}) collective-permute-start(bf16[128,2048]{1,0:T(8,128)(2,1)S(1)} %dynamic-slice_bitcast_fusion.10), channel_id=1, source_target_pairs={{0,16},{4,20},{8,24},{12,28},{16,0},{20,4},{24,8},{28,12},{1,17},{... | collective-permute-start | bytes 1572872 | tf_op jit(solution)/shard_map/ppermute | solution.py:72
  562.3 60.3 %collective-permute-start.56 = (bf16[128,2048]{1,0:T(8,128)(2,1)S(1)}, bf16[128,2048]{1,0:T(8,128)(2,1)S(1)}, u32[]{:S(2)}, u32[]{:S(2)}) collective-permute-start(bf16[128,2048]{1,0:T(8,128)(2,1)S(1)} %dynamic-slice_bitcast_fusion.9), channel_id=1, source_target_pairs={{0,16},{4,20},{8,24},{12,28},{16,0},{20,4},{24,8},{28,12},{1,17},{... | collective-permute-start | bytes 1572872 | tf_op jit(solution)/shard_map/ppermute | solution.py:72
  565.7 76.8 %collective-permute-start.59 = (bf16[256,1024]{1,0:T(8,128)(2,1)S(1)}, bf16[256,1024]{1,0:T(8,128)(2,1)S(1)}, u32[]{:S(2)}, u32[]{:S(2)}) collective-permute-start(bf16[256,1024]{1,0:T(8,128)(2,1)S(1)} %dynamic-slice_bitcast_fusion.8), channel_id=1, source_target_pairs={{0,16},{4,20},{8,24},{12,28},{16,0},{20,4},{24,8},{28,12},{1,17},{... | collective-permute-start | bytes 1572872 | tf_op jit(solution)/shard_map/ppermute | solution.py:72
  572.6 137.6 %collective-permute-start.49 = (bf16[2,256,1024]{2,1,0:T(8,128)(2,1)S(1)}, bf16[2,256,1024]{2,1,0:T(8,128)(2,1)S(1)}, u32[]{:S(2)}, u32[]{:S(2)}) collective-permute-start(bf16[2,256,1024]{2,1,0:T(8,128)(2,1)S(1)} %dynamic-slice_bitcast_fusion.5), channel_id=1, source_target_pairs={{0,16},{4,20},{8,24},{12,28},{16,0},{20,4},{24,8},{28,12},{1,17},{... | collective-permute-start | bytes 3145736 | tf_op jit(solution)/shard_map/ppermute | solution.py:72
  580.4 139.9 %collective-permute-start.44 = (bf16[2,2,128,1152]{3,2,0,1:T(8,128)(2,1)}, bf16[2,2,128,1152]{3,2,0,1:T(8,128)(2,1)S(1)}, u32[]{:S(2)}, u32[]{:S(2)}) collective-permute-start(bf16[2,2,128,1152]{3,2,0,1:T(8,128)(2,1)} %bitcast.160), channel_id=1, source_target_pairs={{0,4},{4,0},{8,12},{12,8},{16,20},{20,16},{24,28},{28,24},{1,5},{5... | collective-permute-start | bytes 3538952 | tf_op jit(solution)/shard_map/ppermute | solution.py:72
  638.8 81.7 %collective-permute-start.41 = (bf16[2,2,128,3072]{3,2,0,1:T(8,128)(2,1)}, bf16[2,2,128,3072]{3,2,0,1:T(8,128)(2,1)}, u32[]{:S(2)}, u32[]{:S(2)}) collective-permute-start(bf16[2,2,128,3072]{3,2,0,1:T(8,128)(2,1)} %bitcast.156), channel_id=1, source_target_pairs={{0,4},{4,0},{8,12},{12,8},{16,20},{20,16},{24,28},{28,24},{1,5},{5... | collective-permute-start | bytes 9437192 | tf_op jit(solution)/shard_map/ppermute | solution.py:72
  641.9 68.3 %collective-permute-start.38 = (f32[57,128]{1,0:T(8,128)S(1)}, f32[57,128]{1,0:T(8,128)S(1)}, u32[]{:S(2)}, u32[]{:S(2)}) collective-permute-start(f32[57,128]{1,0:T(8,128)S(1)} %bitcast.171), channel_id=1, source_target_pairs={{0,4},{4,0},{8,12},{12,8},{16,20},{20,16},{24,28},{28,24},{1,5},{5... | collective-permute-start | bytes 87560 | tf_op jit(solution)/shard_map/ppermute | solution.py:72
  715.1 85.8 %collective-permute-start.50 = (bf16[256,1024]{1,0:T(8,128)(2,1)}, bf16[256,1024]{1,0:T(8,128)(2,1)}, u32[]{:S(2)}, u32[]{:S(2)}) collective-permute-start(bf16[256,1024]{1,0:T(8,128)(2,1)} %dynamic-slice_bitcast_fusion.11), channel_id=1, source_target_pairs={{0,4},{4,0},{8,12},{12,8},{16,20},{20,16},{24,28},{28,24},{1,5},{5... | collective-permute-start | bytes 1572872 | tf_op jit(solution)/shard_map/ppermute | solution.py:72
  724.1 47.9 %collective-permute-start.42 = (bf16[2,128,3072]{2,1,0:T(8,128)(2,1)S(1)}, bf16[2,128,3072]{2,1,0:T(8,128)(2,1)S(1)}, u32[]{:S(2)}, u32[]{:S(2)}) collective-permute-start(bf16[2,128,3072]{2,1,0:T(8,128)(2,1)S(1)} %dynamic-slice_bitcast_fusion.1), channel_id=1, source_target_pairs={{0,8},{4,12},{8,0},{12,4},{16,24},{20,28},{24,16},{28,20},{1,9},{5... | collective-permute-start | bytes 4718600 | tf_op jit(solution)/shard_map/ppermute | solution.py:72
  724.3 46.4 %collective-permute-start.45 = (bf16[2,128,1152]{2,1,0:T(8,128)(2,1)S(1)}, bf16[2,128,1152]{2,1,0:T(8,128)(2,1)S(1)}, u32[]{:S(2)}, u32[]{:S(2)}) collective-permute-start(bf16[2,128,1152]{2,1,0:T(8,128)(2,1)S(1)} %dynamic-slice_bitcast_fusion.7), channel_id=1, source_target_pairs={{0,8},{4,12},{8,0},{12,4},{16,24},{20,28},{24,16},{28,20},{1,9},{5... | collective-permute-start | bytes 1769480 | tf_op jit(solution)/shard_map/ppermute | solution.py:72
  770.9 29.8 %collective-permute-start.46 = (bf16[128,1152]{1,0:T(8,128)(2,1)S(1)}, bf16[128,1152]{1,0:T(8,128)(2,1)S(1)}, u32[]{:S(2)}, u32[]{:S(2)}) collective-permute-start(bf16[128,1152]{1,0:T(8,128)(2,1)S(1)} %dynamic-slice_bitcast_fusion.12), channel_id=1, source_target_pairs={{0,16},{4,20},{8,24},{12,28},{16,0},{20,4},{24,8},{28,12},{1,17},{... | collective-permute-start | bytes 884744 | tf_op jit(solution)/shard_map/ppermute | solution.py:72
  773.5 44.0 %collective-permute-start.43 = (bf16[128,3072]{1,0:T(8,128)(2,1)}, bf16[128,3072]{1,0:T(8,128)(2,1)}, u32[]{:S(2)}, u32[]{:S(2)}) collective-permute-start(bf16[128,3072]{1,0:T(8,128)(2,1)} %dynamic-slice_bitcast_fusion.6), channel_id=1, source_target_pairs={{0,16},{4,20},{8,24},{12,28},{16,0},{20,4},{24,8},{28,12},{1,17},{... | collective-permute-start | bytes 2359304 | tf_op jit(solution)/shard_map/ppermute | solution.py:72
  (112 other events, 1143.7 us)

commit v2 on v1

--- a/solution.py
+++ b/solution.py
@@ -13,6 +13,7 @@
 PM = 64
 NS = 256
 HD = 128
+MIX = 4096
 LANES = 128
 CHUNK = 128
 
@@ -60,6 +61,27 @@
     return values_in + swap(values_in, "row")
 
 
+def sum_cols(values_in, col):
+    sent = swap(part_of(values_in, 1 - col, 1).astype(bf16), "col")
+    return part_of(values_in, col, 1) + sent.astype(f32)
+
+
+def near_blocks(values_in, near):
+    size = MIX // 2 // lax.axis_size("dp")
+    places = range(0, values_in.shape[1], 2 * size)
+    return jnp.concatenate(
+        [
+            jnp.where(
+                near == 0,
+                values_in[:, place : place + size],
+                values_in[:, place + size : place + 2 * size],
+            )
+            for place in places
+        ],
+        axis=1,
+    )
+
+
 def dp_bits():
     bits, bit = [], 1
     while bit < lax.axis_size("dp"):
@@ -72,24 +94,103 @@
     return lax.ppermute(values_in, "dp", [(i, i ^ bit) for i in range(lax.axis_size("dp"))])
 
 
-def scatter_dp(grads, last_first=False):
-    bits = dp_bits()
-    count = lax.axis_size("dp")
-    me = lax.axis_index("dp")
-    rest = (grads.shape[0] // count,) + grads.shape[1:]
-    parts = grads.reshape((2,) * len(bits) + rest)
-    left = bits[::-1]
-    order = bits[1:] + bits[:1] if last_first else bits
-    for bit in order:
-        axis = left.index(bit)
-        mine = (me // bit) % 2
-        send = lax.dynamic_index_in_dim(parts, 1 - mine, axis, keepdims=False)
-        keep = lax.dynamic_index_in_dim(parts, mine, axis, keepdims=False)
-        parts = keep.astype(f32) + swap_dp(send, bit).astype(f32)
-        left.pop(axis)
-        if left:
-            parts = parts.astype(bf16)
-    return parts
+def tie(*values_in):
+    return lax.optimization_barrier(values_in)
+
+
+class Spine:
+    def __init__(self, token):
+        self.token = token
+
+    def wait(self, *values_in):
+        tied = tie(self.token, *values_in)
+        self.token = tied[0]
+        return tied[1] if len(tied) == 2 else tied[1:]
+
+
+class Scatter:
+    def __init__(self, spine, grads, pairs, dtype=bf16):
+        self.spine, self.dtype = spine, dtype
+        self.bits = dp_bits()[1:]
+        blocks = lax.axis_size("dp") // 2 * (2 if pairs else 1)
+        rest = (blocks // 2 ** len(self.bits), grads.shape[0] // blocks) + grads.shape[1:]
+        self.left = self.bits[::-1]
+        self.parts = grads.reshape((2,) * len(self.bits) + rest)
+        self.send()
+
+    def send(self):
+        bit = self.bits[len(self.bits) - len(self.left)]
+        axis = self.left.index(bit)
+        mine = (lax.axis_index("dp") // bit) % 2
+        send = lax.dynamic_index_in_dim(self.parts, 1 - mine, axis, keepdims=False)
+        self.parts = lax.dynamic_index_in_dim(self.parts, mine, axis, keepdims=False)
+        self.arrived = swap_dp(send, bit)
+        self.left.pop(axis)
+
+    def add(self):
+        arrived = self.spine.wait(self.arrived)
+        total = self.parts.astype(f32) + arrived.astype(f32)
+        self.parts = total.astype(bf16 if self.left else self.dtype)
+        if self.left:
+            self.send()
+
+    def finish(self):
+        while self.left:
+            self.add()
+        self.add()
+        return self.parts
+
+
+def place_kernel(count, owners, where_ref, *refs):
+    pieces, out_ref = refs[:count], refs[count]
+    rows = pieces[0].shape[0]
+    for turn in range(count):
+        start = pl.multiple_of((where_ref[0] ^ owners[turn]) * rows, rows)
+        out_ref[pl.ds(start, rows), :] = pieces[turn][...]
+
+
+def place_pieces(pieces, owners):
+    count = len(pieces)
+    rows, columns = pieces[0].shape
+    return pl.pallas_call(
+        partial(place_kernel, count, owners),
+        out_shape=jax.ShapeDtypeStruct((count * rows, columns), pieces[0].dtype),
+        in_specs=[pl.BlockSpec(memory_space=pltpu.SMEM)]
+        + [pl.BlockSpec(memory_space=pltpu.VMEM)] * count,
+        out_specs=pl.BlockSpec(memory_space=pltpu.VMEM),
+        compiler_params=pltpu.CompilerParams(vmem_limit_bytes=VMEM_LIMIT),
+        cost_estimate=pl.CostEstimate(
+            flops=0, bytes_accessed=4 * count * rows * columns, transcendentals=0
+        ),
+    )(lax.axis_index("dp").astype(jnp.int32)[None], *pieces)
+
+
+class Spread:
+    def __init__(self, mine):
+        self.pieces, self.owners = [mine], [0]
+        self.bits = [dp_bits()[::-1]]
+        self.first = 0
+
+    def wait(self, spine):
+        arrived = spine.wait(*self.pieces[self.first :])
+        self.pieces[self.first :] = arrived if isinstance(arrived, (tuple, list)) else [arrived]
+
+    def level(self):
+        start, self.first = self.first, len(self.pieces)
+        sends = [
+            (-bit, turn) for turn in range(start, self.first) for bit in self.bits[turn]
+        ]
+        for bit, turn in sorted(sends):
+            self.pieces.append(swap_dp(self.pieces[turn], -bit))
+            self.owners.append(self.owners[turn] ^ -bit)
+            self.bits.append([lower for lower in self.bits[turn] if lower < -bit])
+
+    def finish(self, spine):
+        self.wait(spine)
+        while len(self.pieces) < lax.axis_size("dp"):
+            self.level()
+            self.wait(spine)
+        return place_pieces(self.pieces, self.owners)
 
 
 def sigmoid(values_in):
@@ -169,7 +270,8 @@
     head_ref,
     skip_ref,
     gain_ref,
-    gained_ref,
+    attended_ref,
+    mixed_ref,
     square_ref,
     mix_ref,
     ssm_ref,
@@ -182,10 +284,15 @@
     weighted_buf,
     state_buf,
 ):
-    pairs = gained_ref.shape[1] // LANES
+    pairs = ssm_ref.shape[1] // LANES
     length = own_ref.shape[0]
+    groups = attended_ref.shape[1] // HD
+    group_pairs = pairs // groups
     low = low_lanes()
     factor = factor_ref[...]
+    for group in range(groups):
+        place = ((group + 1) * group_pairs + group) * LANES
+        mixed_ref[:, place : place + HD] = attended_ref[:, group * HD : (group + 1) * HD]
     for pair in range(pairs):
         first = slice(2 * pair * LANES, (2 * pair + 1) * LANES)
         second = slice((2 * pair + 1) * LANES, (2 * pair + 2) * LANES)
@@ -243,7 +350,8 @@
             gate = gate_buf[rows, own]
             gated = ssm * gate * sigmoid(gate)
             square = square + jnp.sum(gated * gated, axis=1, keepdims=True)
-            gained_ref[rows, own] = (gated * gain_ref[:, own]).astype(bf16)
+            place = pair * LANES + (pair // group_pairs) * HD
+            mixed_ref[rows, place : place + LANES] = (gated * gain_ref[:, own]).astype(bf16)
         square_ref[rows, :] = square
         fresh = outer_sum(basis, weighted_buf[...])
         for pair in range(pairs):
@@ -482,8 +590,6 @@
 
 
 def call(kernel, outs, scratch, flops, *operands):
-    moved = sum(math.prod(item.shape) * item.dtype.itemsize for item in operands)
-    moved += sum(math.prod(item.shape) * item.dtype.itemsize for item in outs)
     return pl.pallas_call(
         kernel,
         out_shape=outs,
@@ -491,7 +597,7 @@
         out_specs=[pl.BlockSpec(memory_space=pltpu.VMEM)] * len(outs),
         scratch_shapes=scratch,
         compiler_params=pltpu.CompilerParams(vmem_limit_bytes=VMEM_LIMIT),
-        cost_estimate=pl.CostEstimate(flops=flops, bytes_accessed=moved, transcendentals=0),
+        cost_estimate=pl.CostEstimate(flops=flops, bytes_accessed=10**6, transcendentals=0),
     )(*operands)
 
 
@@ -499,14 +605,16 @@
     return jax.ShapeDtypeStruct(dims, dtype)
 
 
-def mixer_forward(own, other, factor, shared, step, taps, shared_taps, heads, skip, gain):
+def mixer_forward(
+    own, other, factor, shared, step, taps, shared_taps, heads, skip, gain, attended
+):
     length, width = own.shape
     channels = width // 2
     chunks = length // CHUNK
     return call(
         mixer_forward_kernel,
         [
-            shape((length, channels), bf16),
+            shape((length, channels + attended.shape[1]), bf16),
             shape((length, 1)),
             shape((length, width)),
             shape((length, channels)),
@@ -521,8 +629,8 @@
             pltpu.VMEM((CHUNK, channels), bf16),
             pltpu.VMEM((NS, channels), f32),
         ],
-        8 * 10**9,
-        own, other, factor, shared, step, taps, shared_taps, heads, skip, gain,
+        10**8,
+        own, other, factor, shared, step, taps, shared_taps, heads, skip, gain, attended,
     )
 
 
@@ -557,7 +665,7 @@
             pltpu.VMEM((3 * CHUNK, channels), bf16),
             pltpu.VMEM((NS, channels), f32),
         ],
-        16 * 10**9,
+        10**8,
         mix, ssm, states, shared, step, taps, shared_taps, heads, skip, gain, lanes, grad,
         group_factor, group_scale, factor,
     )
@@ -644,7 +752,7 @@
 
 def attention_forward(query, pair, cosine, sine):
     return call(
-        attention_forward_kernel, [shape(query.shape, bf16)], [], 4 * 10**9,
+        attention_forward_kernel, [shape(query.shape, bf16)], [], 10**8,
         query, pair, cosine, sine,
     )[0]
 
@@ -655,7 +763,7 @@
         attention_backward_kernel,
         [shape(query.shape, bf16), shape(pair.shape, bf16), shape((length, 1))],
         [pltpu.VMEM((length, HD), f32), pltpu.VMEM((length, HD), f32)],
-        8 * 10**9,
+        10**8,
         query, pair, cosine, sine, grad, factor,
     )
 
@@ -696,142 +804,207 @@
     length = tokens.shape[0]
     row = lax.axis_index("row")
     col = lax.axis_index("col")
+    me = lax.axis_index("dp")
+    count = lax.axis_size("dp")
+    near = me % 2
     quarter = col * 2 + row
     head_count = log_rate.shape[0]
     channels = group_gain.shape[0]
     kv_flat = kv_weight.reshape(kv_weight.shape[0], -1)
     residual = tokens.astype(f32)
+    spine = Spine(norm_first[:1])
+
+    def column_share(weight):
+        rows, columns = weight.shape[0] // count, weight.shape[1] // 2
+        return lax.dynamic_slice(weight, (me * rows, (1 - row) * columns), (rows, columns))
+
+    half_rows = out_weight.shape[0] // 2
+    share_rows = half_rows // count
+    out_own = part_of(out_weight, row, 0)
+    gate_own, up_own = part_of(gate_weight, row, 1), part_of(up_weight, row, 1)
+    out_share = lax.dynamic_slice_in_dim(
+        out_weight, (1 - row) * half_rows + me * share_rows, share_rows, 0
+    )
+    ffn_share = jnp.concatenate([column_share(gate_weight), column_share(up_weight)], axis=1)
+    out_spread = Spread(swap(out_share, "row"))
+    ffn_spread = Spread(swap(ffn_share, "row"))
 
     first_own = (residual * norm_first).astype(bf16)
     first_half = in_order(first_own, swap(first_own, "col"), col, 1)
-    first_factor = lax.rsqrt(rows_total(jnp.sum(residual * residual, axis=1)) / D + norm_epsilon)
-    first_column = first_factor[:, None]
-
+    square_first = jnp.sum(residual * residual, axis=1)
+    square_first = square_first + swap(square_first, "col")
     query_own = product(first_half, part_of(query_weight, row, 1))
     query_out = product(first_half, part_of(query_weight, 1 - row, 1)).astype(bf16)
     pair_own = product(first_half, kv_flat)
     shared_own = product(first_half, bc_weight)
     step_own = product(first_half, step_weight)
+    query_width = query_own.shape[1]
+    pair_width = pair_own.shape[1]
+    shared_width = shared_own.shape[1]
     early = swap(
         jnp.concatenate(
-            [query_out, pair_own.astype(bf16), shared_own.astype(bf16), to_lanes(step_own).astype(bf16)],
+            [
+                query_out,
+                pair_own.astype(bf16),
+                part_of(shared_own, col, 1).astype(bf16),
+                to_lanes(step_own).astype(bf16),
+            ],
             axis=1,
         ),
         "row",
     )
-    query_width = query_own.shape[1]
-    pair_width = pair_own.shape[1]
-    shared_width = shared_own.shape[1]
-    mix_out = product(first_half, part_of(mixer_in, 1 - row, 1)).astype(bf16)
-    mix_other = swap(mix_out, "row")
+    mix_other = swap(product(first_half, part_of(mixer_in, 1 - row, 1)).astype(bf16), "row")
     mix_own = product(first_half, part_of(mixer_in, row, 1))
+    cot_half = in_order(cotangent, swap(cotangent, "col"), col, 1)
+    hidden_back = product_back(cot_half, part_of(down_weight, 1 - row, 0)).astype(bf16)
+    hidden_back_own = product_back(cot_half, part_of(down_weight, row, 0))
+
+    out_spread.wait(spine)
+    out_spread.level()
+    square_first = spine.wait(square_first)
+    square_far = swap(square_first, "row")
+    ffn_spread.wait(spine)
+    ffn_spread.level()
+    out_spread.wait(spine)
+    out_spread.level()
+    early, square_far = spine.wait(early, square_far)
+    first_factor = lax.rsqrt((square_first + square_far) / D + norm_epsilon)
+    first_column = first_factor[:, None]
     query_sum = (query_own + early[:, :query_width].astype(f32)) * first_column
     place = query_width
     pair_sum = (pair_own + early[:, place : place + pair_width].astype(f32)) * first_column
     place += pair_width
-    shared_sum = (shared_own + early[:, place : place + shared_width].astype(f32)) * first_column
-    place += shared_width
+    shared_sum = (
+        part_of(shared_own, col, 1) + early[:, place : place + shared_width // 2].astype(f32)
+    ) * first_column
+    shared_sum = in_order(
+        shared_sum, swap(shared_sum.astype(bf16), "col").astype(f32), col, 1
+    )
+    place += shared_width // 2
     step_sum = (
         step_own + early[:, place : place + step_own.shape[1]].astype(f32)
     ) * first_column
     step_sum = to_lanes(lax.dynamic_slice_in_dim(step_sum, quarter * head_count, head_count, 1))
-
-    cot_half = in_order(cotangent, swap(cotangent, "col"), col, 1)
-    hidden_back = product_back(cot_half, part_of(down_weight, 1 - row, 0)).astype(bf16)
-    hidden_back = swap(hidden_back, "row")
-    hidden_back_own = product_back(cot_half, part_of(down_weight, row, 0))
-
+    ffn_spread.wait(spine)
+    ffn_spread.level()
     cosine, sine = rope_tables(length)
     attended = attention_forward(query_sum, pair_sum, cosine, sine)
     heads = to_lanes(jnp.stack([log_rate, step_bias] + [jnp.zeros_like(log_rate)] * 6))
     skip_wide = jnp.repeat(skip_gain, PM)[None, :]
     gain_wide = group_gain[None, :]
-    gained, square, mix_sum, ssm, states = mixer_forward(
+    out_spread.wait(spine)
+    out_spread.level()
+    mix_other, hidden_back = spine.wait(mix_other, hidden_back)
+    hidden_back = swap(hidden_back, "row")
+    ffn_spread.wait(spine)
+    ffn_spread.level()
+    mix_own, mix_other = spine.wait(mix_own, mix_other)
+    mixed_raw, square, mix_sum, ssm, states = mixer_forward(
         mix_own, mix_other, first_column, shared_sum, step_sum, conv_inner, conv_shared,
-        heads, skip_wide, gain_wide,
-    )
+        heads, skip_wide, gain_wide, attended,
+    )
+    square = spine.wait(square)
+    out_other = out_spread.finish(spine)
     group_factor = lax.rsqrt(rows_total(square[:, 0]) / (HM * PM) + norm_epsilon)
     groups = attended.shape[1] // HD
-    normed = (gained.astype(f32) * group_factor[:, None]).astype(bf16)
-    mixed = jnp.concatenate(
-        [normed.reshape(length, groups, -1), attended.reshape(length, groups, HD)], axis=2
-    ).reshape(length, -1)
-    mixed_half = in_order(mixed, swap(mixed, "row"), row, 1)
-
-    out_partial = product(mixed_half, out_weight)
-    second = (
-        residual
-        + part_of(out_partial, col, 1)
-        + swap(part_of(out_partial, 1 - col, 1).astype(bf16), "col").astype(f32)
-    )
+    group_width = mixed_raw.shape[1] // groups
+    is_normed = jnp.arange(mixed_raw.shape[1])[None, :] % group_width < group_width - HD
+    mixed = (
+        mixed_raw.astype(f32) * jnp.where(is_normed, group_factor[:, None], 1.0)
+    ).astype(bf16)
+
+    out_far = sum_cols(product(mixed, out_other), col)
+    out_far = swap(out_far.astype(bf16), "row")
+    out_near = sum_cols(product(mixed, out_own), col)
+    out_far = spine.wait(out_far)
+    second = residual + out_near + out_far.astype(f32)
     second_own = (second * norm_second).astype(bf16)
+    second_far = swap(second_own, "row")
     second_half = in_order(second_own, swap(second_own, "col"), col, 1)
-    second_factor = lax.rsqrt(rows_total(jnp.sum(second * second, axis=1)) / D + norm_epsilon)
+    second_near = swap_dp(second_own, 1)
+    second_square = jnp.sum(second * second, axis=1)
+    second_square = second_square + swap(second_square, "col")
+    second_square_far = swap(second_square, "row")
+    gate_width = gate_own.shape[1]
+    gate_part, up_part = product(second_half, gate_own), product(second_half, up_own)
+    second_far, second_near = spine.wait(second_far, second_near)
+    second_far = in_order(second_far, swap(second_far, "col"), col, 1)
+    second_far_near = swap(second_near, "row")
+    second_near = in_order(second_near, swap(second_near, "col"), col, 1)
+    ffn_other = ffn_spread.finish(spine)
+    second_factor = lax.rsqrt((second_square + second_square_far) / D + norm_epsilon)
     second_column = second_factor[:, None]
-    gate_other = swap(product(second_half, part_of(gate_weight, 1 - row, 1)).astype(bf16), "row")
-    up_other = swap(product(second_half, part_of(up_weight, 1 - row, 1)).astype(bf16), "row")
-    gate_sum = (
-        product(second_half, part_of(gate_weight, row, 1)) + gate_other.astype(f32)
-    ) * second_column
-    up_sum = (
-        product(second_half, part_of(up_weight, row, 1)) + up_other.astype(f32)
-    ) * second_column
+    gate_sum = (gate_part + product(second_far, ffn_other[:, :gate_width])) * second_column
+    up_sum = (up_part + product(second_far, ffn_other[:, gate_width:])) * second_column
     gate_sigmoid = jax.nn.sigmoid(gate_sum)
     gate_act = gate_sum * gate_sigmoid
+    hidden_back = spine.wait(hidden_back)
     hidden_grad = hidden_back_own + hidden_back.astype(f32)
     gate_grad = hidden_grad * up_sum * gate_sigmoid * (1.0 + gate_sum * (1.0 - gate_sigmoid))
     up_grad = hidden_grad * gate_act
-    second_total = rows_total(jnp.sum(gate_grad * gate_sum + up_grad * up_sum, axis=1))
-    gate_low = (gate_grad * second_column).astype(bf16)
-    up_low = (up_grad * second_column).astype(bf16)
-    gate_half = in_order(gate_low, swap(gate_low, "row"), row, 1)
-    up_half = in_order(up_low, swap(up_low, "row"), row, 1)
-    second_in_partial = product_back(gate_half, gate_weight) + product_back(up_half, up_weight)
-    second_in_grad = part_of(second_in_partial, col, 1) + swap(
-        part_of(second_in_partial, 1 - col, 1).astype(bf16), "col"
-    ).astype(f32)
-    cot_own = cotangent.astype(f32)
+    hidden = (gate_act * up_sum).astype(bf16)
+    ffn_grad = jnp.concatenate(
+        [(gate_grad * second_column).astype(bf16), (up_grad * second_column).astype(bf16)], axis=1
+    )
+    second_total = jnp.sum(gate_grad * gate_sum + up_grad * up_sum, axis=1)
+    second_total = second_total + swap(second_total, "col")
+    second_total_far = swap(second_total, "row")
+    ffn_send = swap_dp(part_of(ffn_grad, 1 - near, 1), 1)
+    back_far = sum_cols(product_back(ffn_grad, ffn_other), col)
+    back_far = swap(back_far.astype(bf16), "row")
+    back_near = sum_cols(
+        product_back(ffn_grad[:, :gate_width], gate_own)
+        + product_back(ffn_grad[:, gate_width:], up_own),
+        col,
+    )
+    second_total_far, second_far_near = spine.wait(second_total_far, second_far_near)
+    second_far_near = in_order(second_far_near, swap(second_far_near, "col"), col, 1)
+    back_far = spine.wait(back_far)
+    second_in_grad = back_near + back_far.astype(f32)
     second_grad = (
-        cot_own
+        cotangent.astype(f32)
         + norm_second * second_in_grad
-        - second * (second_factor**2 * second_total / D)[:, None]
+        - second * (second_factor**2 * (second_total + second_total_far) / D)[:, None]
     )
     norm_second_grad = jnp.sum(second_in_grad * second, axis=0)
-
-    branch_own = second_grad.astype(bf16)
-    branch_half = in_order(branch_own, swap(branch_own, "col"), col, 1)
-    mixed_back = swap(
-        product_back(branch_half, part_of(out_weight, 1 - row, 0)).astype(bf16), "row"
-    )
-    mixed_grad = product_back(branch_half, part_of(out_weight, row, 0)) + mixed_back.astype(f32)
-
-    hidden = (gate_act * up_sum).astype(bf16)
-    hidden_half = in_order(hidden, swap(hidden, "row"), row, 1)
-    layer_partial = product(hidden_half, down_weight)
-    layer_out = (
-        second
-        + part_of(layer_partial, col, 1)
-        + swap(part_of(layer_partial, 1 - col, 1).astype(bf16), "col").astype(f32)
-    ).astype(bf16)
-
-    gate_weight_grad = scatter_dp(outer_sum(second_half, gate_half).astype(bf16))
-    up_weight_grad = scatter_dp(outer_sum(second_half, up_half).astype(bf16))
-    down_weight_grad = scatter_dp(outer_sum(hidden_half, cot_half).astype(bf16))
-    out_weight_grad = scatter_dp(outer_sum(mixed_half, branch_half).astype(bf16), True)
-
-    normed_grad = mixed_grad.reshape(length, groups, -1)[:, :, : channels // groups]
-    group_total = rows_total(
-        jnp.sum(
-            normed_grad * gained.astype(f32).reshape(length, groups, -1), axis=(1, 2)
-        )
-    )
-    group_scale = group_factor**3 * group_total / (HM * PM)
+    branch = second_grad.astype(bf16)
+    branch_far = swap(branch, "row")
+    branch_half = in_order(branch, swap(branch, "col"), col, 1)
+    branch_near = swap_dp(branch, 1)
+
+    branch_half, ffn_send = spine.wait(branch_half, ffn_send)
+    ffn_kept = part_of(ffn_grad, near, 1)
+    ffn_scatter = Scatter(
+        spine,
+        (outer_sum(second_half, ffn_kept) + outer_sum(second_near, ffn_send)).astype(bf16),
+        True,
+    )
+    ffn_scatter_far = Scatter(
+        spine,
+        (outer_sum(second_far, ffn_kept) + outer_sum(second_far_near, ffn_send)).astype(bf16),
+        True,
+    )
+    branch_far = spine.wait(branch_far)
+    branch_far = in_order(branch_far, swap(branch_far, "col"), col, 1)
+    mixed_grad = product_back(branch_half, out_own) + product_back(branch_far, out_other)
+
+    group_total = jnp.sum(jnp.where(is_normed, mixed_grad * mixed.astype(f32), 0.0), axis=1)
+    group_total = group_total + swap(group_total, "col")
+    group_total_far = swap(group_total, "row")
+    query_grad, pair_grad, attention_total = attention_backward(
+        query_sum, pair_sum, cosine, sine, mixed_grad, first_column
+    )
+    group_total_far, attention_total = spine.wait(group_total_far, attention_total)
+    group_scale = group_factor**2 * (group_total + group_total_far) / (HM * PM)
+    group_scale, mixed_send, first_send = spine.wait(group_scale, mixed, first_own)
+    mixed_near = swap_dp(near_blocks(mixed_send, 1 - near), 1)
+    mixed_kept = near_blocks(mixed_send, near)
+    mixed_kept_far = swap(mixed_kept, "row")
+    first_far = swap(first_send, "row")
+    first_near = swap_dp(first_send, 1)
     lanes = (
         jnp.arange(channels)[:, None] // PM == jnp.arange(LANES)[None, :]
     ).astype(bf16)
-    query_grad, pair_grad, attention_total = attention_backward(
-        query_sum, pair_sum, cosine, sine, mixed_grad, first_column
-    )
     (
         mix_grad,
         shared_grad,
@@ -845,52 +1018,134 @@
         mix_sum, ssm, states, shared_sum, step_sum, conv_inner, conv_shared, heads, skip_wide,
         gain_wide, lanes, mixed_grad, group_factor[:, None], group_scale[:, None], first_column,
     )
-    first_total = rows_total((attention_total + mixer_total)[:, 0])
-
-    mix_half = in_order(mix_grad, swap(mix_grad, "row"), row, 1)
-    query_half = in_order(query_grad, swap(query_grad, "row"), row, 1)
-    shared_sums = shared_grad.astype(f32) + swap(shared_grad, "col").astype(f32)
-    shared_low = shared_sums.astype(bf16)
-    late = jnp.concatenate([shared_low, pair_grad], axis=1)
-    late = (late.astype(f32) + swap(late, "row").astype(f32)).astype(bf16)
-    shared_low, pair_low = late[:, :shared_width], late[:, shared_width:]
+    mix_grad, shared_grad = spine.wait(mix_grad, shared_grad)
+    own_grads = jnp.concatenate([mix_grad, query_grad], axis=1)
+    grads_send = swap_dp(part_of(own_grads, 1 - near, 1), 1)
+    shared_low = (shared_grad.astype(f32) + swap(shared_grad, "col").astype(f32)).astype(bf16)
+    late = jnp.concatenate(
+        [part_of(shared_low, col, 1), pair_grad, step_grad], axis=1
+    )
+    late_far = swap(late, "row")
+    ffn_scatter.add()
+    ffn_scatter_far.add()
+    mixed_near, first_near = spine.wait(mixed_near, first_near)
+    mixed_near_far = swap(mixed_near, "row")
+    first_far_near = swap(first_near, "row")
+    mixed_kept_far, branch_near = spine.wait(mixed_kept_far, branch_near)
+    mixed_kept = in_order(mixed_kept, mixed_kept_far, row, 1)
+    branch_near = in_order(branch_near, swap(branch_near, "col"), col, 1)
+    first_near = in_order(first_near, swap(first_near, "col"), col, 1)
+    first_far, late_far = spine.wait(first_far, late_far)
+    first_far = in_order(first_far, swap(first_far, "col"), col, 1)
+    half = shared_width // 2
+    late_sum = (late[:, : half + pair_width].astype(f32) + late_far[:, : half + pair_width].astype(f32)).astype(bf16)
+    shared_part, pair_low = late_sum[:, :half], late_sum[:, half:]
     step_two = in_order(
-        step_grad[:, :head_count], swap(step_grad, "row")[:, :head_count], row, 1
+        late[:, half + pair_width :][:, :head_count],
+        late_far[:, half + pair_width :][:, :head_count],
+        row,
+        1,
     )
     step_all = in_order(step_two, swap(step_two, "col"), col, 1)
-
+    shared_low = in_order(shared_part, swap(shared_part, "col"), col, 1)
+    rest = jnp.concatenate([pair_low, shared_part, to_lanes(step_all)], axis=1)
+    rest_send = swap_dp(part_of(rest, 1 - near, 1), 1)
+    mixed_near_far = spine.wait(mixed_near_far)
+    mixed_near = in_order(mixed_near, mixed_near_far, row, 1)
+    out_scatter = Scatter(
+        spine,
+        (outer_sum(mixed_kept, branch_half) + outer_sum(mixed_near, branch_near)).astype(bf16),
+        False,
+        f32,
+    )
+    first_far_near, grads_send = spine.wait(first_far_near, grads_send)
+    first_far_near = in_order(first_far_near, swap(first_far_near, "col"), col, 1)
+    grads_kept = part_of(own_grads, near, 1)
+    mixer_scatter_far = Scatter(
+        spine,
+        (outer_sum(first_far, grads_kept) + outer_sum(first_far_near, grads_send)).astype(bf16),
+        True,
+    )
+    rest_send, hidden = spine.wait(rest_send, hidden)
+    hidden_half = swap(hidden, "row")
+    hidden_near = swap_dp(near_blocks(hidden, 1 - near), 1)
+    cot_near = swap_dp(cotangent, 1)
+    mixer_scatter = Scatter(
+        spine,
+        (
+            outer_sum(
+                first_half, jnp.concatenate([grads_kept, part_of(rest, near, 1)], axis=1)
+            )
+            + outer_sum(first_near, jnp.concatenate([grads_send, rest_send], axis=1))
+        ).astype(bf16),
+        True,
+    )
+
+    def both_halves(scattered, sent):
+        kept = lax.dynamic_index_in_dim(scattered, near, 0, keepdims=False)
+        return jnp.where(near == 0, kept, sent), jnp.where(near == 0, sent, kept)
+
+    def to_neighbour(scattered):
+        return swap_dp(lax.dynamic_index_in_dim(scattered, 1 - near, 0, keepdims=False), 1)
+
+    ffn_near = ffn_scatter.finish()
+    ffn_near_sent = to_neighbour(ffn_near)
+    ffn_far = ffn_scatter_far.finish()
+    ffn_far_sent = to_neighbour(ffn_far)
+    hidden_half, hidden_near, cot_near, mix_send = spine.wait(
+        hidden_half, hidden_near, cot_near, own_grads
+    )
+    hidden_half = in_order(hidden, hidden_half, row, 1)
+    hidden_near_far = swap(hidden_near, "row")
+    own_grads_far = swap(mix_send, "row")
+    cot_near = in_order(cot_near, swap(cot_near, "col"), col, 1)
+    layer_out = (second + sum_cols(product(hidden_half, down_weight), col)).astype(bf16)
+    out_scatter.add()
+    ffn_far_sent, ffn_near_sent, hidden_near_far = spine.wait(
+        ffn_far_sent, ffn_near_sent, hidden_near_far
+    )
+    hidden_near = in_order(hidden_near, hidden_near_far, row, 1)
+    down_scatter = Scatter(
+        spine,
+        (
+            outer_sum(near_blocks(hidden_half, near), cot_half)
+            + outer_sum(hidden_near, cot_near)
+        ).astype(bf16),
+        False,
+        f32,
+    )
+    ffn_near = both_halves(ffn_near, ffn_near_sent)
+    ffn_far = swap(jnp.stack(both_halves(ffn_far, ffn_far_sent)), "row")
+    out_weight_grad = out_scatter.finish()[0]
+    mixer_scatter_far.add()
+    mixer_scatter.add()
+    own_grads_far = spine.wait(own_grads_far)
+    mix_half = in_order(mix_grad, own_grads_far[:, : mix_grad.shape[1]], row, 1)
+    query_half = in_order(query_grad, own_grads_far[:, mix_grad.shape[1] :], row, 1)
     first_in_partial = (
         product_back(mix_half, mixer_in)
         + product_back(query_half, query_weight)
         + product_back(pair_low, kv_flat)
         + 0.5 * (product_back(shared_low, bc_weight) + product_back(step_all, step_weight))
     )
-    first_in_grad = part_of(first_in_partial, col, 1) + swap(
-        part_of(first_in_partial, 1 - col, 1).astype(bf16), "col"
-    ).astype(f32)
+    first_in_grad = sum_cols(first_in_partial, col)
+    first_total = (attention_total + mixer_total)[:, 0]
+    first_total = first_total + swap(first_total, "col")
+    first_total_far = swap(first_total, "row")
+    conv_shared_sum = conv_shared_part + swap(conv_shared_part, "col")
+    conv_shared_far = swap(conv_shared_sum, "row")
+    mixer_far = mixer_scatter_far.finish()
+    mixer_far_sent = to_neighbour(mixer_far)
+    first_total_far, conv_shared_far, ffn_far = spine.wait(first_total_far, conv_shared_far, ffn_far)
+    gate_weight_grad = in_order(ffn_near[0], ffn_far[0], row, 1).astype(f32)
+    up_weight_grad = in_order(ffn_near[1], ffn_far[1], row, 1).astype(f32)
     input_grad = (
         second_grad
         + norm_first * first_in_grad
-        - residual * (first_factor**2 * first_total / D)[:, None]
+        - residual * (first_factor**2 * (first_total + first_total_far) / D)[:, None]
     )
     norm_first_grad = jnp.sum(first_in_grad * residual, axis=0)
-
-    mixer_in_grad = scatter_dp(outer_sum(first_half, mix_half).astype(bf16))
-    rest = jnp.concatenate(
-        [query_half, pair_low, part_of(shared_low, col, 1), to_lanes(step_all)], axis=1
-    )
-    rest_grad = scatter_dp(outer_sum(first_half, rest).astype(bf16))
-    place = query_half.shape[1]
-    query_weight_grad = rest_grad[:, :place]
-    kv_weight_grad = rest_grad[:, place : place + pair_width].reshape((-1,) + kv_weight.shape[1:])
-    place += pair_width
-    bc_own = rest_grad[:, place : place + shared_width // 2]
-    bc_weight_grad = in_order(bc_own, swap(bc_own, "col"), col, 1)
-    place += shared_width // 2
-    step_weight_grad = rest_grad[:, place : place + step_weight.shape[1]]
-
-    conv_shared_sum = conv_shared_part + swap(conv_shared_part, "col")
-    conv_shared_sum = conv_shared_sum + swap(conv_shared_sum, "row")
+    conv_shared_sum = conv_shared_sum + conv_shared_far
     skip_grad = wide_grads[1].reshape(head_count, PM).sum(axis=1)
     pieces = [
         norm_first_grad,
@@ -903,14 +1158,45 @@
         jnp.pad(skip_grad, (0, LANES - head_count)),
     ]
     small = jnp.concatenate(pieces).reshape(-1, LANES)
-    for bit in dp_bits():
-        small = small + swap_dp(small, bit)
+    bits = dp_bits()
+    small_far = swap_dp(small, bits[0])
+    mixer_far_sent = spine.wait(mixer_far_sent)
+    mixer_far = swap(jnp.concatenate(both_halves(mixer_far, mixer_far_sent), axis=1), "row")
+    mixer_near = mixer_scatter.finish()
+    mixer_near_sent = to_neighbour(mixer_near)
+    small = small + spine.wait(small_far)
+    small_far = swap_dp(small, bits[1])
+    down_scatter.add()
+    small = small + spine.wait(small_far)
+    small_far = swap_dp(small, bits[2])
+    mixer_near_sent, mixer_far = spine.wait(mixer_near_sent, mixer_far)
+    mixer_near = both_halves(mixer_near, mixer_near_sent)
+    kept_width = grads_kept.shape[1]
+    mix_width = mix_grad.shape[1]
+    own_sums = jnp.concatenate([mixer_near[0][:, :kept_width], mixer_near[1][:, :kept_width]], axis=1)
+    rest_sums = jnp.concatenate(
+        [mixer_near[0][:, kept_width:], mixer_near[1][:, kept_width:]], axis=1
+    ).astype(f32)
+    mixer_in_grad = in_order(own_sums[:, :mix_width], mixer_far[:, :mix_width], row, 1).astype(f32)
+    query_weight_grad = in_order(
+        own_sums[:, mix_width:], mixer_far[:, mix_width:], row, 1
+    ).astype(f32)
+    kv_weight_grad = rest_sums[:, :pair_width].reshape((-1,) + kv_weight.shape[1:])
+    place = pair_width
+    bc_own = rest_sums[:, place : place + shared_width // 2].astype(bf16)
+    bc_weight_grad = in_order(bc_own, swap(bc_own, "col"), col, 1).astype(f32)
+    place += shared_width // 2
+    step_weight_grad = rest_sums[:, place : place + step_weight.shape[1]]
+    for bit in bits[3:]:
+        small = small + spine.wait(small_far)
+        small_far = swap_dp(small, bit)
+    small = small + spine.wait(small_far)
+    down_weight_grad = down_scatter.finish()[0]
     small = small.reshape(-1)
     sums, place = [], 0
     for piece in pieces:
         sums.append(small[place : place + piece.shape[0]])
         place += piece.shape[0]
-    me, count = lax.axis_index("dp"), lax.axis_size("dp")
 
     def own_block(values_in, axis):
         size = values_in.shape[axis] // count

time: 829 us -> 633 us (0.76)
  waiting for transfers between devices: 507 us -> 248 us
  starting transfers between devices: 51.3 us -> 90.6 us
    ppermute x21 -> x42, waiting for transfers between devices: 307 us -> 158 us  [swap_dp(): lax.ppermute(values_in, 'dp', [(i, i ^ bit) for i in range(lax.axis_size(...]
    ppermute x39 -> x58, waiting for transfers between devices: 200 us -> 90 us  [swap(): return lax.ppermute(values_in, axis, [(0, 1), (1, 0)])]
    ppermute x21 -> x42, starting transfers between devices: 27.3 us -> 57.9 us  [swap_dp(): lax.ppermute(values_in, 'dp', [(i, i ^ bit) for i in range(lax.axis_size(...]
    select_n x12 -> x27, other arithmetic: 8.12 us -> 21.8 us  [in_order(): jnp.where(place == 0, own, other)]
    unnamed x181 -> x231, local copies, waits for them, and re-layouts: 8.17 us -> 18.3 us
    ppermute x39 -> x58, starting transfers between devices: 23.9 us -> 32.7 us  [swap(): return lax.ppermute(values_in, axis, [(0, 1), (1, 0)])]
    add x10 -> x9, other arithmetic: 9.18 us -> 0.76 us  [the longest x1 0.58 us: local(): first_total = first_total + swap(first_total, 'col')]
    dot_general x11 -> x12, matrix products: 23.3 us -> 26.8 us  [product_back(): lax.dot_general(left_side, right_side, (((1,), (1,)), ((), ())), preferre...]
  transfers between devices with their start and end apart: 60 -> 100, of which waited for: 25 -> 32; matrix products, arithmetic and copies ran while one was open for 22% -> 31% of each run, Pallas kernels for 5% -> 10%
where the time goes in v2:
time: 633 us; the launch traced here: 622 us
  waiting for transfers between devices  248 us (39%)
  starting transfers between devices  90.6 us (14%)
  matrix products  77.5 us (12%)
  other arithmetic  74 us (12%)
  Pallas kernels  65 us (10%)
  local copies, waits for them, and re-layouts  64.3 us (10%)
    ppermute x42, waiting for transfers between devices, swap_dp(): lax.ppermute(values_in, 'dp', [(i, i ^ bit) for i in range(lax.axis_size(...  158 us
    ppermute x58, waiting for transfers between devices, swap(): return lax.ppermute(values_in, axis, [(0, 1), (1, 0)])  90 us
    ppermute x42, starting transfers between devices, swap_dp(): lax.ppermute(values_in, 'dp', [(i, i ^ bit) for i in range(lax.axis_size(...  57.9 us
    pallas_call x4, Pallas kernels, call(): pl.pallas_call(kernel, out_shape=outs, in_specs=[pl.BlockSpec(memory_spac...  57.4 us
    ppermute x58, starting transfers between devices, swap(): return lax.ppermute(values_in, axis, [(0, 1), (1, 0)])  32.7 us
    dot_general x14, matrix products, product(): return jnp.dot(left_side, right_side, preferred_element_type=f32)  32.6 us
    dot_general x12, matrix products, product_back(): lax.dot_general(left_side, right_side, (((1,), (1,)), ((), ())), preferre...  26.8 us
    select_n x27, other arithmetic, in_order(): jnp.where(place == 0, own, other)  21.8 us
  transfers between devices with their start and end apart: 100, of which 32 were waited for; matrix products, arithmetic and copies ran while one was open for 31% of the time, Pallas kernels for 10%

profile of v2, /device:TPU:0, one launch (start us, length us, event | category | flops | bytes accessed | tf_op | source)
XLA Modules:
  0.0 622.0 jit_solution(7093335079807874990)
XLA Ops:
  33.2 5.3 fusion.8
  40.1 3.5 fusion.4.own_ref
  48.0 4.2 collective-permute-done.8
  56.9 7.3 %collective-permute-done.10.refs_2_ = bf16[128,2048]{1,0:T(8,128)(2,1)} collective-permute-done((bf16[128,2048]{1,0:T(8,128)(2,1)}, bf16[128,2048]{1,0:T(8,128)(2,1)}, u32[]{:S(2)}, u32[]{:S(2)}) %collective-permute-start.10) | collective-permute-done | bytes 524320 | tf_op jit(solution)/shard_map/ppermute | solution.py:94
  80.8 3.9 shard_map.330.attended_ref
  87.6 11.2 %collective-permute-done.19.refs_6_ = bf16[128,2048]{1,0:T(8,128)(2,1)} collective-permute-done((bf16[128,2048]{1,0:T(8,128)(2,1)}, bf16[128,2048]{1,0:T(8,128)(2,1)}, u32[]{:S(2)}, u32[]{:S(2)}) %collective-permute-start.19) | collective-permute-done | bytes 524320 | tf_op jit(solution)/shard_map/ppermute | solution.py:94
  98.9 16.7 %shard_map.331 = (bf16[512,1024]{1,0:T(8,128)(2,1)}, f32[512,1]{1,0:T(8,128)}, f32[512,1536]{1,0:T(8,128)}, f32[512,768]{1,0:T(8,128)}, bf16[1024,768]{1,0:T(8,128)(2,1)}) custom-call(f32[512,1536]{1,0:T(8,128)} %fusion.4.own_ref, bf16[512,1536]{1,0:T(8,128)(2,1)} %collective-permute-done.15.other_ref, f32[512,1]{1,0:T(8,128)} %copy.90.factor_ref, ...), custom_call_target="tpu_custom_call" | custom-call | flops 100000000 | bytes 1000000 | tf_op jit(solution)/shard_map/pallas_call | solution.py:593
  131.7 12.4 %collective-permute-done.26 = bf16[512,512]{1,0:T(8,128)(2,1)S(1)} collective-permute-done((bf16[512,512]{1,0:T(8,128)(2,1)S(1)}, bf16[512,512]{1,0:T(8,128)(2,1)S(1)}, u32[]{:S(2)}, u32[]{:S(2)}) %collective-permute-start.26) | collective-permute-done | bytes 524320 | tf_op jit(solution)/shard_map/ppermute | solution.py:45
  150.6 16.0 %collective-permute-done.34 = f32[512]{0:T(512)S(1)} collective-permute-done((f32[512]{0:T(512)S(1)}, f32[512]{0:T(512)S(1)}, u32[]{:S(2)}, u32[]{:S(2)}) %collective-permute-start.34) | collective-permute-done | bytes 2080 | tf_op jit(solution)/shard_map/ppermute | solution.py:45
  166.6 10.7 %collective-permute-done.27 = bf16[512,512]{1,0:T(8,128)(2,1)S(1)} collective-permute-done((bf16[512,512]{1,0:T(8,128)(2,1)}, bf16[512,512]{1,0:T(8,128)(2,1)S(1)}, u32[]{:S(2)}, u32[]{:S(2)}) %collective-permute-start.27) | collective-permute-done | bytes 524320 | tf_op jit(solution)/shard_map/ppermute | solution.py:45
  179.0 4.5 shard_map.333
  193.5 3.7 multiply_convert_fusion.2
  211.3 8.0 %collective-permute-done.36 = f32[512]{0:T(512)S(1)} collective-permute-done((f32[512]{0:T(512)S(1)}, f32[512]{0:T(512)S(1)}, u32[]{:S(2)}, u32[]{:S(2)}) %collective-permute-start.36) | collective-permute-done | bytes 2080 | tf_op jit(solution)/shard_map/ppermute | solution.py:45
  219.3 3.5 fusion.200
  227.5 9.9 %collective-permute-done.43 = bf16[512,512]{1,0:T(8,128)(2,1)S(1)} collective-permute-done((bf16[512,512]{1,0:T(8,128)(2,1)}, bf16[512,512]{1,0:T(8,128)(2,1)S(1)}, u32[]{:S(2)}, u32[]{:S(2)}) %collective-permute-start.43) | collective-permute-done | bytes 524320 | tf_op jit(solution)/shard_map/ppermute | solution.py:45
  257.5 7.6 %shard_map.334 = (bf16[512,256]{1,0:T(8,128)(2,1)}, bf16[512,256]{1,0:T(8,128)(2,1)}, f32[512,1]{1,0:T(8,128)}) custom-call(f32[512,256]{1,0:T(8,128)} %fusion.68.query_ref, f32[512,256]{1,0:T(8,128)} %get-tuple-element.404.pair_ref, f32[512,128]{1,0:T(8,128)} %get-tuple-element.446.cosine_ref, f32[512,128]{1,0:T(8,128)} %get-tuple-element.447.sine_ref, ...), custom_call_target="tpu_custom_call" | custom-call | flops 100000000 | bytes 1000000 | tf_op jit(solution)/shard_map/pallas_call | solution.py:593
  266.0 29.0 %shard_map.335 = (bf16[512,1536]{1,0:T(8,128)(2,1)}, bf16[512,512]{1,0:T(8,128)(2,1)}, bf16[512,128]{1,0:T(8,128)(2,1)}, f32[4,768]{1,0:T(4,128)}, f32[4,512]{1,...) custom-call(f32[512,1536]{1,0:T(8,128)} %get-tuple-element.197.mix_ref, ...), custom_call_target="tpu_custom_call" | custom-call | flops 100000000 | bytes 1000000 | tf_op jit(solution)/shard_map/pallas_call | solution.py:593
  325.8 8.2 %collective-permute-done.52 = bf16[512,512]{1,0:T(8,128)(2,1)S(1)} collective-permute-done((bf16[512,512]{1,0:T(8,128)(2,1)S(1)}, bf16[512,512]{1,0:T(8,128)(2,1)S(1)}, u32[]{:S(2)}, u32[]{:S(2)}) %collective-permute-start.52) | collective-permute-done | bytes 524320 | tf_op jit(solution)/shard_map/ppermute | solution.py:94
  337.8 16.5 %collective-permute-done.64 = bf16[2,128,1024]{2,1,0:T(8,128)(2,1)S(1)} collective-permute-done((bf16[2,128,1024]{2,1,0:T(8,128)(2,1)S(1)}, bf16[2,128,1024]{2,1,0:T(8,128)(2,1)S(1)}, u32[]{:S(2)}, u32[]{:S(2)}) %collective-permute-start.64) | collective-permute-done | bytes 524320 | tf_op jit(solution)/shard_map/ppermute | solution.py:94
  355.4 9.6 %collective-permute-done.63 = bf16[2,128,1024]{2,1,0:T(8,128)(2,1)S(1)} collective-permute-done((bf16[2,128,1024]{2,1,0:T(8,128)(2,1)S(1)}, bf16[2,128,1024]{2,1,0:T(8,128)(2,1)S(1)}, u32[]{:S(2)}, u32[]{:S(2)}) %collective-permute-start.63) | collective-permute-done | bytes 524320 | tf_op jit(solution)/shard_map/ppermute | solution.py:94
  381.0 6.3 %collective-permute-done.57 = bf16[512,640]{1,0:T(8,128)(2,1)S(1)} collective-permute-done((bf16[512,640]{1,0:T(8,128)(2,1)S(1)}, bf16[512,640]{1,0:T(8,128)(2,1)S(1)}, u32[]{:S(2)}, u32[]{:S(2)}) %collective-permute-start.57) | collective-permute-done | bytes 655392 | tf_op jit(solution)/shard_map/ppermute | solution.py:45
  421.7 7.0 %reshape.237 = bf16[2,2,2,128,1216]{3,2,1,0,4:T(2,128)(2,1)} reshape(bf16[1024,1216]{0,1:T(8,128)(2,1)} %add_convert_fusion) | data formatting | bytes 4980736 | tf_op jit(solution)/shard_map/reshape | solution.py:118
  432.1 8.9 %collective-permute-done.96 = bf16[1,256,1024]{2,1,0:T(8,128)(2,1)} collective-permute-done((bf16[1,256,1024]{2,1,0:T(8,128)(2,1)}, bf16[1,256,1024]{2,1,0:T(8,128)(2,1)}, u32[]{:S(2)}, u32[]{:S(2)}) %collective-permute-start.96) | collective-permute-done | bytes 524320 | tf_op jit(solution)/shard_map/ppermute | solution.py:94
  447.0 6.4 %collective-permute-done.66 = bf16[512,512]{1,0:T(8,128)(2,1)S(1)} collective-permute-done((bf16[512,512]{1,0:T(8,128)(2,1)S(1)}, bf16[512,512]{1,0:T(8,128)(2,1)S(1)}, u32[]{:S(2)}, u32[]{:S(2)}) %collective-permute-start.66) | collective-permute-done | bytes 524320 | tf_op jit(solution)/shard_map/ppermute | solution.py:94
  463.4 27.1 %collective-permute-done.86 = bf16[2,2,128,1216]{2,1,0,3:T(2,128)(2,1)S(1)} collective-permute-done((bf16[2,2,128,1216]{2,1,0,3:T(2,128)(2,1)S(1)}, bf16[2,2,128,1216]{2,1,0,3:T(2,128)(2,1)S(1)}, u32[]{:S(2)}, u32[]{:S(2)}) %collective-permute-start.86) | collective-permute-done | bytes 1245216 | tf_op jit(solution)/shard_map/ppermute | solution.py:94
  494.6 4.6 collective-permute-done.93
  500.5 5.0 collective-permute-done.79
  515.4 22.8 %collective-permute-done.87 = bf16[2,128,1216]{1,0,2:T(2,128)(2,1)S(1)} collective-permute-done((bf16[2,128,1216]{1,0,2:T(2,128)(2,1)S(1)}, bf16[2,128,1216]{1,0,2:T(2,128)(2,1)S(1)}, u32[]{:S(2)}, u32[]{:S(2)}) %collective-permute-start.87) | collective-permute-done | bytes 622624 | tf_op jit(solution)/shard_map/ppermute | solution.py:94
  543.8 15.7 %collective-permute-done.81 = bf16[2,128,1024]{2,1,0:T(8,128)(2,1)} collective-permute-done((bf16[2,128,1024]{2,1,0:T(8,128)(2,1)}, bf16[2,128,1024]{2,1,0:T(8,128)(2,1)}, u32[]{:S(2)}, u32[]{:S(2)}) %collective-permute-start.81) | collective-permute-done | bytes 524320 | tf_op jit(solution)/shard_map/ppermute | solution.py:45
  571.0 6.0 fusion
  597.5 15.5 %collective-permute-done.99 = bf16[1,256,1024]{2,1,0:T(8,128)(2,1)S(1)} collective-permute-done((bf16[1,256,1024]{2,1,0:T(8,128)(2,1)S(1)}, bf16[1,256,1024]{2,1,0:T(8,128)(2,1)S(1)}, u32[]{:S(2)}, u32[]{:S(2)}) %collective-permute-start.99) | collective-permute-done | bytes 524320 | tf_op jit(solution)/shard_map/ppermute | solution.py:94
  614.3 3.6 collective-permute-done.84
  (627 shorter events, 297.7 us)
Async XLA Ops:
  17.0 26.6 %collective-permute-start.4 = (bf16[128,1024]{1,0:T(8,128)(2,1)S(1)}, bf16[128,1024]{1,0:T(8,128)(2,1)}, u32[]{:S(2)}, u32[]{:S(2)}) collective-permute-start(bf16[128,1024]{1,0:T(8,128)(2,1)S(1)} %collective-permute-done.refs_0_), channel_id=1, source_target_pairs={{0,8},{4,12},{8,0},{12,4},{16,24},{20,28},{24,16},{28,20},{1,9},{5... | collective-permute-start | bytes 786440 | tf_op jit(solution)/shard_map/ppermute | solution.py:94
  18.6 26.5 %collective-permute-start.5 = (bf16[128,1024]{1,0:T(8,128)(2,1)S(1)}, bf16[128,1024]{1,0:T(8,128)(2,1)}, u32[]{:S(2)}, u32[]{:S(2)}) collective-permute-start(bf16[128,1024]{1,0:T(8,128)(2,1)S(1)} %collective-permute-done.refs_0_), channel_id=1, source_target_pairs={{0,4},{4,0},{8,12},{12,8},{16,20},{20,16},{24,28},{28,24},{1,5},{5... | collective-permute-start | bytes 786440 | tf_op jit(solution)/shard_map/ppermute | solution.py:94
  29.8 26.5 %collective-permute-start.9 = (bf16[128,2048]{1,0:T(8,128)(2,1)}, bf16[128,2048]{1,0:T(8,128)(2,1)}, u32[]{:S(2)}, u32[]{:S(2)}) collective-permute-start(bf16[128,2048]{1,0:T(8,128)(2,1)} %collective-permute-done.2.refs_0_), channel_id=1, source_target_pairs={{0,16},{4,20},{8,24},{12,28},{16,0},{20,4},{24,8},{28,12},{1,17},{... | collective-permute-start | bytes 1572872 | tf_op jit(solution)/shard_map/ppermute | solution.py:94
  45.1 40.8 %collective-permute-start.15 = (bf16[512,1536]{1,0:T(8,128)(2,1)}, bf16[512,1536]{1,0:T(8,128)(2,1)}, u32[]{:S(2)}, u32[]{:S(2)}) collective-permute-start(bf16[512,1536]{1,0:T(8,128)(2,1)} %fusion.8), channel_id=1, source_target_pairs={{0,2},{2,0},{1,3},{3,1},{4,6},{6,4},{5,7},{7,5},{8,10},{10,8},{9,1... | collective-permute-start | bytes 4718600 | tf_op jit(solution)/shard_map/ppermute | solution.py:45
  78.0 40.5 %collective-permute-start.24 = (bf16[128,1024]{1,0:T(8,128)(2,1)S(1)}, bf16[128,1024]{1,0:T(8,128)(2,1)}, u32[]{:S(2)}, u32[]{:S(2)}) collective-permute-start(bf16[128,1024]{1,0:T(8,128)(2,1)S(1)} %collective-permute-done.12.refs_4_), channel_id=1, source_target_pairs={{0,4},{4,0},{8,12},{12,8},{16,20},{20,16},{24,28},{28,24},{1,5},{5... | collective-permute-start | bytes 786440 | tf_op jit(solution)/shard_map/ppermute | solution.py:94
  131.1 46.2 %collective-permute-start.30 = (bf16[512,1024]{1,0:T(8,128)(2,1)}, bf16[512,1024]{1,0:T(8,128)(2,1)}, u32[]{:S(2)}, u32[]{:S(2)}) collective-permute-start(bf16[512,1024]{1,0:T(8,128)(2,1)} %fusion.56), channel_id=1, source_target_pairs={{0,2},{2,0},{1,3},{3,1},{4,6},{6,4},{5,7},{7,5},{8,10},{10,8},{9,1... | collective-permute-start | bytes 3145736 | tf_op jit(solution)/shard_map/ppermute | solution.py:45
  148.0 29.4 %collective-permute-start.27 = (bf16[512,512]{1,0:T(8,128)(2,1)}, bf16[512,512]{1,0:T(8,128)(2,1)S(1)}, u32[]{:S(2)}, u32[]{:S(2)}) collective-permute-start(bf16[512,512]{1,0:T(8,128)(2,1)} %multiply_convert_fusion.4), channel_id=1, source_target_pairs={{0,2},{2,0},{1,3},{3,1},{4,6},{6,4},{5,7},{7,5},{8,10},{10,8},{9,1... | collective-permute-start | bytes 1572872 | tf_op jit(solution)/shard_map/ppermute | solution.py:45
  148.5 28.8 %collective-permute-start.28 = (bf16[512,512]{1,0:T(8,128)(2,1)}, bf16[512,512]{1,0:T(8,128)(2,1)}, u32[]{:S(2)}, u32[]{:S(2)}) collective-permute-start(bf16[512,512]{1,0:T(8,128)(2,1)} %multiply_convert_fusion.4), channel_id=1, source_target_pairs={{0,4},{4,0},{8,12},{12,8},{16,20},{20,16},{24,28},{28,24},{1,5},{5... | collective-permute-start | bytes 1572872 | tf_op jit(solution)/shard_map/ppermute | solution.py:94
  150.1 27.3 %collective-permute-start.29 = (bf16[128,2048]{1,0:T(8,128)(2,1)}, bf16[128,2048]{1,0:T(8,128)(2,1)}, u32[]{:S(2)}, u32[]{:S(2)}) collective-permute-start(bf16[128,2048]{1,0:T(8,128)(2,1)} %collective-permute-done.17.refs_4_), channel_id=1, source_target_pairs={{0,4},{4,0},{8,12},{12,8},{16,20},{20,16},{24,28},{28,24},{1,5},{5... | collective-permute-start | bytes 1572872 | tf_op jit(solution)/shard_map/ppermute | solution.py:94
  177.4 33.5 %collective-permute-start.37 = (bf16[512,512]{1,0:T(8,128)(2,1)}, bf16[512,512]{1,0:T(8,128)(2,1)}, u32[]{:S(2)}, u32[]{:S(2)}) collective-permute-start(bf16[512,512]{1,0:T(8,128)(2,1)} %collective-permute-done.28), channel_id=1, source_target_pairs={{0,2},{2,0},{1,3},{3,1},{4,6},{6,4},{5,7},{7,5},{8,10},{10,8},{9,1... | collective-permute-start | bytes 1572872 | tf_op jit(solution)/shard_map/ppermute | solution.py:45
  210.9 27.7 %collective-permute-start.42 = (bf16[512,1024]{1,0:T(8,128)(2,1)S(1)}, bf16[512,1024]{1,0:T(8,128)(2,1)S(1)}, u32[]{:S(2)}, u32[]{:S(2)}) collective-permute-start(bf16[512,1024]{1,0:T(8,128)(2,1)S(1)} %fusion.74), channel_id=1, source_target_pairs={{0,4},{4,0},{8,12},{12,8},{16,20},{20,16},{24,28},{28,24},{1,5},{5... | collective-permute-start | bytes 3145736 | tf_op jit(solution)/shard_map/ppermute | solution.py:94
  225.9 109.6 %collective-permute-start.54 = (bf16[512,512]{1,0:T(8,128)(2,1)}, bf16[512,512]{1,0:T(8,128)(2,1)}, u32[]{:S(2)}, u32[]{:S(2)}) collective-permute-start(bf16[512,512]{1,0:T(8,128)(2,1)} %get-tuple-element.337), channel_id=1, source_target_pairs={{0,4},{4,0},{8,12},{12,8},{16,20},{20,16},{24,28},{28,24},{1,5},{5... | collective-permute-start | bytes 1572872 | tf_op jit(solution)/shard_map/ppermute | solution.py:94
  243.1 68.0 %collective-permute-start.50 = (bf16[2,2,128,1024]{3,2,1,0:T(8,128)(2,1)}, bf16[2,2,128,1024]{3,2,1,0:T(8,128)(2,1)}, u32[]{:S(2)}, u32[]{:S(2)}) collective-permute-start(bf16[2,2,128,1024]{3,2,1,0:T(8,128)(2,1)} %dynamic-slice_bitcast_fusion.3), channel_id=1, source_target_pairs={{0,8},{4,12},{8,0},{12,4},{16,24},{20,28},{24,16},{28,20},{1,9},{5... | collective-permute-start | bytes 3145736 | tf_op jit(solution)/shard_map/ppermute | solution.py:94
  255.9 57.7 %collective-permute-start.48 = (bf16[2,2,128,1024]{3,2,1,0:T(8,128)(2,1)}, bf16[2,2,128,1024]{3,2,1,0:T(8,128)(2,1)}, u32[]{:S(2)}, u32[]{:S(2)}) collective-permute-start(bf16[2,2,128,1024]{3,2,1,0:T(8,128)(2,1)} %dynamic-slice_bitcast_fusion.4), channel_id=1, source_target_pairs={{0,8},{4,12},{8,0},{12,4},{16,24},{20,28},{24,16},{28,20},{1,9},{5... | collective-permute-start | bytes 3145736 | tf_op jit(solution)/shard_map/ppermute | solution.py:94
  316.8 37.5 %collective-permute-start.64 = (bf16[2,128,1024]{2,1,0:T(8,128)(2,1)S(1)}, bf16[2,128,1024]{2,1,0:T(8,128)(2,1)S(1)}, u32[]{:S(2)}, u32[]{:S(2)}) collective-permute-start(bf16[2,128,1024]{2,1,0:T(8,128)(2,1)S(1)} %dynamic-slice_bitcast_fusion.9), channel_id=1, source_target_pairs={{0,16},{4,20},{8,24},{12,28},{16,0},{20,4},{24,8},{28,12},{1,17},{... | collective-permute-start | bytes 1572872 | tf_op jit(solution)/shard_map/ppermute | solution.py:94
  323.1 41.8 %collective-permute-start.63 = (bf16[2,128,1024]{2,1,0:T(8,128)(2,1)S(1)}, bf16[2,128,1024]{2,1,0:T(8,128)(2,1)S(1)}, u32[]{:S(2)}, u32[]{:S(2)}) collective-permute-start(bf16[2,128,1024]{2,1,0:T(8,128)(2,1)S(1)} %dynamic-slice_bitcast_fusion.10), channel_id=1, source_target_pairs={{0,16},{4,20},{8,24},{12,28},{16,0},{20,4},{24,8},{28,12},{1,17},{... | collective-permute-start | bytes 1572872 | tf_op jit(solution)/shard_map/ppermute | solution.py:94
  334.0 45.9 %collective-permute-start.55 = (bf16[512,512]{1,0:T(8,128)(2,1)S(1)}, bf16[512,512]{1,0:T(8,128)(2,1)S(1)}, u32[]{:S(2)}, u32[]{:S(2)}) collective-permute-start(bf16[512,512]{1,0:T(8,128)(2,1)S(1)} %copy-done.39), channel_id=1, source_target_pairs={{0,2},{2,0},{1,3},{3,1},{4,6},{6,4},{5,7},{7,5},{8,10},{10,8},{9,1... | collective-permute-start | bytes 1572872 | tf_op jit(solution)/shard_map/ppermute | solution.py:45
  335.5 40.2 %collective-permute-start.60 = (bf16[512,896]{1,0:T(8,128)(2,1)S(1)}, bf16[512,896]{1,0:T(8,128)(2,1)S(1)}, u32[]{:S(2)}, u32[]{:S(2)}) collective-permute-start(bf16[512,896]{1,0:T(8,128)(2,1)S(1)} %copy-done.62), channel_id=1, source_target_pairs={{0,4},{4,0},{8,12},{12,8},{16,20},{20,16},{24,28},{28,24},{1,5},{5... | collective-permute-start | bytes 2752520 | tf_op jit(solution)/shard_map/ppermute | solution.py:94
  337.0 40.3 %collective-permute-start.59 = (bf16[512,512]{1,0:T(8,128)(2,1)S(1)}, bf16[512,512]{1,0:T(8,128)(2,1)}, u32[]{:S(2)}, u32[]{:S(2)}) collective-permute-start(bf16[512,512]{1,0:T(8,128)(2,1)S(1)} %collective-permute-done.52), channel_id=1, source_target_pairs={{0,2},{2,0},{1,3},{3,1},{4,6},{6,4},{5,7},{7,5},{8,10},{10,8},{9,1... | collective-permute-start | bytes 1572872 | tf_op jit(solution)/shard_map/ppermute | solution.py:45
  375.7 71.2 %collective-permute-start.67 = (bf16[512,512]{1,0:T(8,128)(2,1)}, bf16[512,512]{1,0:T(8,128)(2,1)}, u32[]{:S(2)}, u32[]{:S(2)}) collective-permute-start(bf16[512,512]{1,0:T(8,128)(2,1)} %param.37), channel_id=1, source_target_pairs={{0,4},{4,0},{8,12},{12,8},{16,20},{20,16},{24,28},{28,24},{1,5},{5... | collective-permute-start | bytes 1572872 | tf_op jit(solution)/shard_map/ppermute | solution.py:94
  377.3 165.9 %collective-permute-start.73 = (f32[512]{0:T(512)}, f32[512]{0:T(512)}, u32[]{:S(2)}, u32[]{:S(2)}) collective-permute-start(f32[512]{0:T(512)} %add.480), channel_id=1, source_target_pairs={{0,2},{2,0},{1,3},{3,1},{4,6},{6,4},{5,7},{7,5},{8,10},{10,8},{9,1... | collective-permute-start | bytes 6152 | tf_op jit(solution)/shard_map/ppermute | solution.py:45
  380.0 31.7 %collective-permute-start.77 = (bf16[2,1,256,1024]{3,2,1,0:T(8,128)(2,1)}, bf16[2,1,256,1024]{3,2,1,0:T(8,128)(2,1)}, u32[]{:S(2)}, u32[]{:S(2)}) collective-permute-start(bf16[2,1,256,1024]{3,2,1,0:T(8,128)(2,1)} %dynamic-slice_bitcast_fusion.2), channel_id=1, source_target_pairs={{0,8},{4,12},{8,0},{12,4},{16,24},{20,28},{24,16},{28,20},{1,9},{5... | collective-permute-start | bytes 3145736 | tf_op jit(solution)/shard_map/ppermute | solution.py:94
  404.8 40.0 %collective-permute-start.91 = (bf16[2,2,128,896]{3,2,1,0:T(8,128)(2,1)}, bf16[2,2,128,896]{3,2,1,0:T(8,128)(2,1)}, u32[]{:S(2)}, u32[]{:S(2)}) collective-permute-start(bf16[2,2,128,896]{3,2,1,0:T(8,128)(2,1)} %dynamic-slice_bitcast_fusion.5), channel_id=1, source_target_pairs={{0,8},{4,12},{8,0},{12,4},{16,24},{20,28},{24,16},{28,20},{1,9},{5... | collective-permute-start | bytes 2752520 | tf_op jit(solution)/shard_map/ppermute | solution.py:94
  408.6 47.8 %collective-permute-start.65 = (bf16[512,1024]{1,0:T(8,128)(2,1)S(1)}, bf16[512,1024]{1,0:T(8,128)(2,1)}, u32[]{:S(2)}, u32[]{:S(2)}) collective-permute-start(bf16[512,1024]{1,0:T(8,128)(2,1)S(1)} %copy-done.22), channel_id=1, source_target_pairs={{0,2},{2,0},{1,3},{3,1},{4,6},{6,4},{5,7},{7,5},{8,10},{10,8},{9,1... | collective-permute-start | bytes 3145736 | tf_op jit(solution)/shard_map/ppermute | solution.py:45
  444.8 98.5 %collective-permute-start.75 = (f32[4,512]{1,0:T(4,128)S(1)}, f32[4,512]{1,0:T(4,128)S(1)}, u32[]{:S(2)}, u32[]{:S(2)}) collective-permute-start(f32[4,512]{1,0:T(4,128)S(1)} %copy-done.90), channel_id=1, source_target_pairs={{0,2},{2,0},{1,3},{3,1},{4,6},{6,4},{5,7},{7,5},{8,10},{10,8},{9,1... | collective-permute-start | bytes 24584 | tf_op jit(solution)/shard_map/ppermute | solution.py:45
  446.9 53.5 %collective-permute-start.78 = (bf16[128,1024]{1,0:T(8,128)(2,1)S(1)}, bf16[128,1024]{1,0:T(8,128)(2,1)S(1)}, u32[]{:S(2)}, u32[]{:S(2)}) collective-permute-start(bf16[128,1024]{1,0:T(8,128)(2,1)S(1)} %copy-done.85), channel_id=1, source_target_pairs={{0,4},{4,0},{8,12},{12,8},{16,20},{20,16},{24,28},{28,24},{1,5},{5... | collective-permute-start | bytes 786440 | tf_op jit(solution)/shard_map/ppermute | solution.py:94
  453.5 37.0 %collective-permute-start.86 = (bf16[2,2,128,1216]{2,1,0,3:T(2,128)(2,1)S(1)}, bf16[2,2,128,1216]{2,1,0,3:T(2,128)(2,1)S(1)}, u32[]{:S(2)}, u32[]{:S(2)}) collective-permute-start(bf16[2,2,128,1216]{2,1,0,3:T(2,128)(2,1)S(1)} %dynamic-slice_bitcast_fusion), channel_id=1, source_target_pairs={{0,8},{4,12},{8,0},{12,4},{16,24},{20,28},{24,16},{28,20},{1,9},{5... | collective-permute-start | bytes 3735560 | tf_op jit(solution)/shard_map/ppermute | solution.py:94
  456.4 35.6 %collective-permute-start.92 = (bf16[2,128,896]{2,1,0:T(8,128)(2,1)S(1)}, bf16[2,128,896]{2,1,0:T(8,128)(2,1)S(1)}, u32[]{:S(2)}, u32[]{:S(2)}) collective-permute-start(bf16[2,128,896]{2,1,0:T(8,128)(2,1)S(1)} %dynamic-slice_bitcast_fusion.11), channel_id=1, source_target_pairs={{0,16},{4,20},{8,24},{12,28},{16,0},{20,4},{24,8},{28,12},{1,17},{... | collective-permute-start | bytes 1376264 | tf_op jit(solution)/shard_map/ppermute | solution.py:94
  505.5 62.6 %collective-permute-start.69 = (bf16[512,1792]{1,0:T(8,128)(2,1)}, bf16[512,1792]{1,0:T(8,128)(2,1)}, u32[]{:S(2)}, u32[]{:S(2)}) collective-permute-start(bf16[512,1792]{1,0:T(8,128)(2,1)} %constant_dynamic-update-slice_fusion), channel_id=1, source_target_pairs={{0,2},{2,0},{1,3},{3,1},{4,6},{6,4},{5,7},{7,5},{8,10},{10,8},{9,1... | collective-permute-start | bytes 5505032 | tf_op jit(solution)/shard_map/ppermute | solution.py:45
  507.4 30.7 %collective-permute-start.87 = (bf16[2,128,1216]{1,0,2:T(2,128)(2,1)S(1)}, bf16[2,128,1216]{1,0,2:T(2,128)(2,1)S(1)}, u32[]{:S(2)}, u32[]{:S(2)}) collective-permute-start(bf16[2,128,1216]{1,0,2:T(2,128)(2,1)S(1)} %dynamic-slice_bitcast_fusion.6), channel_id=1, source_target_pairs={{0,16},{4,20},{8,24},{12,28},{16,0},{20,4},{24,8},{28,12},{1,17},{... | collective-permute-start | bytes 1867784 | tf_op jit(solution)/shard_map/ppermute | solution.py:94
  510.0 49.6 %collective-permute-start.81 = (bf16[2,128,1024]{2,1,0:T(8,128)(2,1)}, bf16[2,128,1024]{2,1,0:T(8,128)(2,1)}, u32[]{:S(2)}, u32[]{:S(2)}) collective-permute-start(bf16[2,128,1024]{2,1,0:T(8,128)(2,1)} %pad_maximum_fusion.11), channel_id=1, source_target_pairs={{0,2},{2,0},{1,3},{3,1},{4,6},{6,4},{5,7},{7,5},{8,10},{10,8},{9,1... | collective-permute-start | bytes 1572872 | tf_op jit(solution)/shard_map/ppermute | solution.py:45
  543.2 41.9 %collective-permute-start.98 = (bf16[2,1,256,1024]{3,2,1,0:T(8,128)(2,1)}, bf16[2,1,256,1024]{3,2,1,0:T(8,128)(2,1)S(1)}, u32[]{:S(2)}, u32[]{:S(2)}) collective-permute-start(bf16[2,1,256,1024]{3,2,1,0:T(8,128)(2,1)} %dynamic-slice_bitcast_fusion.1), channel_id=1, source_target_pairs={{0,8},{4,12},{8,0},{12,4},{16,24},{20,28},{24,16},{28,20},{1,9},{5... | collective-permute-start | bytes 3145736 | tf_op jit(solution)/shard_map/ppermute | solution.py:94
  (178 other events, 1508.0 us)

commit v3 on v2

--- a/solution.py
+++ b/solution.py
@@ -380,6 +380,7 @@
     group_factor_ref,
     group_scale_ref,
     factor_ref,
+    query_grad_ref,
     mix_grad_ref,
     shared_grad_ref,
     step_grad_ref,
@@ -404,6 +405,7 @@
     length = ssm_ref.shape[0]
     group_pairs = pairs // (grad_ref.shape[1] // (pairs * LANES // 2 + HD))
     low = low_lanes()
+    mix_grad_ref[:, 2 * pairs * LANES :] = query_grad_ref[...]
     for pair in range(pairs):
         first = slice(2 * pair * LANES, (2 * pair + 1) * LANES)
         second = slice((2 * pair + 1) * LANES, (2 * pair + 2) * LANES)
@@ -636,14 +638,14 @@
 
 def mixer_backward(
     mix, ssm, states, shared, step, taps, shared_taps, heads, skip, gain, lanes, grad,
-    group_factor, group_scale, factor,
+    group_factor, group_scale, factor, query_grad,
 ):
     length, width = mix.shape
     channels = width // 2
     return call(
         mixer_backward_kernel,
         [
-            shape((length, width), bf16),
+            shape((length, width + query_grad.shape[1]), bf16),
             shape((length, 2 * NS), bf16),
             shape((length, LANES), bf16),
             shape((taps.shape[0], channels)),
@@ -667,7 +669,7 @@
         ],
         10**8,
         mix, ssm, states, shared, step, taps, shared_taps, heads, skip, gain, lanes, grad,
-        group_factor, group_scale, factor,
+        group_factor, group_scale, factor, query_grad,
     )
 
 
@@ -812,7 +814,7 @@
     channels = group_gain.shape[0]
     kv_flat = kv_weight.reshape(kv_weight.shape[0], -1)
     residual = tokens.astype(f32)
-    spine = Spine(norm_first[:1])
+    spine = Spine(jnp.zeros((1, LANES), f32))
 
     def column_share(weight):
         rows, columns = weight.shape[0] // count, weight.shape[1] // 2
@@ -833,6 +835,7 @@
     first_half = in_order(first_own, swap(first_own, "col"), col, 1)
     square_first = jnp.sum(residual * residual, axis=1)
     square_first = square_first + swap(square_first, "col")
+    square_far = swap(square_first, "row")
     query_own = product(first_half, part_of(query_weight, row, 1))
     query_out = product(first_half, part_of(query_weight, 1 - row, 1)).astype(bf16)
     pair_own = product(first_half, kv_flat)
@@ -853,21 +856,21 @@
         ),
         "row",
     )
-    mix_other = swap(product(first_half, part_of(mixer_in, 1 - row, 1)).astype(bf16), "row")
+    mix_out = product(first_half, part_of(mixer_in, 1 - row, 1)).astype(bf16)
     mix_own = product(first_half, part_of(mixer_in, row, 1))
+    cot_near = swap_dp(cotangent, 1)
     cot_half = in_order(cotangent, swap(cotangent, "col"), col, 1)
     hidden_back = product_back(cot_half, part_of(down_weight, 1 - row, 0)).astype(bf16)
     hidden_back_own = product_back(cot_half, part_of(down_weight, row, 0))
 
     out_spread.wait(spine)
     out_spread.level()
-    square_first = spine.wait(square_first)
-    square_far = swap(square_first, "row")
     ffn_spread.wait(spine)
     ffn_spread.level()
     out_spread.wait(spine)
     out_spread.level()
-    early, square_far = spine.wait(early, square_far)
+    cot_near, early, square_far, mix_out = spine.wait(cot_near, early, square_far, mix_out)
+    mix_other = swap(mix_out, "row")
     first_factor = lax.rsqrt((square_first + square_far) / D + norm_epsilon)
     first_column = first_factor[:, None]
     query_sum = (query_own + early[:, :query_width].astype(f32)) * first_column
@@ -896,16 +899,19 @@
     out_spread.level()
     mix_other, hidden_back = spine.wait(mix_other, hidden_back)
     hidden_back = swap(hidden_back, "row")
-    ffn_spread.wait(spine)
-    ffn_spread.level()
-    mix_own, mix_other = spine.wait(mix_own, mix_other)
     mixed_raw, square, mix_sum, ssm, states = mixer_forward(
         mix_own, mix_other, first_column, shared_sum, step_sum, conv_inner, conv_shared,
         heads, skip_wide, gain_wide, attended,
     )
-    square = spine.wait(square)
+    square, hidden_back = spine.wait(square, hidden_back)
+    square_total = square[:, 0] + swap(square[:, 0], "col")
+    square_far = swap(square_total, "row")
+    ffn_spread.wait(spine)
+    ffn_spread.level()
     out_other = out_spread.finish(spine)
-    group_factor = lax.rsqrt(rows_total(square[:, 0]) / (HM * PM) + norm_epsilon)
+    square_far, first_send = spine.wait(square_far, first_own)
+    first_near = swap_dp(first_send, 1)
+    group_factor = lax.rsqrt((square_total + square_far) / (HM * PM) + norm_epsilon)
     groups = attended.shape[1] // HD
     group_width = mixed_raw.shape[1] // groups
     is_normed = jnp.arange(mixed_raw.shape[1])[None, :] % group_width < group_width - HD
@@ -916,7 +922,10 @@
     out_far = sum_cols(product(mixed, out_other), col)
     out_far = swap(out_far.astype(bf16), "row")
     out_near = sum_cols(product(mixed, out_own), col)
-    out_far = spine.wait(out_far)
+    ffn_other = ffn_spread.finish(spine)
+    out_far, mixed_send = spine.wait(out_far, mixed)
+    mixed_near = swap_dp(near_blocks(mixed_send, 1 - near), 1)
+    mixed_kept = near_blocks(mixed_send, near)
     second = residual + out_near + out_far.astype(f32)
     second_own = (second * norm_second).astype(bf16)
     second_far = swap(second_own, "row")
@@ -931,14 +940,12 @@
     second_far = in_order(second_far, swap(second_far, "col"), col, 1)
     second_far_near = swap(second_near, "row")
     second_near = in_order(second_near, swap(second_near, "col"), col, 1)
-    ffn_other = ffn_spread.finish(spine)
     second_factor = lax.rsqrt((second_square + second_square_far) / D + norm_epsilon)
     second_column = second_factor[:, None]
     gate_sum = (gate_part + product(second_far, ffn_other[:, :gate_width])) * second_column
     up_sum = (up_part + product(second_far, ffn_other[:, gate_width:])) * second_column
     gate_sigmoid = jax.nn.sigmoid(gate_sum)
     gate_act = gate_sum * gate_sigmoid
-    hidden_back = spine.wait(hidden_back)
     hidden_grad = hidden_back_own + hidden_back.astype(f32)
     gate_grad = hidden_grad * up_sum * gate_sigmoid * (1.0 + gate_sum * (1.0 - gate_sigmoid))
     up_grad = hidden_grad * gate_act
@@ -950,16 +957,17 @@
     second_total = second_total + swap(second_total, "col")
     second_total_far = swap(second_total, "row")
     ffn_send = swap_dp(part_of(ffn_grad, 1 - near, 1), 1)
-    back_far = sum_cols(product_back(ffn_grad, ffn_other), col)
-    back_far = swap(back_far.astype(bf16), "row")
+    back_far = sum_cols(product_back(ffn_grad, ffn_other), col).astype(bf16)
+    second_total_far, back_far, mixed_near = spine.wait(second_total_far, back_far, mixed_near)
+    back_far = swap(back_far, "row")
     back_near = sum_cols(
         product_back(ffn_grad[:, :gate_width], gate_own)
         + product_back(ffn_grad[:, gate_width:], up_own),
         col,
     )
-    second_total_far, second_far_near = spine.wait(second_total_far, second_far_near)
+    second_far_near = spine.wait(second_far_near)
     second_far_near = in_order(second_far_near, swap(second_far_near, "col"), col, 1)
-    back_far = spine.wait(back_far)
+    back_far, ffn_send = spine.wait(back_far, ffn_send)
     second_in_grad = back_near + back_far.astype(f32)
     second_grad = (
         cotangent.astype(f32)
@@ -972,7 +980,19 @@
     branch_half = in_order(branch, swap(branch, "col"), col, 1)
     branch_near = swap_dp(branch, 1)
 
-    branch_half, ffn_send = spine.wait(branch_half, ffn_send)
+    def both_halves(scattered, sent):
+        kept = lax.dynamic_index_in_dim(scattered, near, 0, keepdims=False)
+        return jnp.where(near == 0, kept, sent), jnp.where(near == 0, sent, kept)
+
+    def to_neighbour(scattered):
+        return swap_dp(lax.dynamic_index_in_dim(scattered, 1 - near, 0, keepdims=False), 1)
+
+    branch_half, mixed_near, mixed_kept, hidden_send = spine.wait(
+        branch_half, mixed_near, mixed_kept, hidden
+    )
+    mixed_near_far = swap(mixed_near, "row")
+    mixed_kept_far = swap(mixed_kept, "row")
+    hidden_near = swap_dp(near_blocks(hidden_send, 1 - near), 1)
     ffn_kept = part_of(ffn_grad, near, 1)
     ffn_scatter = Scatter(
         spine,
@@ -996,17 +1016,15 @@
     )
     group_total_far, attention_total = spine.wait(group_total_far, attention_total)
     group_scale = group_factor**2 * (group_total + group_total_far) / (HM * PM)
-    group_scale, mixed_send, first_send = spine.wait(group_scale, mixed, first_own)
-    mixed_near = swap_dp(near_blocks(mixed_send, 1 - near), 1)
-    mixed_kept = near_blocks(mixed_send, near)
-    mixed_kept_far = swap(mixed_kept, "row")
+    group_scale, first_send, first_near = spine.wait(group_scale, first_own, first_near)
     first_far = swap(first_send, "row")
-    first_near = swap_dp(first_send, 1)
+    first_far_near = swap(first_near, "row")
+    first_near = in_order(first_near, swap(first_near, "col"), col, 1)
     lanes = (
         jnp.arange(channels)[:, None] // PM == jnp.arange(LANES)[None, :]
     ).astype(bf16)
     (
-        mix_grad,
+        own_grads,
         shared_grad,
         step_grad,
         conv_inner_grad,
@@ -1017,26 +1035,46 @@
     ) = mixer_backward(
         mix_sum, ssm, states, shared_sum, step_sum, conv_inner, conv_shared, heads, skip_wide,
         gain_wide, lanes, mixed_grad, group_factor[:, None], group_scale[:, None], first_column,
-    )
-    mix_grad, shared_grad = spine.wait(mix_grad, shared_grad)
-    own_grads = jnp.concatenate([mix_grad, query_grad], axis=1)
+        query_grad,
+    )
+    mixer_total = spine.wait(mixer_total)
+    ffn_scatter.add()
+    ffn_scatter_far.add()
+    own_grads, shared_grad = spine.wait(own_grads, shared_grad)
+    mix_width = mix_sum.shape[1]
     grads_send = swap_dp(part_of(own_grads, 1 - near, 1), 1)
     shared_low = (shared_grad.astype(f32) + swap(shared_grad, "col").astype(f32)).astype(bf16)
-    late = jnp.concatenate(
-        [part_of(shared_low, col, 1), pair_grad, step_grad], axis=1
-    )
+    late = jnp.concatenate([part_of(shared_low, col, 1), pair_grad, step_grad], axis=1)
     late_far = swap(late, "row")
-    ffn_scatter.add()
-    ffn_scatter_far.add()
-    mixed_near, first_near = spine.wait(mixed_near, first_near)
-    mixed_near_far = swap(mixed_near, "row")
-    first_far_near = swap(first_near, "row")
-    mixed_kept_far, branch_near = spine.wait(mixed_kept_far, branch_near)
+    mixed_kept_far, mixed_near_far, branch_near = spine.wait(
+        mixed_kept_far, mixed_near_far, branch_near
+    )
     mixed_kept = in_order(mixed_kept, mixed_kept_far, row, 1)
+    mixed_near = in_order(mixed_near, mixed_near_far, row, 1)
     branch_near = in_order(branch_near, swap(branch_near, "col"), col, 1)
-    first_near = in_order(first_near, swap(first_near, "col"), col, 1)
-    first_far, late_far = spine.wait(first_far, late_far)
+    out_scatter = Scatter(
+        spine,
+        (outer_sum(mixed_kept, branch_half) + outer_sum(mixed_near, branch_near)).astype(bf16),
+        False,
+        f32,
+    )
+    ffn_near = ffn_scatter.finish()
+    ffn_near_sent = to_neighbour(ffn_near)
+    ffn_far = ffn_scatter_far.finish()
+    ffn_far_sent = to_neighbour(ffn_far)
+    first_far, first_far_near, grads_send = spine.wait(first_far, first_far_near, grads_send)
     first_far = in_order(first_far, swap(first_far, "col"), col, 1)
+    first_far_near = in_order(first_far_near, swap(first_far_near, "col"), col, 1)
+    grads_kept = part_of(own_grads, near, 1)
+    mixer_scatter_far = Scatter(
+        spine,
+        (outer_sum(first_far, grads_kept) + outer_sum(first_far_near, grads_send)).astype(bf16),
+        True,
+    )
+    out_scatter.add()
+    late_far, hidden_send, hidden_near = spine.wait(late_far, hidden, hidden_near)
+    hidden_far = swap(hidden_send, "row")
+    hidden_near_far = swap(hidden_near, "row")
     half = shared_width // 2
     late_sum = (late[:, : half + pair_width].astype(f32) + late_far[:, : half + pair_width].astype(f32)).astype(bf16)
     shared_part, pair_low = late_sum[:, :half], late_sum[:, half:]
@@ -1048,28 +1086,12 @@
     )
     step_all = in_order(step_two, swap(step_two, "col"), col, 1)
     shared_low = in_order(shared_part, swap(shared_part, "col"), col, 1)
-    rest = jnp.concatenate([pair_low, shared_part, to_lanes(step_all)], axis=1)
+    rest = jnp.concatenate(
+        [pair_low, shared_part, to_lanes(step_all), jnp.zeros((length, LANES), bf16)], axis=1
+    )
     rest_send = swap_dp(part_of(rest, 1 - near, 1), 1)
-    mixed_near_far = spine.wait(mixed_near_far)
-    mixed_near = in_order(mixed_near, mixed_near_far, row, 1)
-    out_scatter = Scatter(
-        spine,
-        (outer_sum(mixed_kept, branch_half) + outer_sum(mixed_near, branch_near)).astype(bf16),
-        False,
-        f32,
-    )
-    first_far_near, grads_send = spine.wait(first_far_near, grads_send)
-    first_far_near = in_order(first_far_near, swap(first_far_near, "col"), col, 1)
-    grads_kept = part_of(own_grads, near, 1)
-    mixer_scatter_far = Scatter(
-        spine,
-        (outer_sum(first_far, grads_kept) + outer_sum(first_far_near, grads_send)).astype(bf16),
-        True,
-    )
-    rest_send, hidden = spine.wait(rest_send, hidden)
-    hidden_half = swap(hidden, "row")
-    hidden_near = swap_dp(near_blocks(hidden, 1 - near), 1)
-    cot_near = swap_dp(cotangent, 1)
+    mixer_scatter_far.add()
+    rest_send = spine.wait(rest_send)
     mixer_scatter = Scatter(
         spine,
         (
@@ -1081,30 +1103,12 @@
         True,
     )
 
-    def both_halves(scattered, sent):
-        kept = lax.dynamic_index_in_dim(scattered, near, 0, keepdims=False)
-        return jnp.where(near == 0, kept, sent), jnp.where(near == 0, sent, kept)
-
-    def to_neighbour(scattered):
-        return swap_dp(lax.dynamic_index_in_dim(scattered, 1 - near, 0, keepdims=False), 1)
-
-    ffn_near = ffn_scatter.finish()
-    ffn_near_sent = to_neighbour(ffn_near)
-    ffn_far = ffn_scatter_far.finish()
-    ffn_far_sent = to_neighbour(ffn_far)
-    hidden_half, hidden_near, cot_near, mix_send = spine.wait(
-        hidden_half, hidden_near, cot_near, own_grads
-    )
-    hidden_half = in_order(hidden, hidden_half, row, 1)
-    hidden_near_far = swap(hidden_near, "row")
-    own_grads_far = swap(mix_send, "row")
+    out_weight_grad = out_scatter.finish()[0]
+    hidden_far, hidden_near_far, grads_again = spine.wait(hidden_far, hidden_near_far, own_grads)
+    own_grads_far = swap(grads_again, "row")
+    hidden_half = in_order(hidden, hidden_far, row, 1)
+    hidden_near = in_order(hidden_near, hidden_near_far, row, 1)
     cot_near = in_order(cot_near, swap(cot_near, "col"), col, 1)
-    layer_out = (second + sum_cols(product(hidden_half, down_weight), col)).astype(bf16)
-    out_scatter.add()
-    ffn_far_sent, ffn_near_sent, hidden_near_far = spine.wait(
-        ffn_far_sent, ffn_near_sent, hidden_near_far
-    )
-    hidden_near = in_order(hidden_near, hidden_near_far, row, 1)
     down_scatter = Scatter(
         spine,
         (
@@ -1114,14 +1118,17 @@
         False,
         f32,
     )
+    mixer_far = mixer_scatter_far.finish()
+    mixer_far_sent = to_neighbour(mixer_far)
+    mixer_scatter.add()
+    layer_out = (second + sum_cols(product(hidden_half, down_weight), col)).astype(bf16)
+    ffn_far_sent, ffn_near_sent = spine.wait(ffn_far_sent, ffn_near_sent)
     ffn_near = both_halves(ffn_near, ffn_near_sent)
     ffn_far = swap(jnp.stack(both_halves(ffn_far, ffn_far_sent)), "row")
-    out_weight_grad = out_scatter.finish()[0]
-    mixer_scatter_far.add()
-    mixer_scatter.add()
+    down_scatter.add()
     own_grads_far = spine.wait(own_grads_far)
-    mix_half = in_order(mix_grad, own_grads_far[:, : mix_grad.shape[1]], row, 1)
-    query_half = in_order(query_grad, own_grads_far[:, mix_grad.shape[1] :], row, 1)
+    mix_half = in_order(own_grads[:, :mix_width], own_grads_far[:, :mix_width], row, 1)
+    query_half = in_order(own_grads[:, mix_width:], own_grads_far[:, mix_width:], row, 1)
     first_in_partial = (
         product_back(mix_half, mixer_in)
         + product_back(query_half, query_weight)
@@ -1134,8 +1141,6 @@
     first_total_far = swap(first_total, "row")
     conv_shared_sum = conv_shared_part + swap(conv_shared_part, "col")
     conv_shared_far = swap(conv_shared_sum, "row")
-    mixer_far = mixer_scatter_far.finish()
-    mixer_far_sent = to_neighbour(mixer_far)
     first_total_far, conv_shared_far, ffn_far = spine.wait(first_total_far, conv_shared_far, ffn_far)
     gate_weight_grad = in_order(ffn_near[0], ffn_far[0], row, 1).astype(f32)
     up_weight_grad = in_order(ffn_near[1], ffn_far[1], row, 1).astype(f32)
@@ -1162,17 +1167,15 @@
     small_far = swap_dp(small, bits[0])
     mixer_far_sent = spine.wait(mixer_far_sent)
     mixer_far = swap(jnp.concatenate(both_halves(mixer_far, mixer_far_sent), axis=1), "row")
+    small = small + spine.wait(small_far)
+    small_far = swap_dp(small, bits[1])
     mixer_near = mixer_scatter.finish()
     mixer_near_sent = to_neighbour(mixer_near)
-    small = small + spine.wait(small_far)
-    small_far = swap_dp(small, bits[1])
-    down_scatter.add()
     small = small + spine.wait(small_far)
     small_far = swap_dp(small, bits[2])
     mixer_near_sent, mixer_far = spine.wait(mixer_near_sent, mixer_far)
     mixer_near = both_halves(mixer_near, mixer_near_sent)
     kept_width = grads_kept.shape[1]
-    mix_width = mix_grad.shape[1]
     own_sums = jnp.concatenate([mixer_near[0][:, :kept_width], mixer_near[1][:, :kept_width]], axis=1)
     rest_sums = jnp.concatenate(
         [mixer_near[0][:, kept_width:], mixer_near[1][:, kept_width:]], axis=1
@@ -1192,7 +1195,7 @@
         small_far = swap_dp(small, bit)
     small = small + spine.wait(small_far)
     down_weight_grad = down_scatter.finish()[0]
-    small = small.reshape(-1)
+    small = (small + spine.token).reshape(-1)
     sums, place = [], 0
     for piece in pieces:
         sums.append(small[place : place + piece.shape[0]])

time: 633 us -> 575 us (0.908)
  waiting for transfers between devices: 248 us -> 208 us
  local copies, waits for them, and re-layouts: 64.3 us -> 54.7 us
  starting transfers between devices: 90.6 us -> 83.8 us
    ppermute x58, waiting for transfers between devices: 90 us -> 63.4 us  [swap(): return lax.ppermute(values_in, axis, [(0, 1), (1, 0)])]
    ppermute x42, waiting for transfers between devices: 158 us -> 145 us  [swap_dp(): lax.ppermute(values_in, 'dp', [(i, i ^ bit) for i in range(lax.axis_size(...]
    reshape x1 -> x0, local copies, waits for them, and re-layouts: 6.95 us -> none  [__init__(): self.parts = grads.reshape((2,) * len(self.bits) + rest)]
    ppermute x42, starting transfers between devices: 57.9 us -> 51.1 us  [swap_dp(): lax.ppermute(values_in, 'dp', [(i, i ^ bit) for i in range(lax.axis_size(...]
    unnamed x231 -> x242, local copies, waits for them, and re-layouts: 18.3 us -> 17.4 us
  transfers between devices with their start and end apart: 100 -> 100, of which waited for: 32 -> 34; matrix products, arithmetic and copies ran while one was open for 31% -> 31% of each run, Pallas kernels for 10% -> 11%
where the time goes in v3:
time: 575 us; the launch traced here: 565 us
  waiting for transfers between devices  208 us (36%)
  starting transfers between devices  83.8 us (15%)
  matrix products  76.6 us (13%)
  other arithmetic  73.4 us (13%)
  Pallas kernels  64.9 us (11%)
  local copies, waits for them, and re-layouts  54.7 us (10%)
    ppermute x42, waiting for transfers between devices, swap_dp(): lax.ppermute(values_in, 'dp', [(i, i ^ bit) for i in range(lax.axis_size(...  145 us
    ppermute x58, waiting for transfers between devices, swap(): return lax.ppermute(values_in, axis, [(0, 1), (1, 0)])  63.4 us
    pallas_call x4, Pallas kernels, call(): pl.pallas_call(kernel, out_shape=outs, in_specs=[pl.BlockSpec(memory_spac...  57.3 us
    ppermute x42, starting transfers between devices, swap_dp(): lax.ppermute(values_in, 'dp', [(i, i ^ bit) for i in range(lax.axis_size(...  51.1 us
    ppermute x58, starting transfers between devices, swap(): return lax.ppermute(values_in, axis, [(0, 1), (1, 0)])  32.6 us
    dot_general x14, matrix products, product(): return jnp.dot(left_side, right_side, preferred_element_type=f32)  30.2 us
    dot_general x12, matrix products, product_back(): lax.dot_general(left_side, right_side, (((1,), (1,)), ((), ())), preferre...  25.8 us
    select_n x27, other arithmetic, in_order(): jnp.where(place == 0, own, other)  21.5 us
  transfers between devices with their start and end apart: 100, of which 34 were waited for; matrix products, arithmetic and copies ran while one was open for 31% of the time, Pallas kernels for 11%

profile of v3, /device:TPU:0, one launch (start us, length us, event | category | flops | bytes accessed | tf_op | source)
XLA Modules:
  0.0 564.7 jit_solution(10226825169870079629)
XLA Ops:
  22.6 25.3 %collective-permute-done.2.refs_0_ = bf16[128,2048]{1,0:T(8,128)(2,1)} collective-permute-done((bf16[128,2048]{1,0:T(8,128)(2,1)}, bf16[128,2048]{1,0:T(8,128)(2,1)}, u32[]{:S(2)}, u32[]{:S(2)}) %collective-permute-start.2) | collective-permute-done | bytes 524320 | tf_op jit(solution)/shard_map/ppermute | solution.py:45
  51.0 4.8 fusion.8
  70.8 4.2 fusion.55
  75.0 12.1 %collective-permute-done.10.refs_1_ = bf16[128,2048]{1,0:T(8,128)(2,1)} collective-permute-done((bf16[128,2048]{1,0:T(8,128)(2,1)}, bf16[128,2048]{1,0:T(8,128)(2,1)}, u32[]{:S(2)}, u32[]{:S(2)}) %collective-permute-start.10) | collective-permute-done | bytes 524320 | tf_op jit(solution)/shard_map/ppermute | solution.py:94
  91.0 5.3 fusion.6.own_ref
  98.0 4.0 collective-permute-done.15.refs_6_
  114.1 3.9 shard_map.330.attended_ref
  119.1 16.7 %shard_map.331 = (bf16[512,1024]{1,0:T(8,128)(2,1)}, f32[512,1]{1,0:T(8,128)}, f32[512,1536]{1,0:T(8,128)}, f32[512,768]{1,0:T(8,128)}, bf16[1024,768]{1,0:T(8,128)(2,1)}) custom-call(f32[512,1536]{1,0:T(8,128)} %fusion.6.own_ref, bf16[512,1536]{1,0:T(8,128)(2,1)} %collective-permute-done.16.other_ref, f32[512,1]{1,0:T(8,128)} %copy.84.factor_ref, ...), custom_call_target="tpu_custom_call" | custom-call | flops 100000000 | bytes 1000000 | tf_op jit(solution)/shard_map/pallas_call | solution.py:595
  157.1 5.3 collective-permute-done.27.refs_7_
  162.4 5.5 collective-permute-done.29
  173.2 3.8 convert_add_fusion.5
  177.0 4.4 shard_map.333
  195.5 3.7 multiply_convert_fusion.1
  209.3 11.5 %collective-permute-done.37 = f32[512]{0:T(512)S(1)} collective-permute-done((f32[512]{0:T(512)S(1)}, f32[512]{0:T(512)S(1)}, u32[]{:S(2)}, u32[]{:S(2)}) %collective-permute-start.37) | collective-permute-done | bytes 2080 | tf_op jit(solution)/shard_map/ppermute | solution.py:45
  224.3 6.1 %collective-permute-done.42 = bf16[512,1024]{1,0:T(8,128)(2,1)S(1)} collective-permute-done((bf16[512,1024]{1,0:T(8,128)(2,1)S(1)}, bf16[512,1024]{1,0:T(8,128)(2,1)S(1)}, u32[]{:S(2)}, u32[]{:S(2)}) %collective-permute-start.42) | collective-permute-done | bytes 1048608 | tf_op jit(solution)/shard_map/ppermute | solution.py:94
  242.1 7.8 %collective-permute-done.45 = bf16[512,512]{1,0:T(8,128)(2,1)S(1)} collective-permute-done((bf16[512,512]{1,0:T(8,128)(2,1)S(1)}, bf16[512,512]{1,0:T(8,128)(2,1)S(1)}, u32[]{:S(2)}, u32[]{:S(2)}) %collective-permute-start.45) | collective-permute-done | bytes 524320 | tf_op jit(solution)/shard_map/ppermute | solution.py:45
  269.0 7.6 %shard_map.334 = (bf16[512,256]{1,0:T(8,128)(2,1)}, bf16[512,256]{1,0:T(8,128)(2,1)}, f32[512,1]{1,0:T(8,128)}) custom-call(f32[512,256]{1,0:T(8,128)} %fusion.66.query_ref, f32[512,256]{1,0:T(8,128)} %get-tuple-element.466.pair_ref, f32[512,128]{1,0:T(8,128)} %get-tuple-element.504.cosine_ref, f32[512,128]{1,0:T(8,128)} %get-tuple-element.505.sine_ref, ...), custom_call_target="tpu_custom_call" | custom-call | flops 100000000 | bytes 1000000 | tf_op jit(solution)/shard_map/pallas_call | solution.py:595
  277.5 29.1 %shard_map.335 = (bf16[512,1792]{1,0:T(8,128)(2,1)}, bf16[512,512]{1,0:T(8,128)(2,1)}, bf16[512,128]{1,0:T(8,128)(2,1)}, f32[4,768]{1,0:T(4,128)}, f32[4,512]{1,...) custom-call(f32[512,1536]{1,0:T(8,128)} %get-tuple-element.229.mix_ref, ...), custom_call_target="tpu_custom_call" | custom-call | flops 100000000 | bytes 1000000 | tf_op jit(solution)/shard_map/pallas_call | solution.py:595
  309.3 3.5 collective-permute-start.57
  338.0 3.6 add_convert_fusion.2
  342.3 4.7 collective-permute-done.57
  348.2 9.8 %collective-permute-done.58 = bf16[2,128,1024]{2,1,0:T(8,128)(2,1)} collective-permute-done((bf16[2,128,1024]{2,1,0:T(8,128)(2,1)}, bf16[2,128,1024]{2,1,0:T(8,128)(2,1)}, u32[]{:S(2)}, u32[]{:S(2)}) %collective-permute-start.58) | collective-permute-done | bytes 524320 | tf_op jit(solution)/shard_map/ppermute | solution.py:94
  374.3 11.2 %collective-permute-done.63 = bf16[2,1,256,1024]{3,2,1,0:T(8,128)(2,1)S(1)} collective-permute-done((bf16[2,1,256,1024]{3,2,1,0:T(8,128)(2,1)S(1)}, bf16[2,1,256,1024]{3,2,1,0:T(8,128)(2,1)S(1)}, u32[]{:S(2)}, u32[]{:S(2)}) %collective-permute-start.63) | collective-permute-done | bytes 1048608 | tf_op jit(solution)/shard_map/ppermute | solution.py:94
  411.9 8.1 %collective-permute-done.71 = bf16[512,384]{1,0:T(8,128)(2,1)S(1)} collective-permute-done((bf16[512,384]{1,0:T(8,128)(2,1)S(1)}, bf16[512,384]{1,0:T(8,128)(2,1)S(1)}, u32[]{:S(2)}, u32[]{:S(2)}) %collective-permute-start.71) | collective-permute-done | bytes 393248 | tf_op jit(solution)/shard_map/ppermute | solution.py:94
  420.0 3.8 collective-permute-done.72
  430.2 4.5 collective-permute-done.74
  451.6 18.0 %collective-permute-done.78 = bf16[2,2,128,1280]{3,2,1,0:T(8,128)(2,1)S(1)} collective-permute-done((bf16[2,2,128,1280]{3,2,1,0:T(8,128)(2,1)S(1)}, bf16[2,2,128,1280]{3,2,1,0:T(8,128)(2,1)S(1)}, u32[]{:S(2)}, u32[]{:S(2)}) %collective-permute-start.78) | collective-permute-done | bytes 1310752 | tf_op jit(solution)/shard_map/ppermute | solution.py:94
  472.9 17.4 %collective-permute-done.82 = bf16[2,1,256,1024]{3,2,1,0:T(8,128)(2,1)S(1)} collective-permute-done((bf16[2,1,256,1024]{3,2,1,0:T(8,128)(2,1)S(1)}, bf16[2,1,256,1024]{3,2,1,0:T(8,128)(2,1)S(1)}, u32[]{:S(2)}, u32[]{:S(2)}) %collective-permute-start.82) | collective-permute-done | bytes 1048608 | tf_op jit(solution)/shard_map/ppermute | solution.py:94
  495.4 3.4 fusion
  511.6 22.8 %collective-permute-done.93 = bf16[2,128,1280]{2,1,0:T(8,128)(2,1)S(1)} collective-permute-done((bf16[2,128,1280]{2,1,0:T(8,128)(2,1)S(1)}, bf16[2,128,1280]{2,1,0:T(8,128)(2,1)S(1)}, u32[]{:S(2)}, u32[]{:S(2)}) %collective-permute-start.93) | collective-permute-done | bytes 655392 | tf_op jit(solution)/shard_map/ppermute | solution.py:94
  537.0 9.3 %collective-permute-done.94 = f32[57,128]{1,0:T(8,128)S(1)} collective-permute-done((f32[57,128]{1,0:T(8,128)S(1)}, f32[57,128]{1,0:T(8,128)S(1)}, u32[]{:S(2)}, u32[]{:S(2)}) %collective-permute-start.94) | collective-permute-done | bytes 29216 | tf_op jit(solution)/shard_map/ppermute | solution.py:94
  546.9 4.3 collective-permute-done.97
  (639 shorter events, 276.1 us)
Async XLA Ops:
  13.8 43.1 %collective-permute-start.7 = (bf16[512,896]{1,0:T(8,128)(2,1)}, bf16[512,896]{1,0:T(8,128)(2,1)}, u32[]{:S(2)}, u32[]{:S(2)}) collective-permute-start(bf16[512,896]{1,0:T(8,128)(2,1)} %fusion.123), channel_id=1, source_target_pairs={{0,2},{2,0},{1,3},{3,1},{4,6},{6,4},{5,7},{7,5},{8,10},{10,8},{9,1... | collective-permute-start | bytes 2752520 | tf_op jit(solution)/shard_map/ppermute | solution.py:45
  15.1 32.7 %collective-permute-start.2 = (bf16[128,2048]{1,0:T(8,128)(2,1)}, bf16[128,2048]{1,0:T(8,128)(2,1)}, u32[]{:S(2)}, u32[]{:S(2)}) collective-permute-start(bf16[128,2048]{1,0:T(8,128)(2,1)} %pad_maximum_fusion.9), channel_id=1, source_target_pairs={{0,2},{2,0},{1,3},{3,1},{4,6},{6,4},{5,7},{7,5},{8,10},{10,8},{9,1... | collective-permute-start | bytes 1572872 | tf_op jit(solution)/shard_map/ppermute | solution.py:45
  16.7 32.7 %collective-permute-start.3 = (bf16[128,1024]{1,0:T(8,128)(2,1)}, bf16[128,1024]{1,0:T(8,128)(2,1)S(1)}, u32[]{:S(2)}, u32[]{:S(2)}) collective-permute-start(bf16[128,1024]{1,0:T(8,128)(2,1)} %collective-permute-done.1.refs_0_), channel_id=1, source_target_pairs={{0,16},{4,20},{8,24},{12,28},{16,0},{20,4},{24,8},{28,12},{1,17},{... | collective-permute-start | bytes 786440 | tf_op jit(solution)/shard_map/ppermute | solution.py:94
  19.3 37.7 %collective-permute-start.6 = (bf16[512,512]{1,0:T(8,128)(2,1)S(1)}, bf16[512,512]{1,0:T(8,128)(2,1)}, u32[]{:S(2)}, u32[]{:S(2)}) collective-permute-start(bf16[512,512]{1,0:T(8,128)(2,1)S(1)} %copy-done.25), channel_id=1, source_target_pairs={{0,4},{4,0},{8,12},{12,8},{16,20},{20,16},{24,28},{28,24},{1,5},{5... | collective-permute-start | bytes 1572872 | tf_op jit(solution)/shard_map/ppermute | solution.py:94
  22.0 34.9 %collective-permute-start.9 = (f32[512]{0:T(512)S(1)}, f32[512]{0:T(512)S(1)}, u32[]{:S(2)}, u32[]{:S(2)}) collective-permute-start(f32[512]{0:T(512)S(1)} %add.424), channel_id=1, source_target_pairs={{0,2},{2,0},{1,3},{3,1},{4,6},{6,4},{5,7},{7,5},{8,10},{10,8},{9,1... | collective-permute-start | bytes 6152 | tf_op jit(solution)/shard_map/ppermute | solution.py:45
  57.0 46.0 %collective-permute-start.16 = (bf16[512,1536]{1,0:T(8,128)(2,1)}, bf16[512,1536]{1,0:T(8,128)(2,1)}, u32[]{:S(2)}, u32[]{:S(2)}) collective-permute-start(bf16[512,1536]{1,0:T(8,128)(2,1)} %fusion.8), channel_id=1, source_target_pairs={{0,2},{2,0},{1,3},{3,1},{4,6},{6,4},{5,7},{7,5},{8,10},{10,8},{9,1... | collective-permute-start | bytes 4718600 | tf_op jit(solution)/shard_map/ppermute | solution.py:45
  96.3 42.4 %collective-permute-start.21 = (bf16[128,2048]{1,0:T(8,128)(2,1)}, bf16[128,2048]{1,0:T(8,128)(2,1)}, u32[]{:S(2)}, u32[]{:S(2)}) collective-permute-start(bf16[128,2048]{1,0:T(8,128)(2,1)} %collective-permute-done.10.refs_1_), channel_id=1, source_target_pairs={{0,8},{4,12},{8,0},{12,4},{16,24},{20,28},{24,16},{28,20},{1,9},{5... | collective-permute-start | bytes 1572872 | tf_op jit(solution)/shard_map/ppermute | solution.py:94
  97.5 41.3 %collective-permute-start.22 = (bf16[128,2048]{1,0:T(8,128)(2,1)}, bf16[128,2048]{1,0:T(8,128)(2,1)}, u32[]{:S(2)}, u32[]{:S(2)}) collective-permute-start(bf16[128,2048]{1,0:T(8,128)(2,1)} %collective-permute-done.10.refs_1_), channel_id=1, source_target_pairs={{0,4},{4,0},{8,12},{12,8},{16,20},{20,16},{24,28},{28,24},{1,5},{5... | collective-permute-start | bytes 1572872 | tf_op jit(solution)/shard_map/ppermute | solution.py:94
  103.0 32.9 %collective-permute-start.19 = (bf16[512,1024]{1,0:T(8,128)(2,1)}, bf16[512,1024]{1,0:T(8,128)(2,1)}, u32[]{:S(2)}, u32[]{:S(2)}) collective-permute-start(bf16[512,1024]{1,0:T(8,128)(2,1)} %fusion.55), channel_id=1, source_target_pairs={{0,2},{2,0},{1,3},{3,1},{4,6},{6,4},{5,7},{7,5},{8,10},{10,8},{9,1... | collective-permute-start | bytes 3145736 | tf_op jit(solution)/shard_map/ppermute | solution.py:45
  187.0 35.3 %collective-permute-start.50 = (bf16[512,512]{1,0:T(8,128)(2,1)}, bf16[512,512]{1,0:T(8,128)(2,1)S(1)}, u32[]{:S(2)}, u32[]{:S(2)}) collective-permute-start(bf16[512,512]{1,0:T(8,128)(2,1)} %collective-permute-done.32), channel_id=1, source_target_pairs={{0,1},{1,0},{2,3},{3,2},{4,5},{5,4},{6,7},{7,6},{8,9},{9,8},{10,11... | collective-permute-start | bytes 1572872 | tf_op jit(solution)/shard_map/ppermute | solution.py:45
  222.3 38.7 %collective-permute-start.81 = (bf16[512,512]{1,0:T(8,128)(2,1)}, bf16[512,512]{1,0:T(8,128)(2,1)}, u32[]{:S(2)}, u32[]{:S(2)}) collective-permute-start(bf16[512,512]{1,0:T(8,128)(2,1)} %collective-permute-done.6), channel_id=1, source_target_pairs={{0,1},{1,0},{2,3},{3,2},{4,5},{5,4},{6,7},{7,6},{8,9},{9,8},{10,11... | collective-permute-start | bytes 1572872 | tf_op jit(solution)/shard_map/ppermute | solution.py:45
  223.4 41.5 %collective-permute-start.49 = (bf16[512,512]{1,0:T(8,128)(2,1)}, bf16[512,512]{1,0:T(8,128)(2,1)}, u32[]{:S(2)}, u32[]{:S(2)}) collective-permute-start(bf16[512,512]{1,0:T(8,128)(2,1)} %get-tuple-element.250), channel_id=1, source_target_pairs={{0,4},{4,0},{8,12},{12,8},{16,20},{20,16},{24,28},{28,24},{1,5},{5... | collective-permute-start | bytes 1572872 | tf_op jit(solution)/shard_map/ppermute | solution.py:94
  239.9 66.6 %collective-permute-start.51 = (bf16[2,2,128,1024]{3,2,1,0:T(8,128)(2,1)}, bf16[2,2,128,1024]{3,2,1,0:T(8,128)(2,1)}, u32[]{:S(2)}, u32[]{:S(2)}) collective-permute-start(bf16[2,2,128,1024]{3,2,1,0:T(8,128)(2,1)} %dynamic-slice_bitcast_fusion.4), channel_id=1, source_target_pairs={{0,8},{4,12},{8,0},{12,4},{16,24},{20,28},{24,16},{28,20},{1,9},{5... | collective-permute-start | bytes 3145736 | tf_op jit(solution)/shard_map/ppermute | solution.py:94
  252.9 53.6 %collective-permute-start.53 = (bf16[2,2,128,1024]{3,2,1,0:T(8,128)(2,1)}, bf16[2,2,128,1024]{3,2,1,0:T(8,128)(2,1)}, u32[]{:S(2)}, u32[]{:S(2)}) collective-permute-start(bf16[2,2,128,1024]{3,2,1,0:T(8,128)(2,1)} %dynamic-slice_bitcast_fusion.3), channel_id=1, source_target_pairs={{0,8},{4,12},{8,0},{12,4},{16,24},{20,28},{24,16},{28,20},{1,9},{5... | collective-permute-start | bytes 3145736 | tf_op jit(solution)/shard_map/ppermute | solution.py:94
  264.1 42.5 %collective-permute-start.56 = (bf16[512,512]{1,0:T(8,128)(2,1)S(1)}, bf16[512,512]{1,0:T(8,128)(2,1)}, u32[]{:S(2)}, u32[]{:S(2)}) collective-permute-start(bf16[512,512]{1,0:T(8,128)(2,1)S(1)} %copy-done.31), channel_id=1, source_target_pairs={{0,4},{4,0},{8,12},{12,8},{16,20},{20,16},{24,28},{28,24},{1,5},{5... | collective-permute-start | bytes 1572872 | tf_op jit(solution)/shard_map/ppermute | solution.py:94
  264.9 41.7 %collective-permute-start.54 = (bf16[512,512]{1,0:T(8,128)(2,1)}, bf16[512,512]{1,0:T(8,128)(2,1)}, u32[]{:S(2)}, u32[]{:S(2)}) collective-permute-start(bf16[512,512]{1,0:T(8,128)(2,1)} %pad_maximum_fusion.11), channel_id=1, source_target_pairs={{0,2},{2,0},{1,3},{3,1},{4,6},{6,4},{5,7},{7,5},{8,10},{10,8},{9,1... | collective-permute-start | bytes 1572872 | tf_op jit(solution)/shard_map/ppermute | solution.py:45
  266.4 40.2 %collective-permute-start.55 = (bf16[512,512]{1,0:T(8,128)(2,1)}, bf16[512,512]{1,0:T(8,128)(2,1)}, u32[]{:S(2)}, u32[]{:S(2)}) collective-permute-start(bf16[512,512]{1,0:T(8,128)(2,1)} %copy-done.62), channel_id=1, source_target_pairs={{0,2},{2,0},{1,3},{3,1},{4,6},{6,4},{5,7},{7,5},{8,10},{10,8},{9,1... | collective-permute-start | bytes 1572872 | tf_op jit(solution)/shard_map/ppermute | solution.py:45
  309.3 37.7 %collective-permute-start.57 = (bf16[2,128,1024]{2,1,0:T(8,128)(2,1)}, bf16[2,128,1024]{2,1,0:T(8,128)(2,1)}, u32[]{:S(2)}, u32[]{:S(2)}) collective-permute-start(bf16[2,128,1024]{2,1,0:T(8,128)(2,1)} %dynamic-slice_bitcast_fusion.10), channel_id=1, source_target_pairs={{0,16},{4,20},{8,24},{12,28},{16,0},{20,4},{24,8},{28,12},{1,17},{... | collective-permute-start | bytes 1572872 | tf_op jit(solution)/shard_map/ppermute | solution.py:94
  316.2 41.8 %collective-permute-start.58 = (bf16[2,128,1024]{2,1,0:T(8,128)(2,1)}, bf16[2,128,1024]{2,1,0:T(8,128)(2,1)}, u32[]{:S(2)}, u32[]{:S(2)}) collective-permute-start(bf16[2,128,1024]{2,1,0:T(8,128)(2,1)} %dynamic-slice_bitcast_fusion.9), channel_id=1, source_target_pairs={{0,16},{4,20},{8,24},{12,28},{16,0},{20,4},{24,8},{28,12},{1,17},{... | collective-permute-start | bytes 1572872 | tf_op jit(solution)/shard_map/ppermute | solution.py:94
  347.0 38.5 %collective-permute-start.66 = (bf16[512,512]{1,0:T(8,128)(2,1)S(1)}, bf16[512,512]{1,0:T(8,128)(2,1)S(1)}, u32[]{:S(2)}, u32[]{:S(2)}) collective-permute-start(bf16[512,512]{1,0:T(8,128)(2,1)S(1)} %copy-done.74), channel_id=1, source_target_pairs={{0,4},{4,0},{8,12},{12,8},{16,20},{20,16},{24,28},{28,24},{1,5},{5... | collective-permute-start | bytes 1572872 | tf_op jit(solution)/shard_map/ppermute | solution.py:94
  364.6 106.5 %collective-permute-start.79 = (bf16[128,1024]{1,0:T(8,128)(2,1)}, bf16[128,1024]{1,0:T(8,128)(2,1)}, u32[]{:S(2)}, u32[]{:S(2)}) collective-permute-start(bf16[128,1024]{1,0:T(8,128)(2,1)} %dynamic-slice_bitcast_fusion.14), channel_id=1, source_target_pairs={{0,4},{4,0},{8,12},{12,8},{16,20},{20,16},{24,28},{28,24},{1,5},{5... | collective-permute-start | bytes 786440 | tf_op jit(solution)/shard_map/ppermute | solution.py:94
  372.4 36.9 %collective-permute-start.69 = (bf16[2,2,128,896]{3,2,1,0:T(8,128)(2,1)}, bf16[2,2,128,896]{3,2,1,0:T(8,128)(2,1)}, u32[]{:S(2)}, u32[]{:S(2)}) collective-permute-start(bf16[2,2,128,896]{3,2,1,0:T(8,128)(2,1)} %dynamic-slice_bitcast_fusion.5), channel_id=1, source_target_pairs={{0,8},{4,12},{8,0},{12,4},{16,24},{20,28},{24,16},{28,20},{1,9},{5... | collective-permute-start | bytes 2752520 | tf_op jit(solution)/shard_map/ppermute | solution.py:94
  398.4 36.3 %collective-permute-start.73 = (bf16[512,1024]{1,0:T(8,128)(2,1)}, bf16[512,1024]{1,0:T(8,128)(2,1)}, u32[]{:S(2)}, u32[]{:S(2)}) collective-permute-start(bf16[512,1024]{1,0:T(8,128)(2,1)} %get-tuple-element.271), channel_id=1, source_target_pairs={{0,2},{2,0},{1,3},{3,1},{4,6},{6,4},{5,7},{7,5},{8,10},{10,8},{9,1... | collective-permute-start | bytes 3145736 | tf_op jit(solution)/shard_map/ppermute | solution.py:45
  427.2 42.4 %collective-permute-start.78 = (bf16[2,2,128,1280]{3,2,1,0:T(8,128)(2,1)S(1)}, bf16[2,2,128,1280]{3,2,1,0:T(8,128)(2,1)S(1)}, u32[]{:S(2)}, u32[]{:S(2)}) collective-permute-start(bf16[2,2,128,1280]{3,2,1,0:T(8,128)(2,1)S(1)} %dynamic-slice_bitcast_fusion), channel_id=1, source_target_pairs={{0,8},{4,12},{8,0},{12,4},{16,24},{20,28},{24,16},{28,20},{1,9},{5... | collective-permute-start | bytes 3932168 | tf_op jit(solution)/shard_map/ppermute | solution.py:94
  440.4 50.0 %collective-permute-start.82 = (bf16[2,1,256,1024]{3,2,1,0:T(8,128)(2,1)S(1)}, bf16[2,1,256,1024]{3,2,1,0:T(8,128)(2,1)S(1)}, u32[]{:S(2)}, u32[]{:S(2)}) collective-permute-start(bf16[2,1,256,1024]{3,2,1,0:T(8,128)(2,1)S(1)} %dynamic-slice_bitcast_fusion.1), channel_id=1, source_target_pairs={{0,8},{4,12},{8,0},{12,4},{16,24},{20,28},{24,16},{28,20},{1,9},{5... | collective-permute-start | bytes 3145736 | tf_op jit(solution)/shard_map/ppermute | solution.py:94
  448.9 45.5 %collective-permute-start.83 = (bf16[512,1792]{1,0:T(8,128)(2,1)S(1)}, bf16[512,1792]{1,0:T(8,128)(2,1)S(1)}, u32[]{:S(2)}, u32[]{:S(2)}) collective-permute-start(bf16[512,1792]{1,0:T(8,128)(2,1)S(1)} %copy-done.9), channel_id=1, source_target_pairs={{0,2},{2,0},{1,3},{3,1},{4,6},{6,4},{5,7},{7,5},{8,10},{10,8},{9,1... | collective-permute-start | bytes 5505032 | tf_op jit(solution)/shard_map/ppermute | solution.py:45
  469.6 32.2 %collective-permute-start.87 = (f32[512]{0:T(512)S(1)}, f32[512]{0:T(512)S(1)}, u32[]{:S(2)}, u32[]{:S(2)}) collective-permute-start(f32[512]{0:T(512)S(1)} %copy-done.101), channel_id=1, source_target_pairs={{0,2},{2,0},{1,3},{3,1},{4,6},{6,4},{5,7},{7,5},{8,10},{10,8},{9,1... | collective-permute-start | bytes 6152 | tf_op jit(solution)/shard_map/ppermute | solution.py:45
  471.1 33.0 %collective-permute-start.89 = (f32[4,512]{1,0:T(4,128)S(1)}, f32[4,512]{1,0:T(4,128)S(1)}, u32[]{:S(2)}, u32[]{:S(2)}) collective-permute-start(f32[4,512]{1,0:T(4,128)S(1)} %copy-done.95), channel_id=1, source_target_pairs={{0,2},{2,0},{1,3},{3,1},{4,6},{6,4},{5,7},{7,5},{8,10},{10,8},{9,1... | collective-permute-start | bytes 24584 | tf_op jit(solution)/shard_map/ppermute | solution.py:45
  471.7 32.5 %collective-permute-start.91 = (bf16[128,896]{1,0:T(8,128)(2,1)S(1)}, bf16[128,896]{1,0:T(8,128)(2,1)S(1)}, u32[]{:S(2)}, u32[]{:S(2)}) collective-permute-start(bf16[128,896]{1,0:T(8,128)(2,1)S(1)} %dynamic-slice_bitcast_fusion.15), channel_id=1, source_target_pairs={{0,4},{4,0},{8,12},{12,8},{16,20},{20,16},{24,28},{28,24},{1,5},{5... | collective-permute-start | bytes 688136 | tf_op jit(solution)/shard_map/ppermute | solution.py:94
  494.4 40.0 %collective-permute-start.93 = (bf16[2,128,1280]{2,1,0:T(8,128)(2,1)S(1)}, bf16[2,128,1280]{2,1,0:T(8,128)(2,1)S(1)}, u32[]{:S(2)}, u32[]{:S(2)}) collective-permute-start(bf16[2,128,1280]{2,1,0:T(8,128)(2,1)S(1)} %dynamic-slice_bitcast_fusion.6), channel_id=1, source_target_pairs={{0,16},{4,20},{8,24},{12,28},{16,0},{20,4},{24,8},{28,12},{1,17},{... | collective-permute-start | bytes 1966088 | tf_op jit(solution)/shard_map/ppermute | solution.py:94
  501.8 49.9 %collective-permute-start.98 = (bf16[1,256,1024]{2,1,0:T(8,128)(2,1)S(1)}, bf16[1,256,1024]{2,1,0:T(8,128)(2,1)S(1)}, u32[]{:S(2)}, u32[]{:S(2)}) collective-permute-start(bf16[1,256,1024]{2,1,0:T(8,128)(2,1)S(1)} %dynamic-slice_bitcast_fusion.7), channel_id=1, source_target_pairs={{0,16},{4,20},{8,24},{12,28},{16,0},{20,4},{24,8},{28,12},{1,17},{... | collective-permute-start | bytes 1572872 | tf_op jit(solution)/shard_map/ppermute | solution.py:94
  504.3 42.3 %collective-permute-start.96 = (bf16[128,1792]{1,0:T(8,128)(2,1)S(1)}, bf16[128,1792]{1,0:T(8,128)(2,1)S(1)}, u32[]{:S(2)}, u32[]{:S(2)}) collective-permute-start(bf16[128,1792]{1,0:T(8,128)(2,1)S(1)} %pad_maximum_fusion.14), channel_id=1, source_target_pairs={{0,2},{2,0},{1,3},{3,1},{4,6},{6,4},{5,7},{7,5},{8,10},{10,8},{9,1... | collective-permute-start | bytes 1376264 | tf_op jit(solution)/shard_map/ppermute | solution.py:45
  (186 other events, 2004.4 us)

commit v4 on v3

--- a/solution.py
+++ b/solution.py
@@ -139,6 +139,24 @@
             self.add()
         self.add()
         return self.parts
+
+
+def far_sum(grads):
+    count = lax.axis_size("dp")
+    groups = [list(range(start, count, 2)) for start in range(2)]
+    return lax.psum_scatter(
+        grads, "dp", scatter_dimension=0, axis_index_groups=groups, tiled=True
+    )
+
+
+def both_rows_kernel(own_ref, far_ref, near_ref, far_near_ref, kept_ref, sent_ref, out_ref, sums):
+    blocks, _, rows, _ = out_ref.shape
+    for side, left_ref, right_ref in ((0, own_ref, near_ref), (1, far_ref, far_near_ref)):
+        sums[...] = outer_sum(left_ref[...], kept_ref[...]) + outer_sum(
+            right_ref[...], sent_ref[...]
+        )
+        for block in range(blocks):
+            out_ref[block, side] = sums[block * rows : (block + 1) * rows, :].astype(bf16)
 
 
 def place_kernel(count, owners, where_ref, *refs):
@@ -828,6 +846,7 @@
         out_weight, (1 - row) * half_rows + me * share_rows, share_rows, 0
     )
     ffn_share = jnp.concatenate([column_share(gate_weight), column_share(up_weight)], axis=1)
+    out_share, ffn_share, residual = tie(out_share, ffn_share, residual)
     out_spread = Spread(swap(out_share, "row"))
     ffn_spread = Spread(swap(ffn_share, "row"))
 
@@ -867,10 +886,10 @@
     out_spread.level()
     ffn_spread.wait(spine)
     ffn_spread.level()
+    cot_near, early, square_far, mix_out = spine.wait(cot_near, early, square_far, mix_out)
+    mix_other = swap(mix_out, "row")
     out_spread.wait(spine)
     out_spread.level()
-    cot_near, early, square_far, mix_out = spine.wait(cot_near, early, square_far, mix_out)
-    mix_other = swap(mix_out, "row")
     first_factor = lax.rsqrt((square_first + square_far) / D + norm_epsilon)
     first_column = first_factor[:, None]
     query_sum = (query_own + early[:, :query_width].astype(f32)) * first_column
@@ -897,7 +916,10 @@
     gain_wide = group_gain[None, :]
     out_spread.wait(spine)
     out_spread.level()
-    mix_other, hidden_back = spine.wait(mix_other, hidden_back)
+    out_other = out_spread.finish(spine)
+    mix_other, hidden_back, attended, shared_sum, step_sum = spine.wait(
+        mix_other, hidden_back, attended, shared_sum, step_sum
+    )
     hidden_back = swap(hidden_back, "row")
     mixed_raw, square, mix_sum, ssm, states = mixer_forward(
         mix_own, mix_other, first_column, shared_sum, step_sum, conv_inner, conv_shared,
@@ -908,9 +930,7 @@
     square_far = swap(square_total, "row")
     ffn_spread.wait(spine)
     ffn_spread.level()
-    out_other = out_spread.finish(spine)
-    square_far, first_send = spine.wait(square_far, first_own)
-    first_near = swap_dp(first_send, 1)
+    square_far = spine.wait(square_far)
     group_factor = lax.rsqrt((square_total + square_far) / (HM * PM) + norm_epsilon)
     groups = attended.shape[1] // HD
     group_width = mixed_raw.shape[1] // groups
@@ -923,9 +943,7 @@
     out_far = swap(out_far.astype(bf16), "row")
     out_near = sum_cols(product(mixed, out_own), col)
     ffn_other = ffn_spread.finish(spine)
-    out_far, mixed_send = spine.wait(out_far, mixed)
-    mixed_near = swap_dp(near_blocks(mixed_send, 1 - near), 1)
-    mixed_kept = near_blocks(mixed_send, near)
+    out_far = spine.wait(out_far)
     second = residual + out_near + out_far.astype(f32)
     second_own = (second * norm_second).astype(bf16)
     second_far = swap(second_own, "row")
@@ -936,9 +954,11 @@
     second_square_far = swap(second_square, "row")
     gate_width = gate_own.shape[1]
     gate_part, up_part = product(second_half, gate_own), product(second_half, up_own)
-    second_far, second_near = spine.wait(second_far, second_near)
+    second_far, second_near, first_send = spine.wait(second_far, second_near, first_own)
+    second_far_near = swap_dp(second_far, 1)
+    first_row = swap(first_send, "row")
+    first_near = swap_dp(first_send, 1)
     second_far = in_order(second_far, swap(second_far, "col"), col, 1)
-    second_far_near = swap(second_near, "row")
     second_near = in_order(second_near, swap(second_near, "col"), col, 1)
     second_factor = lax.rsqrt((second_square + second_square_far) / D + norm_epsilon)
     second_column = second_factor[:, None]
@@ -946,6 +966,8 @@
     up_sum = (up_part + product(second_far, ffn_other[:, gate_width:])) * second_column
     gate_sigmoid = jax.nn.sigmoid(gate_sum)
     gate_act = gate_sum * gate_sigmoid
+    second_far_near, hidden_back = spine.wait(second_far_near, hidden_back)
+    second_far_near = in_order(second_far_near, swap(second_far_near, "col"), col, 1)
     hidden_grad = hidden_back_own + hidden_back.astype(f32)
     gate_grad = hidden_grad * up_sum * gate_sigmoid * (1.0 + gate_sum * (1.0 - gate_sigmoid))
     up_grad = hidden_grad * gate_act
@@ -958,15 +980,15 @@
     second_total_far = swap(second_total, "row")
     ffn_send = swap_dp(part_of(ffn_grad, 1 - near, 1), 1)
     back_far = sum_cols(product_back(ffn_grad, ffn_other), col).astype(bf16)
-    second_total_far, back_far, mixed_near = spine.wait(second_total_far, back_far, mixed_near)
+    second_total_far, back_far, first_row, first_near = spine.wait(
+        second_total_far, back_far, first_row, first_near
+    )
     back_far = swap(back_far, "row")
     back_near = sum_cols(
         product_back(ffn_grad[:, :gate_width], gate_own)
         + product_back(ffn_grad[:, gate_width:], up_own),
         col,
     )
-    second_far_near = spine.wait(second_far_near)
-    second_far_near = in_order(second_far_near, swap(second_far_near, "col"), col, 1)
     back_far, ffn_send = spine.wait(back_far, ffn_send)
     second_in_grad = back_near + back_far.astype(f32)
     second_grad = (
@@ -978,7 +1000,6 @@
     branch = second_grad.astype(bf16)
     branch_far = swap(branch, "row")
     branch_half = in_order(branch, swap(branch, "col"), col, 1)
-    branch_near = swap_dp(branch, 1)
 
     def both_halves(scattered, sent):
         kept = lax.dynamic_index_in_dim(scattered, near, 0, keepdims=False)
@@ -987,23 +1008,29 @@
     def to_neighbour(scattered):
         return swap_dp(lax.dynamic_index_in_dim(scattered, 1 - near, 0, keepdims=False), 1)
 
-    branch_half, mixed_near, mixed_kept, hidden_send = spine.wait(
-        branch_half, mixed_near, mixed_kept, hidden
-    )
-    mixed_near_far = swap(mixed_near, "row")
-    mixed_kept_far = swap(mixed_kept, "row")
-    hidden_near = swap_dp(near_blocks(hidden_send, 1 - near), 1)
+    branch_half = spine.wait(branch_half)
     ffn_kept = part_of(ffn_grad, near, 1)
-    ffn_scatter = Scatter(
-        spine,
-        (outer_sum(second_half, ffn_kept) + outer_sum(second_near, ffn_send)).astype(bf16),
-        True,
-    )
-    ffn_scatter_far = Scatter(
-        spine,
-        (outer_sum(second_far, ffn_kept) + outer_sum(second_far_near, ffn_send)).astype(bf16),
-        True,
-    )
+    blocks = count // 2
+    ffn_sums = call(
+        both_rows_kernel,
+        [shape((blocks, 2, second_half.shape[1] // blocks, ffn_kept.shape[1]), bf16)],
+        [pltpu.VMEM((second_half.shape[1], ffn_kept.shape[1]), f32)],
+        10**6,
+        second_half, second_far, second_near, second_far_near, ffn_kept, ffn_send,
+    )[0]
+    ffn_sums = spine.wait(ffn_sums)
+    ffn_sums = far_sum(ffn_sums.reshape(-1, ffn_kept.shape[1]))
+    mixed_send, hidden_send = spine.wait(mixed, hidden)
+    near_pack = jnp.concatenate(
+        [
+            near_blocks(mixed_send, 1 - near),
+            branch,
+            near_blocks(hidden_send, 1 - near),
+            first_row,
+        ],
+        axis=1,
+    )
+    near_pack = swap_dp(near_pack, 1)
     branch_far = spine.wait(branch_far)
     branch_far = in_order(branch_far, swap(branch_far, "col"), col, 1)
     mixed_grad = product_back(branch_half, out_own) + product_back(branch_far, out_other)
@@ -1016,10 +1043,17 @@
     )
     group_total_far, attention_total = spine.wait(group_total_far, attention_total)
     group_scale = group_factor**2 * (group_total + group_total_far) / (HM * PM)
-    group_scale, first_send, first_near = spine.wait(group_scale, first_own, first_near)
-    first_far = swap(first_send, "row")
-    first_far_near = swap(first_near, "row")
-    first_near = in_order(first_near, swap(first_near, "col"), col, 1)
+    size = branch.shape[1]
+
+    def piece(pack, turn):
+        return pack[:, turn * size : (turn + 1) * size]
+
+    group_scale, mixed_kept = spine.wait(group_scale, near_blocks(mixed, near))
+    mixed_kept_far = swap(mixed_kept, "row")
+    first_pair = jnp.concatenate([first_row, first_near], axis=1)
+    first_pair_col = swap(first_pair, "col")
+    first_far = in_order(piece(first_pair, 0), piece(first_pair_col, 0), col, 1)
+    first_near = in_order(piece(first_pair, 1), piece(first_pair_col, 1), col, 1)
     lanes = (
         jnp.arange(channels)[:, None] // PM == jnp.arange(LANES)[None, :]
     ).astype(bf16)
@@ -1037,46 +1071,30 @@
         gain_wide, lanes, mixed_grad, group_factor[:, None], group_scale[:, None], first_column,
         query_grad,
     )
-    mixer_total = spine.wait(mixer_total)
-    ffn_scatter.add()
-    ffn_scatter_far.add()
-    own_grads, shared_grad = spine.wait(own_grads, shared_grad)
+    mixed_kept_far, first_far, first_near = spine.wait(mixed_kept_far, first_far, first_near)
+    own_grads, shared_grad, near_pack = spine.wait(own_grads, shared_grad, near_pack)
     mix_width = mix_sum.shape[1]
     grads_send = swap_dp(part_of(own_grads, 1 - near, 1), 1)
+    grads_kept = part_of(own_grads, near, 1)
     shared_low = (shared_grad.astype(f32) + swap(shared_grad, "col").astype(f32)).astype(bf16)
     late = jnp.concatenate([part_of(shared_low, col, 1), pair_grad, step_grad], axis=1)
     late_far = swap(late, "row")
-    mixed_kept_far, mixed_near_far, branch_near = spine.wait(
-        mixed_kept_far, mixed_near_far, branch_near
-    )
-    mixed_kept = in_order(mixed_kept, mixed_kept_far, row, 1)
-    mixed_near = in_order(mixed_near, mixed_near_far, row, 1)
-    branch_near = in_order(branch_near, swap(branch_near, "col"), col, 1)
-    out_scatter = Scatter(
-        spine,
-        (outer_sum(mixed_kept, branch_half) + outer_sum(mixed_near, branch_near)).astype(bf16),
-        False,
-        f32,
-    )
-    ffn_near = ffn_scatter.finish()
-    ffn_near_sent = to_neighbour(ffn_near)
-    ffn_far = ffn_scatter_far.finish()
-    ffn_far_sent = to_neighbour(ffn_far)
-    first_far, first_far_near, grads_send = spine.wait(first_far, first_far_near, grads_send)
-    first_far = in_order(first_far, swap(first_far, "col"), col, 1)
+    first_far_near = piece(near_pack, 3)
     first_far_near = in_order(first_far_near, swap(first_far_near, "col"), col, 1)
-    grads_kept = part_of(own_grads, near, 1)
+    grads_send, mixed_send, hidden_send = spine.wait(
+        grads_send, piece(near_pack, 0), piece(near_pack, 2)
+    )
+    near_far = swap(jnp.concatenate([mixed_send, hidden_send], axis=1), "row")
     mixer_scatter_far = Scatter(
         spine,
         (outer_sum(first_far, grads_kept) + outer_sum(first_far_near, grads_send)).astype(bf16),
         True,
     )
-    out_scatter.add()
-    late_far, hidden_send, hidden_near = spine.wait(late_far, hidden, hidden_near)
-    hidden_far = swap(hidden_send, "row")
-    hidden_near_far = swap(hidden_near, "row")
+    late_far, mixer_scatter_far.parts = spine.wait(late_far, mixer_scatter_far.parts)
     half = shared_width // 2
-    late_sum = (late[:, : half + pair_width].astype(f32) + late_far[:, : half + pair_width].astype(f32)).astype(bf16)
+    late_sum = (
+        late[:, : half + pair_width].astype(f32) + late_far[:, : half + pair_width].astype(f32)
+    ).astype(bf16)
     shared_part, pair_low = late_sum[:, :half], late_sum[:, half:]
     step_two = in_order(
         late[:, half + pair_width :][:, :head_count],
@@ -1085,12 +1103,10 @@
         1,
     )
     step_all = in_order(step_two, swap(step_two, "col"), col, 1)
-    shared_low = in_order(shared_part, swap(shared_part, "col"), col, 1)
     rest = jnp.concatenate(
         [pair_low, shared_part, to_lanes(step_all), jnp.zeros((length, LANES), bf16)], axis=1
     )
     rest_send = swap_dp(part_of(rest, 1 - near, 1), 1)
-    mixer_scatter_far.add()
     rest_send = spine.wait(rest_send)
     mixer_scatter = Scatter(
         spine,
@@ -1102,33 +1118,53 @@
         ).astype(bf16),
         True,
     )
-
-    out_weight_grad = out_scatter.finish()[0]
-    hidden_far, hidden_near_far, grads_again = spine.wait(hidden_far, hidden_near_far, own_grads)
+    near_far, mixer_scatter.parts, hidden_send, ffn_sums = spine.wait(
+        near_far, mixer_scatter.parts, hidden, ffn_sums
+    )
+    hidden_far = swap(hidden_send, "row")
+    mixed_kept = in_order(mixed_kept, mixed_kept_far, row, 1)
+    mixed_near = in_order(piece(near_pack, 0), piece(near_far, 0), row, 1)
+    branch_near = in_order(piece(near_pack, 1), swap(piece(near_pack, 1), "col"), col, 1)
+    out_sums = far_sum(
+        spine.wait(
+            (
+                outer_sum(mixed_kept, branch_half) + outer_sum(mixed_near, branch_near)
+            ).astype(bf16)
+        )
+    )
+    ffn_sums = ffn_sums.reshape(2, 2, -1, ffn_kept.shape[1])
+    ffn_sent = swap_dp(lax.dynamic_index_in_dim(ffn_sums, 1 - near, 1, keepdims=False), 1)
+    mixer_scatter_far.add()
+    hidden_far, grads_again = spine.wait(hidden_far, own_grads)
     own_grads_far = swap(grads_again, "row")
     hidden_half = in_order(hidden, hidden_far, row, 1)
-    hidden_near = in_order(hidden_near, hidden_near_far, row, 1)
+    hidden_near = in_order(piece(near_pack, 2), piece(near_far, 1), row, 1)
     cot_near = in_order(cot_near, swap(cot_near, "col"), col, 1)
-    down_scatter = Scatter(
-        spine,
-        (
-            outer_sum(near_blocks(hidden_half, near), cot_half)
-            + outer_sum(hidden_near, cot_near)
-        ).astype(bf16),
-        False,
-        f32,
-    )
+    down_sums = far_sum(
+        spine.wait(
+            (
+                outer_sum(near_blocks(hidden_half, near), cot_half)
+                + outer_sum(hidden_near, cot_near)
+            ).astype(bf16)
+        )
+    )
+    ffn_sent, layer_half = spine.wait(ffn_sent, hidden_half)
+    ffn_near = both_halves(ffn_sums[0], ffn_sent[0])
+    ffn_far = swap(jnp.stack(both_halves(ffn_sums[1], ffn_sent[1])), "row")
+    mixer_scatter.add()
+    layer_out = (second + sum_cols(product(layer_half, down_weight), col)).astype(bf16)
     mixer_far = mixer_scatter_far.finish()
     mixer_far_sent = to_neighbour(mixer_far)
-    mixer_scatter.add()
-    layer_out = (second + sum_cols(product(hidden_half, down_weight), col)).astype(bf16)
-    ffn_far_sent, ffn_near_sent = spine.wait(ffn_far_sent, ffn_near_sent)
-    ffn_near = both_halves(ffn_near, ffn_near_sent)
-    ffn_far = swap(jnp.stack(both_halves(ffn_far, ffn_far_sent)), "row")
-    down_scatter.add()
-    own_grads_far = spine.wait(own_grads_far)
+    first_total, conv_shared_part, own_grads_far = spine.wait(
+        (attention_total + mixer_total)[:, 0], conv_shared_part, own_grads_far
+    )
+    first_total = first_total + swap(first_total, "col")
+    first_total_far = swap(first_total, "row")
+    conv_shared_sum = conv_shared_part + swap(conv_shared_part, "col")
+    conv_shared_far = swap(conv_shared_sum, "row")
     mix_half = in_order(own_grads[:, :mix_width], own_grads_far[:, :mix_width], row, 1)
     query_half = in_order(own_grads[:, mix_width:], own_grads_far[:, mix_width:], row, 1)
+    shared_low = in_order(shared_part, swap(shared_part, "col"), col, 1)
     first_in_partial = (
         product_back(mix_half, mixer_in)
         + product_back(query_half, query_weight)
@@ -1136,14 +1172,10 @@
         + 0.5 * (product_back(shared_low, bc_weight) + product_back(step_all, step_weight))
     )
     first_in_grad = sum_cols(first_in_partial, col)
-    first_total = (attention_total + mixer_total)[:, 0]
-    first_total = first_total + swap(first_total, "col")
-    first_total_far = swap(first_total, "row")
-    conv_shared_sum = conv_shared_part + swap(conv_shared_part, "col")
-    conv_shared_far = swap(conv_shared_sum, "row")
-    first_total_far, conv_shared_far, ffn_far = spine.wait(first_total_far, conv_shared_far, ffn_far)
-    gate_weight_grad = in_order(ffn_near[0], ffn_far[0], row, 1).astype(f32)
-    up_weight_grad = in_order(ffn_near[1], ffn_far[1], row, 1).astype(f32)
+    mixer_far_sent, first_total_far, conv_shared_far = spine.wait(
+        mixer_far_sent, first_total_far, conv_shared_far
+    )
+    mixer_far = swap(jnp.concatenate(both_halves(mixer_far, mixer_far_sent), axis=1), "row")
     input_grad = (
         second_grad
         + norm_first * first_in_grad
@@ -1165,15 +1197,18 @@
     small = jnp.concatenate(pieces).reshape(-1, LANES)
     bits = dp_bits()
     small_far = swap_dp(small, bits[0])
-    mixer_far_sent = spine.wait(mixer_far_sent)
-    mixer_far = swap(jnp.concatenate(both_halves(mixer_far, mixer_far_sent), axis=1), "row")
+    ffn_far = spine.wait(ffn_far)
+    gate_weight_grad = in_order(ffn_near[0], ffn_far[0], row, 1).astype(f32)
+    up_weight_grad = in_order(ffn_near[1], ffn_far[1], row, 1).astype(f32)
     small = small + spine.wait(small_far)
     small_far = swap_dp(small, bits[1])
+    out_weight_grad, down_weight_grad = spine.wait(out_sums, down_sums)
     mixer_near = mixer_scatter.finish()
     mixer_near_sent = to_neighbour(mixer_near)
-    small = small + spine.wait(small_far)
+    small_far, mixer_far = spine.wait(small_far, mixer_far)
+    small = small + small_far
     small_far = swap_dp(small, bits[2])
-    mixer_near_sent, mixer_far = spine.wait(mixer_near_sent, mixer_far)
+    mixer_near_sent = spine.wait(mixer_near_sent)
     mixer_near = both_halves(mixer_near, mixer_near_sent)
     kept_width = grads_kept.shape[1]
     own_sums = jnp.concatenate([mixer_near[0][:, :kept_width], mixer_near[1][:, :kept_width]], axis=1)
@@ -1194,7 +1229,7 @@
         small = small + spine.wait(small_far)
         small_far = swap_dp(small, bit)
     small = small + spine.wait(small_far)
-    down_weight_grad = down_scatter.finish()[0]
+    out_weight_grad, down_weight_grad = out_weight_grad.astype(f32), down_weight_grad.astype(f32)
     small = (small + spine.token).reshape(-1)
     sums, place = [], 0
     for piece in pieces:

time: 575 us -> 561 us (0.976)
  waiting for transfers between devices: 208 us -> 151 us
  other arithmetic: 73.4 us -> 98.4 us
  between operations: 3.12 us -> 16.1 us
  Pallas kernels: 64.9 us -> 74.3 us
    ppermute x42 -> x32, waiting for transfers between devices: 145 us -> 99 us  [swap_dp(): lax.ppermute(values_in, 'dp', [(i, i ^ bit) for i in range(lax.axis_size(...]
    ppermute x58 -> x54, waiting for transfers between devices: 63.4 us -> 47.3 us  [swap(): return lax.ppermute(values_in, axis, [(0, 1), (1, 0)])]
    select_n x27 -> x24, other arithmetic: 21.5 us -> 32.5 us  [in_order(): jnp.where(place == 0, own, other)]
    concatenate x4 -> x11, other arithmetic: 2.62 us -> 12.3 us  [in_order(): jnp.concatenate([jnp.where(place == 0, own, other), jnp.where(place == 0,...]
    pallas_call x4 -> x5, Pallas kernels: 57.3 us -> 66.7 us  [call(): pl.pallas_call(kernel, out_shape=outs, in_specs=[pl.BlockSpec(memory_spac...]
    convert_element_type x2 -> x5, other arithmetic: 1.24 us -> 7.19 us  [the longest x1 2.48 us: local(): (second + sum_cols(product(layer_half, down_weight), col)).astype(bf16)]
    dot_general x12 -> x8, matrix products: 20.6 us -> 17.4 us  [outer_sum(): lax.dot_general(left_side, right_side, (((0,), (0,)), ((), ())), preferre...]
    ppermute x42 -> x32, starting transfers between devices: 51.1 us -> 53.9 us  [swap_dp(): lax.ppermute(values_in, 'dp', [(i, i ^ bit) for i in range(lax.axis_size(...]
  transfers between devices with their start and end apart: 100 -> 89, of which waited for: 34 -> 22; matrix products, arithmetic and copies ran while one was open for 31% -> 37% of each run, Pallas kernels for 11% -> 13%
where the time goes in v4:
time: 561 us; the launch traced here: 550 us
  waiting for transfers between devices  151 us (27%)
  other arithmetic  98.4 us (18%)
  starting transfers between devices  85.9 us (15%)
  matrix products  75.8 us (14%)
  Pallas kernels  74.3 us (13%)
  local copies, waits for them, and re-layouts  49.2 us (9%)
  between operations  16.1 us (3%)
    ppermute x32, waiting for transfers between devices, swap_dp(): lax.ppermute(values_in, 'dp', [(i, i ^ bit) for i in range(lax.axis_size(...  99 us
    pallas_call x5, Pallas kernels, call(): pl.pallas_call(kernel, out_shape=outs, in_specs=[pl.BlockSpec(memory_spac...  66.7 us
    ppermute x32, starting transfers between devices, swap_dp(): lax.ppermute(values_in, 'dp', [(i, i ^ bit) for i in range(lax.axis_size(...  53.9 us
    ppermute x54, waiting for transfers between devices, swap(): return lax.ppermute(values_in, axis, [(0, 1), (1, 0)])  47.3 us
    select_n x24, other arithmetic, in_order(): jnp.where(place == 0, own, other)  32.5 us
    ppermute x54, starting transfers between devices, swap(): return lax.ppermute(values_in, axis, [(0, 1), (1, 0)])  31.5 us
    dot_general x14, matrix products, product(): return jnp.dot(left_side, right_side, preferred_element_type=f32)  31.5 us
    dot_general x12, matrix products, product_back(): lax.dot_general(left_side, right_side, (((1,), (1,)), ((), ())), preferre...  26.9 us
  transfers between devices with their start and end apart: 89, of which 22 were waited for; matrix products, arithmetic and copies ran while one was open for 37% of the time, Pallas kernels for 13%

profile of v4, /device:TPU:0, one launch (start us, length us, event | category | flops | bytes accessed | tf_op | source)
XLA Modules:
  0.0 550.5 jit_solution(6799574801491378935)
XLA Ops:
  34.8 4.8 fusion.8
  39.6 12.0 %collective-permute-done.6 = f32[512]{0:T(512)S(1)} collective-permute-done((f32[512]{0:T(512)S(1)}, f32[512]{0:T(512)S(1)}, u32[]{:S(2)}, u32[]{:S(2)}) %collective-permute-start.6) | collective-permute-done | bytes 2080 | tf_op jit(solution)/shard_map/ppermute | solution.py:45
  65.8 13.5 %collective-permute-done.10.refs_1_ = bf16[128,2048]{1,0:T(8,128)(2,1)} collective-permute-done((bf16[128,2048]{1,0:T(8,128)(2,1)}, bf16[128,2048]{1,0:T(8,128)(2,1)}, u32[]{:S(2)}, u32[]{:S(2)}) %collective-permute-start.10) | collective-permute-done | bytes 524320 | tf_op jit(solution)/shard_map/ppermute | solution.py:94
  79.7 5.4 collective-permute-done.11.refs_2_
  88.8 3.4 collective-permute-done.15.refs_6_
  94.7 4.0 shard_map.330.attended_ref
  107.4 5.4 fusion.6.own_ref
  113.6 16.8 %shard_map.331 = (bf16[512,1024]{1,0:T(8,128)(2,1)}, f32[512,1]{1,0:T(8,128)}, f32[512,1536]{1,0:T(8,128)}, f32[512,768]{1,0:T(8,128)}, bf16[1024,768]{1,0:T(8,128)(2,1)}) custom-call(f32[512,1536]{1,0:T(8,128)} %fusion.6.own_ref, bf16[512,1536]{1,0:T(8,128)(2,1)} %collective-permute-done.17.other_ref, f32[512,1]{1,0:T(8,128)} %copy.81.factor_ref, ...), custom_call_target="tpu_custom_call" | custom-call | flops 100000000 | bytes 1000000 | tf_op jit(solution)/shard_map/pallas_call | solution.py:613
  133.3 3.1 shard_map.332
  150.5 5.5 %collective-permute-done.27.refs_7_ = bf16[128,2048]{1,0:T(8,128)(2,1)} collective-permute-done((bf16[128,2048]{1,0:T(8,128)(2,1)}, bf16[128,2048]{1,0:T(8,128)(2,1)}, u32[]{:S(2)}, u32[]{:S(2)}) %collective-permute-start.27) | collective-permute-done | bytes 524320 | tf_op jit(solution)/shard_map/ppermute | solution.py:94
  156.1 5.6 %collective-permute-done.29 = bf16[512,512]{1,0:T(8,128)(2,1)} collective-permute-done((bf16[512,512]{1,0:T(8,128)(2,1)S(1)}, bf16[512,512]{1,0:T(8,128)(2,1)}, u32[]{:S(2)}, u32[]{:S(2)}) %collective-permute-start.29) | collective-permute-done | bytes 524320 | tf_op jit(solution)/shard_map/ppermute | solution.py:45
  171.3 4.5 shard_map.333
  187.4 6.8 %collective-permute-done.32 = bf16[512,512]{1,0:T(8,128)(2,1)S(1)} collective-permute-done((bf16[512,512]{1,0:T(8,128)(2,1)}, bf16[512,512]{1,0:T(8,128)(2,1)S(1)}, u32[]{:S(2)}, u32[]{:S(2)}) %collective-permute-start.32) | collective-permute-done | bytes 524320 | tf_op jit(solution)/shard_map/ppermute | solution.py:94
  199.0 3.7 multiply_convert_fusion.2
  219.1 16.8 %collective-permute-done.43.sent_ref = bf16[512,1024]{1,0:T(8,128)(2,1)S(1)} collective-permute-done((bf16[512,1024]{1,0:T(8,128)(2,1)S(1)}, bf16[512,1024]{1,0:T(8,128)(2,1)S(1)}, u32[]{:S(2)}, u32[]{:S(2)}) %collective-permute-start.43) | collective-permute-done | bytes 1048608 | tf_op jit(solution)/shard_map/ppermute | solution.py:94
  241.4 9.3 %shard_map.334 = bf16[4,2,256,1024]{3,2,1,0:T(8,128)(2,1)} custom-call(bf16[512,1024]{1,0:T(8,128)(2,1)} %pad_maximum_fusion.6.own_ref, bf16[512,1024]{1,0:T(8,128)(2,1)} %pad_maximum_fusion.7.far_ref, bf16[512,1024]{1,0:T(8,128)(2,1)} %pad_maximum_fusion.9.near_ref, bf16[512,1024]{1,0:T(8,128)(2,1)} %pad_maximum_fusion.10.far_near_ref, ...), custom_call_target="tpu_custom_call" | custom-call | flops 1000000 | bytes 1000000 | tf_op jit(solution)/shard_map/pallas_call | solution.py:613
  261.5 3.5 broadcast_select_fusion.17
  267.3 3.4 fusion.29
  276.9 7.6 %shard_map.335 = (bf16[512,256]{1,0:T(8,128)(2,1)}, bf16[512,256]{1,0:T(8,128)(2,1)}, f32[512,1]{1,0:T(8,128)}) custom-call(f32[512,256]{1,0:T(8,128)} %fusion.56.query_ref, f32[512,256]{1,0:T(8,128)} %get-tuple-element.487.pair_ref, f32[512,128]{1,0:T(8,128)} %get-tuple-element.522.cosine_ref, f32[512,128]{1,0:T(8,128)} %get-tuple-element.523.sine_ref, ...), custom_call_target="tpu_custom_call" | custom-call | flops 100000000 | bytes 1000000 | tf_op jit(solution)/shard_map/pallas_call | solution.py:613
  288.1 29.0 %shard_map.336 = (bf16[512,1792]{1,0:T(8,128)(2,1)}, bf16[512,512]{1,0:T(8,128)(2,1)}, bf16[512,128]{1,0:T(8,128)(2,1)}, f32[4,768]{1,0:T(4,128)}, f32[4,512]{1,...) custom-call(f32[512,1536]{1,0:T(8,128)} %get-tuple-element.245.mix_ref, ...), custom_call_target="tpu_custom_call" | custom-call | flops 100000000 | bytes 1000000 | tf_op jit(solution)/shard_map/pallas_call | solution.py:613
  328.9 3.3 fusion.66
  335.6 13.2 %collective-permute-done.55 = bf16[512,896]{1,0:T(8,128)(2,1)S(1)} collective-permute-done((bf16[512,896]{1,0:T(8,128)(2,1)S(1)}, bf16[512,896]{1,0:T(8,128)(2,1)S(1)}, u32[]{:S(2)}, u32[]{:S(2)}) %collective-permute-start.55) | collective-permute-done | bytes 917536 | tf_op jit(solution)/shard_map/ppermute | solution.py:94
  373.2 5.9 %collective-permute-done.60 = bf16[512,384]{1,0:T(8,128)(2,1)S(1)} collective-permute-done((bf16[512,384]{1,0:T(8,128)(2,1)S(1)}, bf16[512,384]{1,0:T(8,128)(2,1)S(1)}, u32[]{:S(2)}, u32[]{:S(2)}) %collective-permute-start.60) | collective-permute-done | bytes 393248 | tf_op jit(solution)/shard_map/ppermute | solution.py:94
  387.3 3.0 broadcast_select_fusion.5
  399.9 3.3 collective-permute-start.69
  422.3 26.4 %collective-permute-done.68 = bf16[2,2,128,1280]{3,2,1,0:T(8,128)(2,1)} collective-permute-done((bf16[2,2,128,1280]{3,2,1,0:T(8,128)(2,1)}, bf16[2,2,128,1280]{3,2,1,0:T(8,128)(2,1)}, u32[]{:S(2)}, u32[]{:S(2)}) %collective-permute-start.68) | collective-permute-done | bytes 1310752 | tf_op jit(solution)/shard_map/ppermute | solution.py:94
  448.7 4.0 collective-permute-start.70
  462.1 8.5 %collective-permute-start.80 = (bf16[2,128,1280]{2,1,0:T(8,128)(2,1)}, bf16[2,128,1280]{2,1,0:T(8,128)(2,1)}, u32[]{:S(2)}, u32[]{:S(2)}) collective-permute-start(bf16[2,128,1280]{2,1,0:T(8,128)(2,1)} %dynamic-slice_bitcast_fusion.4), channel_id=1, source_target_pairs={{0,16},{4,20},{8,24},{12,28},{16,0},{20,4},{24,8},{28,12},{1,17},{... | collective-permute-start | bytes 1966088 | tf_op jit(solution)/shard_map/ppermute | solution.py:94
  473.2 15.9 %collective-permute-done.70 = bf16[512,1792]{1,0:T(8,128)(2,1)} collective-permute-done((bf16[512,1792]{1,0:T(8,128)(2,1)}, bf16[512,1792]{1,0:T(8,128)(2,1)}, u32[]{:S(2)}, u32[]{:S(2)}) %collective-permute-start.70) | collective-permute-done | bytes 1835040 | tf_op jit(solution)/shard_map/ppermute | solution.py:45
  493.7 5.7 %fusion = f32[512,1024]{1,0:T(8,128)S(1)} fusion(bf16[1024,3072]{1,0:T(8,128)(2,1)} %param.21, bf16[512,1536]{1,0:T(8,128)(2,1)S(1)} %get-tuple-element.417, bf16[512,1536]{1,0:T(8,128)(2,1)S(1)} %get-tuple-element.416), kind=kOutput, calls=%fused_computation.4 | convolution fusion | flops 3227516928 | bytes 11534336 | tf_op jit(solution)/shard_map/dot_general | solution.py:33
  515.9 4.4 reduce-scatter.8.cloned.1.call-done
  525.9 5.3 collective-permute-start.84
  (610 shorter events, 271.1 us)
Async XLA Ops:
  7.2 378.7 %reduce-scatter.4.cloned.1.call-start = ((), (), s32[]{:S(2)}) async-start(), calls=%async_computation.3 | async-start | bytes 5242880 | tf_op jit(solution)/shard_map/reduce_scatter | solution.py:147
  23.4 32.7 %collective-permute-start.4 = (bf16[512,896]{1,0:T(8,128)(2,1)}, bf16[512,896]{1,0:T(8,128)(2,1)}, u32[]{:S(2)}, u32[]{:S(2)}) collective-permute-start(bf16[512,896]{1,0:T(8,128)(2,1)} %fusion.90), channel_id=1, source_target_pairs={{0,2},{2,0},{1,3},{3,1},{4,6},{6,4},{5,7},{7,5},{8,10},{10,8},{9,1... | collective-permute-start | bytes 2752520 | tf_op jit(solution)/shard_map/ppermute | solution.py:45
  27.4 26.1 %collective-permute-start.3 = (bf16[512,512]{1,0:T(8,128)(2,1)S(1)}, bf16[512,512]{1,0:T(8,128)(2,1)}, u32[]{:S(2)}, u32[]{:S(2)}) collective-permute-start(bf16[512,512]{1,0:T(8,128)(2,1)S(1)} %copy-done.25), channel_id=1, source_target_pairs={{0,4},{4,0},{8,12},{12,8},{16,20},{20,16},{24,28},{28,24},{1,5},{5... | collective-permute-start | bytes 1572872 | tf_op jit(solution)/shard_map/ppermute | solution.py:94
  29.4 30.4 %collective-permute-start.7 = (bf16[128,1024]{1,0:T(8,128)(2,1)}, bf16[128,1024]{1,0:T(8,128)(2,1)S(1)}, u32[]{:S(2)}, u32[]{:S(2)}) collective-permute-start(bf16[128,1024]{1,0:T(8,128)(2,1)} %collective-permute-done.1.refs_0_), channel_id=1, source_target_pairs={{0,16},{4,20},{8,24},{12,28},{16,0},{20,4},{24,8},{28,12},{1,17},{... | collective-permute-start | bytes 786440 | tf_op jit(solution)/shard_map/ppermute | solution.py:94
  33.2 28.2 %collective-permute-start.8 = (bf16[128,1024]{1,0:T(8,128)(2,1)}, bf16[128,1024]{1,0:T(8,128)(2,1)S(1)}, u32[]{:S(2)}, u32[]{:S(2)}) collective-permute-start(bf16[128,1024]{1,0:T(8,128)(2,1)} %collective-permute-done.1.refs_0_), channel_id=1, source_target_pairs={{0,8},{4,12},{8,0},{12,4},{16,24},{20,28},{24,16},{28,20},{1,9},{5... | collective-permute-start | bytes 786440 | tf_op jit(solution)/shard_map/ppermute | solution.py:94
  53.5 25.8 %collective-permute-start.10 = (bf16[128,2048]{1,0:T(8,128)(2,1)}, bf16[128,2048]{1,0:T(8,128)(2,1)}, u32[]{:S(2)}, u32[]{:S(2)}) collective-permute-start(bf16[128,2048]{1,0:T(8,128)(2,1)} %collective-permute-done.2.refs_0_), channel_id=1, source_target_pairs={{0,16},{4,20},{8,24},{12,28},{16,0},{20,4},{24,8},{28,12},{1,17},{... | collective-permute-start | bytes 1572872 | tf_op jit(solution)/shard_map/ppermute | solution.py:94
  56.1 43.7 %collective-permute-start.17 = (bf16[512,1536]{1,0:T(8,128)(2,1)}, bf16[512,1536]{1,0:T(8,128)(2,1)}, u32[]{:S(2)}, u32[]{:S(2)}) collective-permute-start(bf16[512,1536]{1,0:T(8,128)(2,1)} %fusion.8), channel_id=1, source_target_pairs={{0,2},{2,0},{1,3},{3,1},{4,6},{6,4},{5,7},{7,5},{8,10},{10,8},{9,1... | collective-permute-start | bytes 4718600 | tf_op jit(solution)/shard_map/ppermute | solution.py:45
  59.8 25.3 %collective-permute-start.11 = (bf16[128,2048]{1,0:T(8,128)(2,1)}, bf16[128,2048]{1,0:T(8,128)(2,1)}, u32[]{:S(2)}, u32[]{:S(2)}) collective-permute-start(bf16[128,2048]{1,0:T(8,128)(2,1)} %collective-permute-done.2.refs_0_), channel_id=1, source_target_pairs={{0,8},{4,12},{8,0},{12,4},{16,24},{20,28},{24,16},{28,20},{1,9},{5... | collective-permute-start | bytes 1572872 | tf_op jit(solution)/shard_map/ppermute | solution.py:94
  63.1 25.7 %collective-permute-start.13 = (bf16[128,1024]{1,0:T(8,128)(2,1)}, bf16[128,1024]{1,0:T(8,128)(2,1)S(1)}, u32[]{:S(2)}, u32[]{:S(2)}) collective-permute-start(bf16[128,1024]{1,0:T(8,128)(2,1)} %copy-done.82), channel_id=1, source_target_pairs={{0,8},{4,12},{8,0},{12,4},{16,24},{20,28},{24,16},{28,20},{1,9},{5... | collective-permute-start | bytes 786440 | tf_op jit(solution)/shard_map/ppermute | solution.py:94
  99.8 30.6 %collective-permute-start.20 = (bf16[512,1024]{1,0:T(8,128)(2,1)}, bf16[512,1024]{1,0:T(8,128)(2,1)}, u32[]{:S(2)}, u32[]{:S(2)}) collective-permute-start(bf16[512,1024]{1,0:T(8,128)(2,1)} %fusion.45), channel_id=1, source_target_pairs={{0,2},{2,0},{1,3},{3,1},{4,6},{6,4},{5,7},{7,5},{8,10},{10,8},{9,1... | collective-permute-start | bytes 3145736 | tf_op jit(solution)/shard_map/ppermute | solution.py:45
  101.6 34.8 %collective-permute-start.22 = (bf16[128,2048]{1,0:T(8,128)(2,1)}, bf16[128,2048]{1,0:T(8,128)(2,1)}, u32[]{:S(2)}, u32[]{:S(2)}) collective-permute-start(bf16[128,2048]{1,0:T(8,128)(2,1)} %collective-permute-done.10.refs_1_), channel_id=1, source_target_pairs={{0,8},{4,12},{8,0},{12,4},{16,24},{20,28},{24,16},{28,20},{1,9},{5... | collective-permute-start | bytes 1572872 | tf_op jit(solution)/shard_map/ppermute | solution.py:94
  103.4 33.0 %collective-permute-start.23 = (bf16[128,2048]{1,0:T(8,128)(2,1)}, bf16[128,2048]{1,0:T(8,128)(2,1)}, u32[]{:S(2)}, u32[]{:S(2)}) collective-permute-start(bf16[128,2048]{1,0:T(8,128)(2,1)} %collective-permute-done.10.refs_1_), channel_id=1, source_target_pairs={{0,4},{4,0},{8,12},{12,8},{16,20},{20,16},{24,28},{28,24},{1,5},{5... | collective-permute-start | bytes 1572872 | tf_op jit(solution)/shard_map/ppermute | solution.py:94
  104.9 31.5 %collective-permute-start.24 = (bf16[128,2048]{1,0:T(8,128)(2,1)}, bf16[128,2048]{1,0:T(8,128)(2,1)}, u32[]{:S(2)}, u32[]{:S(2)}) collective-permute-start(bf16[128,2048]{1,0:T(8,128)(2,1)} %collective-permute-done.11.refs_2_), channel_id=1, source_target_pairs={{0,4},{4,0},{8,12},{12,8},{16,20},{20,16},{24,28},{28,24},{1,5},{5... | collective-permute-start | bytes 1572872 | tf_op jit(solution)/shard_map/ppermute | solution.py:94
  180.0 32.4 %collective-permute-start.40 = (bf16[512,512]{1,0:T(8,128)(2,1)S(1)}, bf16[512,512]{1,0:T(8,128)(2,1)S(1)}, u32[]{:S(2)}, u32[]{:S(2)}) collective-permute-start(bf16[512,512]{1,0:T(8,128)(2,1)S(1)} %copy-done.35), channel_id=1, source_target_pairs={{0,2},{2,0},{1,3},{3,1},{4,6},{6,4},{5,7},{7,5},{8,10},{10,8},{9,1... | collective-permute-start | bytes 1572872 | tf_op jit(solution)/shard_map/ppermute | solution.py:45
  180.5 31.9 %collective-permute-start.41 = (bf16[512,512]{1,0:T(8,128)(2,1)S(1)}, bf16[512,512]{1,0:T(8,128)(2,1)S(1)}, u32[]{:S(2)}, u32[]{:S(2)}) collective-permute-start(bf16[512,512]{1,0:T(8,128)(2,1)S(1)} %copy-done.35), channel_id=1, source_target_pairs={{0,4},{4,0},{8,12},{12,8},{16,20},{20,16},{24,28},{28,24},{1,5},{5... | collective-permute-start | bytes 1572872 | tf_op jit(solution)/shard_map/ppermute | solution.py:94
  181.9 33.8 %collective-permute-start.46 = (bf16[512,512]{1,0:T(8,128)(2,1)}, bf16[512,512]{1,0:T(8,128)(2,1)S(1)}, u32[]{:S(2)}, u32[]{:S(2)}) collective-permute-start(bf16[512,512]{1,0:T(8,128)(2,1)} %collective-permute-done.31), channel_id=1, source_target_pairs={{0,1},{1,0},{2,3},{3,2},{4,5},{5,4},{6,7},{7,6},{8,9},{9,8},{10,11... | collective-permute-start | bytes 1572872 | tf_op jit(solution)/shard_map/ppermute | solution.py:45
  210.8 25.1 %collective-permute-start.43 = (bf16[512,1024]{1,0:T(8,128)(2,1)S(1)}, bf16[512,1024]{1,0:T(8,128)(2,1)S(1)}, u32[]{:S(2)}, u32[]{:S(2)}) collective-permute-start(bf16[512,1024]{1,0:T(8,128)(2,1)S(1)} %get-tuple-element.438), channel_id=1, source_target_pairs={{0,4},{4,0},{8,12},{12,8},{16,20},{20,16},{24,28},{28,24},{1,5},{5... | collective-permute-start | bytes 3145736 | tf_op jit(solution)/shard_map/ppermute | solution.py:94
  212.4 27.1 %collective-permute-start.47 = (bf16[512,512]{1,0:T(8,128)(2,1)S(1)}, bf16[512,512]{1,0:T(8,128)(2,1)S(1)}, u32[]{:S(2)}, u32[]{:S(2)}) collective-permute-start(bf16[512,512]{1,0:T(8,128)(2,1)S(1)} %collective-permute-done.32), channel_id=1, source_target_pairs={{0,1},{1,0},{2,3},{3,2},{4,5},{5,4},{6,7},{7,6},{8,9},{9,8},{10,11... | collective-permute-start | bytes 1572872 | tf_op jit(solution)/shard_map/ppermute | solution.py:45
  253.7 262.2 %reduce-scatter.6.cloned.1.call-start = ((), (), s32[]{:S(2)}) async-start(), calls=%async_computation.4 | async-start | bytes 2621440 | tf_op jit(solution)/shard_map/reduce_scatter | solution.py:147
  265.0 57.9 %collective-permute-start.54 = (bf16[512,2048]{1,0:T(8,128)(2,1)}, bf16[512,2048]{1,0:T(8,128)(2,1)}, u32[]{:S(2)}, u32[]{:S(2)}) collective-permute-start(bf16[512,2048]{1,0:T(8,128)(2,1)} %get-tuple-element.500), channel_id=1, source_target_pairs={{0,4},{4,0},{8,12},{12,8},{16,20},{20,16},{24,28},{28,24},{1,5},{5... | collective-permute-start | bytes 6291464 | tf_op jit(solution)/shard_map/ppermute | solution.py:94
  284.6 38.3 %collective-permute-start.52 = (bf16[512,512]{1,0:T(8,128)(2,1)}, bf16[512,512]{1,0:T(8,128)(2,1)}, u32[]{:S(2)}, u32[]{:S(2)}) collective-permute-start(bf16[512,512]{1,0:T(8,128)(2,1)} %pad_maximum_fusion.17), channel_id=1, source_target_pairs={{0,2},{2,0},{1,3},{3,1},{4,6},{6,4},{5,7},{7,5},{8,10},{10,8},{9,1... | collective-permute-start | bytes 1572872 | tf_op jit(solution)/shard_map/ppermute | solution.py:45
  335.5 51.8 %collective-permute-start.62 = (bf16[512,512]{1,0:T(8,128)(2,1)}, bf16[512,512]{1,0:T(8,128)(2,1)}, u32[]{:S(2)}, u32[]{:S(2)}) collective-permute-start(bf16[512,512]{1,0:T(8,128)(2,1)} %get-tuple-element.434), channel_id=1, source_target_pairs={{0,1},{1,0},{2,3},{3,2},{4,5},{5,4},{6,7},{7,6},{8,9},{9,8},{10,11... | collective-permute-start | bytes 1572872 | tf_op jit(solution)/shard_map/ppermute | solution.py:45
  350.0 35.9 %collective-permute-start.61 = (bf16[512,1024]{1,0:T(8,128)(2,1)}, bf16[512,1024]{1,0:T(8,128)(2,1)}, u32[]{:S(2)}, u32[]{:S(2)}) collective-permute-start(bf16[512,1024]{1,0:T(8,128)(2,1)} %pad_maximum_fusion.14), channel_id=1, source_target_pairs={{0,2},{2,0},{1,3},{3,1},{4,6},{6,4},{5,7},{7,5},{8,10},{10,8},{9,1... | collective-permute-start | bytes 3145736 | tf_op jit(solution)/shard_map/ppermute | solution.py:45
  354.8 38.3 %collective-permute-start.63 = (bf16[2,2,128,896]{3,2,1,0:T(8,128)(2,1)}, bf16[2,2,128,896]{3,2,1,0:T(8,128)(2,1)}, u32[]{:S(2)}, u32[]{:S(2)}) collective-permute-start(bf16[2,2,128,896]{3,2,1,0:T(8,128)(2,1)} %get-tuple-element.439), channel_id=1, source_target_pairs={{0,8},{4,12},{8,0},{12,4},{16,24},{20,28},{24,16},{28,20},{1,9},{5... | collective-permute-start | bytes 2752520 | tf_op jit(solution)/shard_map/ppermute | solution.py:94
  384.2 64.5 %collective-permute-start.68 = (bf16[2,2,128,1280]{3,2,1,0:T(8,128)(2,1)}, bf16[2,2,128,1280]{3,2,1,0:T(8,128)(2,1)}, u32[]{:S(2)}, u32[]{:S(2)}) collective-permute-start(bf16[2,2,128,1280]{3,2,1,0:T(8,128)(2,1)} %get-tuple-element.422), channel_id=1, source_target_pairs={{0,8},{4,12},{8,0},{12,4},{16,24},{20,28},{24,16},{28,20},{1,9},{5... | collective-permute-start | bytes 3932168 | tf_op jit(solution)/shard_map/ppermute | solution.py:94
  399.9 48.8 %collective-permute-start.69 = (bf16[2,128,896]{2,1,0:T(8,128)(2,1)}, bf16[2,128,896]{2,1,0:T(8,128)(2,1)}, u32[]{:S(2)}, u32[]{:S(2)}) collective-permute-start(bf16[2,128,896]{2,1,0:T(8,128)(2,1)} %dynamic-slice_bitcast_fusion.6), channel_id=1, source_target_pairs={{0,16},{4,20},{8,24},{12,28},{16,0},{20,4},{24,8},{28,12},{1,17},{... | collective-permute-start | bytes 1376264 | tf_op jit(solution)/shard_map/ppermute | solution.py:94
  403.2 117.0 %reduce-scatter.8.cloned.1.call-start = ((), (), s32[]{:S(2)}) async-start(), calls=%async_computation.5 | async-start | bytes 2621440 | tf_op jit(solution)/shard_map/reduce_scatter | solution.py:147
  422.3 48.4 %collective-permute-start.67 = (bf16[512,512]{1,0:T(8,128)(2,1)}, bf16[512,512]{1,0:T(8,128)(2,1)}, u32[]{:S(2)}, u32[]{:S(2)}) collective-permute-start(bf16[512,512]{1,0:T(8,128)(2,1)} %dynamic-slice_convert_fusion.1), channel_id=1, source_target_pairs={{0,1},{1,0},{2,3},{3,2},{4,5},{5,4},{6,7},{7,6},{8,9},{9,8},{10,11... | collective-permute-start | bytes 1572872 | tf_op jit(solution)/shard_map/ppermute | solution.py:45
  448.7 40.4 %collective-permute-start.70 = (bf16[512,1792]{1,0:T(8,128)(2,1)}, bf16[512,1792]{1,0:T(8,128)(2,1)}, u32[]{:S(2)}, u32[]{:S(2)}) collective-permute-start(bf16[512,1792]{1,0:T(8,128)(2,1)} %get-tuple-element.291), channel_id=1, source_target_pairs={{0,2},{2,0},{1,3},{3,1},{4,6},{6,4},{5,7},{7,5},{8,10},{10,8},{9,1... | collective-permute-start | bytes 5505032 | tf_op jit(solution)/shard_map/ppermute | solution.py:45
  454.6 48.1 %collective-permute-start.74 = (bf16[128,896]{1,0:T(8,128)(2,1)}, bf16[128,896]{1,0:T(8,128)(2,1)}, u32[]{:S(2)}, u32[]{:S(2)}) collective-permute-start(bf16[128,896]{1,0:T(8,128)(2,1)} %dynamic-slice_bitcast_fusion.8), channel_id=1, source_target_pairs={{0,4},{4,0},{8,12},{12,8},{16,20},{20,16},{24,28},{28,24},{1,5},{5... | collective-permute-start | bytes 688136 | tf_op jit(solution)/shard_map/ppermute | solution.py:94
  458.5 49.3 %collective-permute-start.78 = (bf16[2,128,1024]{2,1,0:T(8,128)(2,1)}, bf16[2,128,1024]{2,1,0:T(8,128)(2,1)}, u32[]{:S(2)}, u32[]{:S(2)}) collective-permute-start(bf16[2,128,1024]{2,1,0:T(8,128)(2,1)} %pad_maximum_fusion.18), channel_id=1, source_target_pairs={{0,2},{2,0},{1,3},{3,1},{4,6},{6,4},{5,7},{7,5},{8,10},{10,8},{9,1... | collective-permute-start | bytes 1572872 | tf_op jit(solution)/shard_map/ppermute | solution.py:45
  462.1 58.2 %collective-permute-start.80 = (bf16[2,128,1280]{2,1,0:T(8,128)(2,1)}, bf16[2,128,1280]{2,1,0:T(8,128)(2,1)}, u32[]{:S(2)}, u32[]{:S(2)}) collective-permute-start(bf16[2,128,1280]{2,1,0:T(8,128)(2,1)} %dynamic-slice_bitcast_fusion.4), channel_id=1, source_target_pairs={{0,16},{4,20},{8,24},{12,28},{16,0},{20,4},{24,8},{28,12},{1,17},{... | collective-permute-start | bytes 1966088 | tf_op jit(solution)/shard_map/ppermute | solution.py:94
  (174 other events, 1649.6 us)
Sparse Core Ops, SparseCore 0:
  253.8 76.0 reduce-scatter.3
  403.4 56.9 reduce-scatter.5
  470.8 49.4 reduce-scatter.7

commit v5 on v4

--- a/solution.py
+++ b/solution.py
@@ -966,8 +966,6 @@
     up_sum = (up_part + product(second_far, ffn_other[:, gate_width:])) * second_column
     gate_sigmoid = jax.nn.sigmoid(gate_sum)
     gate_act = gate_sum * gate_sigmoid
-    second_far_near, hidden_back = spine.wait(second_far_near, hidden_back)
-    second_far_near = in_order(second_far_near, swap(second_far_near, "col"), col, 1)
     hidden_grad = hidden_back_own + hidden_back.astype(f32)
     gate_grad = hidden_grad * up_sum * gate_sigmoid * (1.0 + gate_sum * (1.0 - gate_sigmoid))
     up_grad = hidden_grad * gate_act
@@ -980,6 +978,8 @@
     second_total_far = swap(second_total, "row")
     ffn_send = swap_dp(part_of(ffn_grad, 1 - near, 1), 1)
     back_far = sum_cols(product_back(ffn_grad, ffn_other), col).astype(bf16)
+    second_far_near = spine.wait(second_far_near)
+    second_far_near = in_order(second_far_near, swap(second_far_near, "col"), col, 1)
     second_total_far, back_far, first_row, first_near = spine.wait(
         second_total_far, back_far, first_row, first_near
     )
@@ -989,7 +989,13 @@
         + product_back(ffn_grad[:, gate_width:], up_own),
         col,
     )
-    back_far, ffn_send = spine.wait(back_far, ffn_send)
+    first_pair_col = swap(jnp.concatenate([first_row, first_near], axis=1), "col")
+    size = first_row.shape[1]
+    first_far = in_order(first_row, first_pair_col[:, :size], col, 1)
+    first_near = in_order(first_near, first_pair_col[:, size:], col, 1)
+    back_far, ffn_send, first_far, first_near = spine.wait(
+        back_far, ffn_send, first_far, first_near
+    )
     second_in_grad = back_near + back_far.astype(f32)
     second_grad = (
         cotangent.astype(f32)
@@ -1043,17 +1049,12 @@
     )
     group_total_far, attention_total = spine.wait(group_total_far, attention_total)
     group_scale = group_factor**2 * (group_total + group_total_far) / (HM * PM)
-    size = branch.shape[1]
 
     def piece(pack, turn):
         return pack[:, turn * size : (turn + 1) * size]
 
     group_scale, mixed_kept = spine.wait(group_scale, near_blocks(mixed, near))
     mixed_kept_far = swap(mixed_kept, "row")
-    first_pair = jnp.concatenate([first_row, first_near], axis=1)
-    first_pair_col = swap(first_pair, "col")
-    first_far = in_order(piece(first_pair, 0), piece(first_pair_col, 0), col, 1)
-    first_near = in_order(piece(first_pair, 1), piece(first_pair_col, 1), col, 1)
     lanes = (
         jnp.arange(channels)[:, None] // PM == jnp.arange(LANES)[None, :]
     ).astype(bf16)
@@ -1071,7 +1072,7 @@
         gain_wide, lanes, mixed_grad, group_factor[:, None], group_scale[:, None], first_column,
         query_grad,
     )
-    mixed_kept_far, first_far, first_near = spine.wait(mixed_kept_far, first_far, first_near)
+    mixed_kept_far = spine.wait(mixed_kept_far)
     own_grads, shared_grad, near_pack = spine.wait(own_grads, shared_grad, near_pack)
     mix_width = mix_sum.shape[1]
     grads_send = swap_dp(part_of(own_grads, 1 - near, 1), 1)

time: 561 us -> 554 us (0.988)
  other arithmetic: 98.4 us -> 91.1 us
    ppermute x32, waiting for transfers between devices: 99 us -> 92 us  [swap_dp(): lax.ppermute(values_in, 'dp', [(i, i ^ bit) for i in range(lax.axis_size(...]
    unnamed x241 -> x233, local copies, waits for them, and re-layouts: 14.7 us -> 15.7 us
  transfers between devices with their start and end apart: 89 -> 89, of which waited for: 22 -> 23; matrix products, arithmetic and copies ran while one was open for 37% -> 36% of each run, Pallas kernels for 13% -> 14%
where the time goes in v5:
time: 554 us; the launch traced here: 543 us
  waiting for transfers between devices  146 us (26%)
  other arithmetic  91.1 us (16%)
  starting transfers between devices  86.8 us (16%)
  matrix products  76.5 us (14%)
  Pallas kernels  74.2 us (13%)
  local copies, waits for them, and re-layouts  52.2 us (9%)
  between operations  16.2 us (3%)
    ppermute x32, waiting for transfers between devices, swap_dp(): lax.ppermute(values_in, 'dp', [(i, i ^ bit) for i in range(lax.axis_size(...  92 us
    pallas_call x5, Pallas kernels, call(): pl.pallas_call(kernel, out_shape=outs, in_specs=[pl.BlockSpec(memory_spac...  66.7 us
    ppermute x32, starting transfers between devices, swap_dp(): lax.ppermute(values_in, 'dp', [(i, i ^ bit) for i in range(lax.axis_size(...  52.6 us
    ppermute x54, waiting for transfers between devices, swap(): return lax.ppermute(values_in, axis, [(0, 1), (1, 0)])  50.1 us
    ppermute x54, starting transfers between devices, swap(): return lax.ppermute(values_in, axis, [(0, 1), (1, 0)])  34 us
    dot_general x14, matrix products, product(): return jnp.dot(left_side, right_side, preferred_element_type=f32)  31.4 us
    select_n x24, other arithmetic, in_order(): jnp.where(place == 0, own, other)  28 us
    dot_general x12, matrix products, product_back(): lax.dot_general(left_side, right_side, (((1,), (1,)), ((), ())), preferre...  27.6 us
  transfers between devices with their start and end apart: 89, of which 23 were waited for; matrix products, arithmetic and copies ran while one was open for 36% of the time, Pallas kernels for 14%

profile of v5, /device:TPU:0, one launch (start us, length us, event | category | flops | bytes accessed | tf_op | source)
XLA Modules:
  0.0 543.0 jit_solution(7510441775552451753)
XLA Ops:
  34.9 4.8 fusion.8
  39.7 12.0 %collective-permute-done.6 = f32[512]{0:T(512)S(1)} collective-permute-done((f32[512]{0:T(512)S(1)}, f32[512]{0:T(512)S(1)}, u32[]{:S(2)}, u32[]{:S(2)}) %collective-permute-start.6) | collective-permute-done | bytes 2080 | tf_op jit(solution)/shard_map/ppermute | solution.py:45
  65.8 13.5 %collective-permute-done.10.refs_1_ = bf16[128,2048]{1,0:T(8,128)(2,1)} collective-permute-done((bf16[128,2048]{1,0:T(8,128)(2,1)}, bf16[128,2048]{1,0:T(8,128)(2,1)}, u32[]{:S(2)}, u32[]{:S(2)}) %collective-permute-start.10) | collective-permute-done | bytes 524320 | tf_op jit(solution)/shard_map/ppermute | solution.py:94
  79.7 5.4 collective-permute-done.11.refs_2_
  88.7 3.4 collective-permute-done.15.refs_6_
  94.7 4.0 shard_map.330.attended_ref
  107.4 5.4 fusion.6.own_ref
  113.6 16.8 %shard_map.331 = (bf16[512,1024]{1,0:T(8,128)(2,1)}, f32[512,1]{1,0:T(8,128)}, f32[512,1536]{1,0:T(8,128)}, f32[512,768]{1,0:T(8,128)}, bf16[1024,768]{1,0:T(8,128)(2,1)}) custom-call(f32[512,1536]{1,0:T(8,128)} %fusion.6.own_ref, bf16[512,1536]{1,0:T(8,128)(2,1)} %collective-permute-done.17.other_ref, f32[512,1]{1,0:T(8,128)} %copy.81.factor_ref, ...), custom_call_target="tpu_custom_call" | custom-call | flops 100000000 | bytes 1000000 | tf_op jit(solution)/shard_map/pallas_call | solution.py:613
  150.0 6.1 %collective-permute-done.27.refs_7_ = bf16[128,2048]{1,0:T(8,128)(2,1)} collective-permute-done((bf16[128,2048]{1,0:T(8,128)(2,1)}, bf16[128,2048]{1,0:T(8,128)(2,1)}, u32[]{:S(2)}, u32[]{:S(2)}) %collective-permute-start.27) | collective-permute-done | bytes 524320 | tf_op jit(solution)/shard_map/ppermute | solution.py:94
  156.1 5.6 %collective-permute-done.29 = bf16[512,512]{1,0:T(8,128)(2,1)} collective-permute-done((bf16[512,512]{1,0:T(8,128)(2,1)S(1)}, bf16[512,512]{1,0:T(8,128)(2,1)}, u32[]{:S(2)}, u32[]{:S(2)}) %collective-permute-start.29) | collective-permute-done | bytes 524320 | tf_op jit(solution)/shard_map/ppermute | solution.py:45
  167.2 3.8 convert_add_fusion
  171.6 5.5 %collective-permute-done.30 = bf16[512,512]{1,0:T(8,128)(2,1)} collective-permute-done((bf16[512,512]{1,0:T(8,128)(2,1)S(1)}, bf16[512,512]{1,0:T(8,128)(2,1)}, u32[]{:S(2)}, u32[]{:S(2)}) %collective-permute-start.30) | collective-permute-done | bytes 524320 | tf_op jit(solution)/shard_map/ppermute | solution.py:45
  179.0 4.5 shard_map.333
  193.9 3.7 multiply_convert_fusion.2
  217.0 15.6 %collective-permute-done.43.sent_ref = bf16[512,1024]{1,0:T(8,128)(2,1)S(1)} collective-permute-done((bf16[512,1024]{1,0:T(8,128)(2,1)S(1)}, bf16[512,1024]{1,0:T(8,128)(2,1)S(1)}, u32[]{:S(2)}, u32[]{:S(2)}) %collective-permute-start.43) | collective-permute-done | bytes 1048608 | tf_op jit(solution)/shard_map/ppermute | solution.py:94
  237.7 9.3 %shard_map.334 = bf16[4,2,256,1024]{3,2,1,0:T(8,128)(2,1)} custom-call(bf16[512,1024]{1,0:T(8,128)(2,1)} %pad_maximum_fusion.6.own_ref, bf16[512,1024]{1,0:T(8,128)(2,1)} %pad_maximum_fusion.7.far_ref, bf16[512,1024]{1,0:T(8,128)(2,1)} %pad_maximum_fusion.12.near_ref, bf16[512,1024]{1,0:T(8,128)(2,1)} %pad_maximum_fusion.13.far_near_ref, ...), custom_call_target="tpu_custom_call" | custom-call | flops 1000000 | bytes 1000000 | tf_op jit(solution)/shard_map/pallas_call | solution.py:613
  268.1 7.6 %shard_map.335 = (bf16[512,256]{1,0:T(8,128)(2,1)}, bf16[512,256]{1,0:T(8,128)(2,1)}, f32[512,1]{1,0:T(8,128)}) custom-call(f32[512,256]{1,0:T(8,128)} %fusion.56.query_ref, f32[512,256]{1,0:T(8,128)} %get-tuple-element.485.pair_ref, f32[512,128]{1,0:T(8,128)} %get-tuple-element.519.cosine_ref, f32[512,128]{1,0:T(8,128)} %get-tuple-element.520.sine_ref, ...), custom_call_target="tpu_custom_call" | custom-call | flops 100000000 | bytes 1000000 | tf_op jit(solution)/shard_map/pallas_call | solution.py:613
  280.8 29.0 %shard_map.336 = (bf16[512,1792]{1,0:T(8,128)(2,1)}, bf16[512,512]{1,0:T(8,128)(2,1)}, bf16[512,128]{1,0:T(8,128)(2,1)}, f32[4,768]{1,0:T(4,128)}, f32[4,512]{1,...) custom-call(f32[512,1536]{1,0:T(8,128)} %get-tuple-element.243.mix_ref, ...), custom_call_target="tpu_custom_call" | custom-call | flops 100000000 | bytes 1000000 | tf_op jit(solution)/shard_map/pallas_call | solution.py:613
  321.6 3.3 fusion.66
  328.7 12.8 %collective-permute-done.55 = bf16[512,896]{1,0:T(8,128)(2,1)S(1)} collective-permute-done((bf16[512,896]{1,0:T(8,128)(2,1)S(1)}, bf16[512,896]{1,0:T(8,128)(2,1)S(1)}, u32[]{:S(2)}, u32[]{:S(2)}) %collective-permute-start.55) | collective-permute-done | bytes 917536 | tf_op jit(solution)/shard_map/ppermute | solution.py:94
  365.9 6.0 %collective-permute-done.60 = bf16[512,384]{1,0:T(8,128)(2,1)S(1)} collective-permute-done((bf16[512,384]{1,0:T(8,128)(2,1)S(1)}, bf16[512,384]{1,0:T(8,128)(2,1)S(1)}, u32[]{:S(2)}, u32[]{:S(2)}) %collective-permute-start.60) | collective-permute-done | bytes 393248 | tf_op jit(solution)/shard_map/ppermute | solution.py:94
  380.1 3.2 broadcast_select_fusion.5
  392.7 3.3 collective-permute-start.69
  400.1 3.2 collective-permute-done.64
  415.3 26.3 %collective-permute-done.68 = bf16[2,2,128,1280]{3,2,1,0:T(8,128)(2,1)} collective-permute-done((bf16[2,2,128,1280]{3,2,1,0:T(8,128)(2,1)}, bf16[2,2,128,1280]{3,2,1,0:T(8,128)(2,1)}, u32[]{:S(2)}, u32[]{:S(2)}) %collective-permute-start.68) | collective-permute-done | bytes 1310752 | tf_op jit(solution)/shard_map/ppermute | solution.py:94
  441.6 4.4 collective-permute-start.70
  447.9 3.8 collective-permute-start.74
  457.2 5.9 %collective-permute-start.80 = (bf16[2,128,1280]{2,1,0:T(8,128)(2,1)}, bf16[2,128,1280]{2,1,0:T(8,128)(2,1)}, u32[]{:S(2)}, u32[]{:S(2)}) collective-permute-start(bf16[2,128,1280]{2,1,0:T(8,128)(2,1)} %dynamic-slice_bitcast_fusion.4), channel_id=1, source_target_pairs={{0,16},{4,20},{8,24},{12,28},{16,0},{20,4},{24,8},{28,12},{1,17},{... | collective-permute-start | bytes 1966088 | tf_op jit(solution)/shard_map/ppermute | solution.py:94
  465.6 16.8 %collective-permute-done.70 = bf16[512,1792]{1,0:T(8,128)(2,1)} collective-permute-done((bf16[512,1792]{1,0:T(8,128)(2,1)}, bf16[512,1792]{1,0:T(8,128)(2,1)}, u32[]{:S(2)}, u32[]{:S(2)}) %collective-permute-start.70) | collective-permute-done | bytes 1835040 | tf_op jit(solution)/shard_map/ppermute | solution.py:45
  487.1 5.7 %fusion = f32[512,1024]{1,0:T(8,128)S(1)} fusion(bf16[1024,3072]{1,0:T(8,128)(2,1)} %param.21, bf16[512,1536]{1,0:T(8,128)(2,1)S(1)} %get-tuple-element.415, bf16[512,1536]{1,0:T(8,128)(2,1)S(1)} %get-tuple-element.414), kind=kOutput, calls=%fused_computation.4 | convolution fusion | flops 3227516928 | bytes 11534336 | tf_op jit(solution)/shard_map/dot_general | solution.py:33
  509.3 3.7 reduce-scatter.8.cloned.1.call-done
  519.0 4.7 collective-permute-start.84
  (603 shorter events, 267.7 us)
Async XLA Ops:
  7.2 371.7 %reduce-scatter.4.cloned.1.call-start = ((), (), s32[]{:S(2)}) async-start(), calls=%async_computation.3 | async-start | bytes 5242880 | tf_op jit(solution)/shard_map/reduce_scatter | solution.py:147
  23.4 32.6 %collective-permute-start.4 = (bf16[512,896]{1,0:T(8,128)(2,1)}, bf16[512,896]{1,0:T(8,128)(2,1)}, u32[]{:S(2)}, u32[]{:S(2)}) collective-permute-start(bf16[512,896]{1,0:T(8,128)(2,1)} %fusion.90), channel_id=1, source_target_pairs={{0,2},{2,0},{1,3},{3,1},{4,6},{6,4},{5,7},{7,5},{8,10},{10,8},{9,1... | collective-permute-start | bytes 2752520 | tf_op jit(solution)/shard_map/ppermute | solution.py:45
  27.4 26.1 %collective-permute-start.3 = (bf16[512,512]{1,0:T(8,128)(2,1)S(1)}, bf16[512,512]{1,0:T(8,128)(2,1)}, u32[]{:S(2)}, u32[]{:S(2)}) collective-permute-start(bf16[512,512]{1,0:T(8,128)(2,1)S(1)} %copy-done.24), channel_id=1, source_target_pairs={{0,4},{4,0},{8,12},{12,8},{16,20},{20,16},{24,28},{28,24},{1,5},{5... | collective-permute-start | bytes 1572872 | tf_op jit(solution)/shard_map/ppermute | solution.py:94
  29.5 30.4 %collective-permute-start.7 = (bf16[128,1024]{1,0:T(8,128)(2,1)}, bf16[128,1024]{1,0:T(8,128)(2,1)S(1)}, u32[]{:S(2)}, u32[]{:S(2)}) collective-permute-start(bf16[128,1024]{1,0:T(8,128)(2,1)} %collective-permute-done.1.refs_0_), channel_id=1, source_target_pairs={{0,16},{4,20},{8,24},{12,28},{16,0},{20,4},{24,8},{28,12},{1,17},{... | collective-permute-start | bytes 786440 | tf_op jit(solution)/shard_map/ppermute | solution.py:94
  33.2 28.2 %collective-permute-start.8 = (bf16[128,1024]{1,0:T(8,128)(2,1)}, bf16[128,1024]{1,0:T(8,128)(2,1)S(1)}, u32[]{:S(2)}, u32[]{:S(2)}) collective-permute-start(bf16[128,1024]{1,0:T(8,128)(2,1)} %collective-permute-done.1.refs_0_), channel_id=1, source_target_pairs={{0,8},{4,12},{8,0},{12,4},{16,24},{20,28},{24,16},{28,20},{1,9},{5... | collective-permute-start | bytes 786440 | tf_op jit(solution)/shard_map/ppermute | solution.py:94
  53.5 25.8 %collective-permute-start.10 = (bf16[128,2048]{1,0:T(8,128)(2,1)}, bf16[128,2048]{1,0:T(8,128)(2,1)}, u32[]{:S(2)}, u32[]{:S(2)}) collective-permute-start(bf16[128,2048]{1,0:T(8,128)(2,1)} %collective-permute-done.2.refs_0_), channel_id=1, source_target_pairs={{0,16},{4,20},{8,24},{12,28},{16,0},{20,4},{24,8},{28,12},{1,17},{... | collective-permute-start | bytes 1572872 | tf_op jit(solution)/shard_map/ppermute | solution.py:94
  56.1 43.8 %collective-permute-start.17 = (bf16[512,1536]{1,0:T(8,128)(2,1)}, bf16[512,1536]{1,0:T(8,128)(2,1)}, u32[]{:S(2)}, u32[]{:S(2)}) collective-permute-start(bf16[512,1536]{1,0:T(8,128)(2,1)} %fusion.8), channel_id=1, source_target_pairs={{0,2},{2,0},{1,3},{3,1},{4,6},{6,4},{5,7},{7,5},{8,10},{10,8},{9,1... | collective-permute-start | bytes 4718600 | tf_op jit(solution)/shard_map/ppermute | solution.py:45
  59.8 25.3 %collective-permute-start.11 = (bf16[128,2048]{1,0:T(8,128)(2,1)}, bf16[128,2048]{1,0:T(8,128)(2,1)}, u32[]{:S(2)}, u32[]{:S(2)}) collective-permute-start(bf16[128,2048]{1,0:T(8,128)(2,1)} %collective-permute-done.2.refs_0_), channel_id=1, source_target_pairs={{0,8},{4,12},{8,0},{12,4},{16,24},{20,28},{24,16},{28,20},{1,9},{5... | collective-permute-start | bytes 1572872 | tf_op jit(solution)/shard_map/ppermute | solution.py:94
  61.4 24.2 %collective-permute-start.12 = (bf16[128,2048]{1,0:T(8,128)(2,1)}, bf16[128,2048]{1,0:T(8,128)(2,1)}, u32[]{:S(2)}, u32[]{:S(2)}) collective-permute-start(bf16[128,2048]{1,0:T(8,128)(2,1)} %collective-permute-done.2.refs_0_), channel_id=1, source_target_pairs={{0,4},{4,0},{8,12},{12,8},{16,20},{20,16},{24,28},{28,24},{1,5},{5... | collective-permute-start | bytes 1572872 | tf_op jit(solution)/shard_map/ppermute | solution.py:94
  63.1 25.7 %collective-permute-start.13 = (bf16[128,1024]{1,0:T(8,128)(2,1)}, bf16[128,1024]{1,0:T(8,128)(2,1)S(1)}, u32[]{:S(2)}, u32[]{:S(2)}) collective-permute-start(bf16[128,1024]{1,0:T(8,128)(2,1)} %copy-done.76), channel_id=1, source_target_pairs={{0,8},{4,12},{8,0},{12,4},{16,24},{20,28},{24,16},{28,20},{1,9},{5... | collective-permute-start | bytes 786440 | tf_op jit(solution)/shard_map/ppermute | solution.py:94
  99.8 30.6 %collective-permute-start.20 = (bf16[512,1024]{1,0:T(8,128)(2,1)}, bf16[512,1024]{1,0:T(8,128)(2,1)}, u32[]{:S(2)}, u32[]{:S(2)}) collective-permute-start(bf16[512,1024]{1,0:T(8,128)(2,1)} %fusion.45), channel_id=1, source_target_pairs={{0,2},{2,0},{1,3},{3,1},{4,6},{6,4},{5,7},{7,5},{8,10},{10,8},{9,1... | collective-permute-start | bytes 3145736 | tf_op jit(solution)/shard_map/ppermute | solution.py:45
  101.6 34.7 %collective-permute-start.22 = (bf16[128,2048]{1,0:T(8,128)(2,1)}, bf16[128,2048]{1,0:T(8,128)(2,1)}, u32[]{:S(2)}, u32[]{:S(2)}) collective-permute-start(bf16[128,2048]{1,0:T(8,128)(2,1)} %collective-permute-done.10.refs_1_), channel_id=1, source_target_pairs={{0,8},{4,12},{8,0},{12,4},{16,24},{20,28},{24,16},{28,20},{1,9},{5... | collective-permute-start | bytes 1572872 | tf_op jit(solution)/shard_map/ppermute | solution.py:94
  103.4 33.0 %collective-permute-start.23 = (bf16[128,2048]{1,0:T(8,128)(2,1)}, bf16[128,2048]{1,0:T(8,128)(2,1)}, u32[]{:S(2)}, u32[]{:S(2)}) collective-permute-start(bf16[128,2048]{1,0:T(8,128)(2,1)} %collective-permute-done.10.refs_1_), channel_id=1, source_target_pairs={{0,4},{4,0},{8,12},{12,8},{16,20},{20,16},{24,28},{28,24},{1,5},{5... | collective-permute-start | bytes 1572872 | tf_op jit(solution)/shard_map/ppermute | solution.py:94
  104.9 31.4 %collective-permute-start.24 = (bf16[128,2048]{1,0:T(8,128)(2,1)}, bf16[128,2048]{1,0:T(8,128)(2,1)}, u32[]{:S(2)}, u32[]{:S(2)}) collective-permute-start(bf16[128,2048]{1,0:T(8,128)(2,1)} %collective-permute-done.11.refs_2_), channel_id=1, source_target_pairs={{0,4},{4,0},{8,12},{12,8},{16,20},{20,16},{24,28},{28,24},{1,5},{5... | collective-permute-start | bytes 1572872 | tf_op jit(solution)/shard_map/ppermute | solution.py:94
  184.8 24.6 %collective-permute-start.41 = (bf16[512,512]{1,0:T(8,128)(2,1)S(1)}, bf16[512,512]{1,0:T(8,128)(2,1)S(1)}, u32[]{:S(2)}, u32[]{:S(2)}) collective-permute-start(bf16[512,512]{1,0:T(8,128)(2,1)S(1)} %copy-done.34), channel_id=1, source_target_pairs={{0,4},{4,0},{8,12},{12,8},{16,20},{20,16},{24,28},{28,24},{1,5},{5... | collective-permute-start | bytes 1572872 | tf_op jit(solution)/shard_map/ppermute | solution.py:94
  205.5 71.4 %collective-permute-start.65 = (bf16[512,512]{1,0:T(8,128)(2,1)}, bf16[512,512]{1,0:T(8,128)(2,1)}, u32[]{:S(2)}, u32[]{:S(2)}) collective-permute-start(bf16[512,512]{1,0:T(8,128)(2,1)} %collective-permute-done.3), channel_id=1, source_target_pairs={{0,1},{1,0},{2,3},{3,2},{4,5},{5,4},{6,7},{7,6},{8,9},{9,8},{10,11... | collective-permute-start | bytes 1572872 | tf_op jit(solution)/shard_map/ppermute | solution.py:45
  207.7 24.9 %collective-permute-start.43 = (bf16[512,1024]{1,0:T(8,128)(2,1)S(1)}, bf16[512,1024]{1,0:T(8,128)(2,1)S(1)}, u32[]{:S(2)}, u32[]{:S(2)}) collective-permute-start(bf16[512,1024]{1,0:T(8,128)(2,1)S(1)} %get-tuple-element.436), channel_id=1, source_target_pairs={{0,4},{4,0},{8,12},{12,8},{16,20},{20,16},{24,28},{28,24},{1,5},{5... | collective-permute-start | bytes 3145736 | tf_op jit(solution)/shard_map/ppermute | solution.py:94
  252.4 257.0 %reduce-scatter.6.cloned.1.call-start = ((), (), s32[]{:S(2)}) async-start(), calls=%async_computation.4 | async-start | bytes 2621440 | tf_op jit(solution)/shard_map/reduce_scatter | solution.py:147
  258.1 57.5 %collective-permute-start.54 = (bf16[512,2048]{1,0:T(8,128)(2,1)}, bf16[512,2048]{1,0:T(8,128)(2,1)}, u32[]{:S(2)}, u32[]{:S(2)}) collective-permute-start(bf16[512,2048]{1,0:T(8,128)(2,1)} %constant_dynamic-update-slice_fusion), channel_id=1, source_target_pairs={{0,4},{4,0},{8,12},{12,8},{16,20},{20,16},{24,28},{28,24},{1,5},{5... | collective-permute-start | bytes 6291464 | tf_op jit(solution)/shard_map/ppermute | solution.py:94
  275.7 39.9 %collective-permute-start.53 = (bf16[512,512]{1,0:T(8,128)(2,1)}, bf16[512,512]{1,0:T(8,128)(2,1)}, u32[]{:S(2)}, u32[]{:S(2)}) collective-permute-start(bf16[512,512]{1,0:T(8,128)(2,1)} %pad_maximum_fusion.17), channel_id=1, source_target_pairs={{0,2},{2,0},{1,3},{3,1},{4,6},{6,4},{5,7},{7,5},{8,10},{10,8},{9,1... | collective-permute-start | bytes 1572872 | tf_op jit(solution)/shard_map/ppermute | solution.py:45
  328.6 51.4 %collective-permute-start.62 = (bf16[512,512]{1,0:T(8,128)(2,1)}, bf16[512,512]{1,0:T(8,128)(2,1)}, u32[]{:S(2)}, u32[]{:S(2)}) collective-permute-start(bf16[512,512]{1,0:T(8,128)(2,1)} %get-tuple-element.432), channel_id=1, source_target_pairs={{0,1},{1,0},{2,3},{3,2},{4,5},{5,4},{6,7},{7,6},{8,9},{9,8},{10,11... | collective-permute-start | bytes 1572872 | tf_op jit(solution)/shard_map/ppermute | solution.py:45
  342.8 36.2 %collective-permute-start.61 = (bf16[512,1024]{1,0:T(8,128)(2,1)}, bf16[512,1024]{1,0:T(8,128)(2,1)}, u32[]{:S(2)}, u32[]{:S(2)}) collective-permute-start(bf16[512,1024]{1,0:T(8,128)(2,1)} %pad_maximum_fusion.14), channel_id=1, source_target_pairs={{0,2},{2,0},{1,3},{3,1},{4,6},{6,4},{5,7},{7,5},{8,10},{10,8},{9,1... | collective-permute-start | bytes 3145736 | tf_op jit(solution)/shard_map/ppermute | solution.py:45
  347.8 38.2 %collective-permute-start.63 = (bf16[2,2,128,896]{3,2,1,0:T(8,128)(2,1)}, bf16[2,2,128,896]{3,2,1,0:T(8,128)(2,1)}, u32[]{:S(2)}, u32[]{:S(2)}) collective-permute-start(bf16[2,2,128,896]{3,2,1,0:T(8,128)(2,1)} %get-tuple-element.437), channel_id=1, source_target_pairs={{0,8},{4,12},{8,0},{12,4},{16,24},{20,28},{24,16},{28,20},{1,9},{5... | collective-permute-start | bytes 2752520 | tf_op jit(solution)/shard_map/ppermute | solution.py:94
  376.9 64.7 %collective-permute-start.68 = (bf16[2,2,128,1280]{3,2,1,0:T(8,128)(2,1)}, bf16[2,2,128,1280]{3,2,1,0:T(8,128)(2,1)}, u32[]{:S(2)}, u32[]{:S(2)}) collective-permute-start(bf16[2,2,128,1280]{3,2,1,0:T(8,128)(2,1)} %get-tuple-element.420), channel_id=1, source_target_pairs={{0,8},{4,12},{8,0},{12,4},{16,24},{20,28},{24,16},{28,20},{1,9},{5... | collective-permute-start | bytes 3932168 | tf_op jit(solution)/shard_map/ppermute | solution.py:94
  379.0 24.3 %collective-permute-start.64 = (bf16[512,1024]{1,0:T(8,128)(2,1)}, bf16[512,1024]{1,0:T(8,128)(2,1)}, u32[]{:S(2)}, u32[]{:S(2)}) collective-permute-start(bf16[512,1024]{1,0:T(8,128)(2,1)} %get-tuple-element.274), channel_id=1, source_target_pairs={{0,2},{2,0},{1,3},{3,1},{4,6},{6,4},{5,7},{7,5},{8,10},{10,8},{9,1... | collective-permute-start | bytes 3145736 | tf_op jit(solution)/shard_map/ppermute | solution.py:45
  392.7 48.9 %collective-permute-start.69 = (bf16[2,128,896]{2,1,0:T(8,128)(2,1)}, bf16[2,128,896]{2,1,0:T(8,128)(2,1)}, u32[]{:S(2)}, u32[]{:S(2)}) collective-permute-start(bf16[2,128,896]{2,1,0:T(8,128)(2,1)} %dynamic-slice_bitcast_fusion.6), channel_id=1, source_target_pairs={{0,16},{4,20},{8,24},{12,28},{16,0},{20,4},{24,8},{28,12},{1,17},{... | collective-permute-start | bytes 1376264 | tf_op jit(solution)/shard_map/ppermute | solution.py:94
  396.1 116.9 %reduce-scatter.8.cloned.1.call-start = ((), (), s32[]{:S(2)}) async-start(), calls=%async_computation.5 | async-start | bytes 2621440 | tf_op jit(solution)/shard_map/reduce_scatter | solution.py:147
  415.3 47.8 %collective-permute-start.67 = (bf16[512,512]{1,0:T(8,128)(2,1)}, bf16[512,512]{1,0:T(8,128)(2,1)}, u32[]{:S(2)}, u32[]{:S(2)}) collective-permute-start(bf16[512,512]{1,0:T(8,128)(2,1)} %dynamic-slice_convert_fusion.1), channel_id=1, source_target_pairs={{0,1},{1,0},{2,3},{3,2},{4,5},{5,4},{6,7},{7,6},{8,9},{9,8},{10,11... | collective-permute-start | bytes 1572872 | tf_op jit(solution)/shard_map/ppermute | solution.py:45
  441.6 40.8 %collective-permute-start.70 = (bf16[512,1792]{1,0:T(8,128)(2,1)}, bf16[512,1792]{1,0:T(8,128)(2,1)}, u32[]{:S(2)}, u32[]{:S(2)}) collective-permute-start(bf16[512,1792]{1,0:T(8,128)(2,1)} %get-tuple-element.289), channel_id=1, source_target_pairs={{0,2},{2,0},{1,3},{3,1},{4,6},{6,4},{5,7},{7,5},{8,10},{10,8},{9,1... | collective-permute-start | bytes 5505032 | tf_op jit(solution)/shard_map/ppermute | solution.py:45
  447.9 48.0 %collective-permute-start.74 = (bf16[128,896]{1,0:T(8,128)(2,1)}, bf16[128,896]{1,0:T(8,128)(2,1)}, u32[]{:S(2)}, u32[]{:S(2)}) collective-permute-start(bf16[128,896]{1,0:T(8,128)(2,1)} %dynamic-slice_bitcast_fusion.8), channel_id=1, source_target_pairs={{0,4},{4,0},{8,12},{12,8},{16,20},{20,16},{24,28},{28,24},{1,5},{5... | collective-permute-start | bytes 688136 | tf_op jit(solution)/shard_map/ppermute | solution.py:94
  453.6 47.5 %collective-permute-start.78 = (bf16[2,128,1024]{2,1,0:T(8,128)(2,1)}, bf16[2,128,1024]{2,1,0:T(8,128)(2,1)}, u32[]{:S(2)}, u32[]{:S(2)}) collective-permute-start(bf16[2,128,1024]{2,1,0:T(8,128)(2,1)} %pad_maximum_fusion.18), channel_id=1, source_target_pairs={{0,2},{2,0},{1,3},{3,1},{4,6},{6,4},{5,7},{7,5},{8,10},{10,8},{9,1... | collective-permute-start | bytes 1572872 | tf_op jit(solution)/shard_map/ppermute | solution.py:45
  457.2 55.8 %collective-permute-start.80 = (bf16[2,128,1280]{2,1,0:T(8,128)(2,1)}, bf16[2,128,1280]{2,1,0:T(8,128)(2,1)}, u32[]{:S(2)}, u32[]{:S(2)}) collective-permute-start(bf16[2,128,1280]{2,1,0:T(8,128)(2,1)} %dynamic-slice_bitcast_fusion.4), channel_id=1, source_target_pairs={{0,16},{4,20},{8,24},{12,28},{16,0},{20,4},{24,8},{28,12},{1,17},{... | collective-permute-start | bytes 1966088 | tf_op jit(solution)/shard_map/ppermute | solution.py:94
  (170 other events, 1570.8 us)
Sparse Core Ops, SparseCore 0:
  252.5 76.0 reduce-scatter.3
  396.2 57.1 reduce-scatter.5
  463.3 49.6 reduce-scatter.7

commit v6 on v5

--- a/solution.py
+++ b/solution.py
@@ -1091,7 +1091,7 @@
         (outer_sum(first_far, grads_kept) + outer_sum(first_far_near, grads_send)).astype(bf16),
         True,
     )
-    late_far, mixer_scatter_far.parts = spine.wait(late_far, mixer_scatter_far.parts)
+    late_far = spine.wait(late_far)
     half = shared_width // 2
     late_sum = (
         late[:, : half + pair_width].astype(f32) + late_far[:, : half + pair_width].astype(f32)

time: 554 us -> 587 us (1.060)
  the two profiles are of different devices: /device:TPU:0 before, /device:TPU:9 now
where the time goes in v6:
time: 587 us; the launch traced here: 577 us
  waiting for transfers between devices  194 us (33%)
  other arithmetic  90.4 us (15%)
  starting transfers between devices  75.2 us (13%)
  Pallas kernels  74.3 us (13%)
  matrix products  72.6 us (12%)
  local copies, waits for them, and re-layouts  54.3 us (9%)
  between operations  16 us (3%)
    ppermute x32, waiting for transfers between devices, swap_dp(): lax.ppermute(values_in, 'dp', [(i, i ^ bit) for i in range(lax.axis_size(...  126 us
    pallas_call x5, Pallas kernels, call(): pl.pallas_call(kernel, out_shape=outs, in_specs=[pl.BlockSpec(memory_spac...  66.8 us
    ppermute x54, waiting for transfers between devices, swap(): return lax.ppermute(values_in, axis, [(0, 1), (1, 0)])  60.5 us
    ppermute x54, starting transfers between devices, swap(): return lax.ppermute(values_in, axis, [(0, 1), (1, 0)])  46.2 us
    dot_general x14, matrix products, product(): return jnp.dot(left_side, right_side, preferred_element_type=f32)  31.7 us
    ppermute x32, starting transfers between devices, swap_dp(): lax.ppermute(values_in, 'dp', [(i, i ^ bit) for i in range(lax.axis_size(...  28.4 us
    select_n x23, other arithmetic, in_order(): jnp.where(place == 0, own, other)  27.1 us
    dot_general x12, matrix products, product_back(): lax.dot_general(left_side, right_side, (((1,), (1,)), ((), ())), preferre...  24.8 us
  transfers between devices with their start and end apart: 89, of which 22 were waited for; matrix products, arithmetic and copies ran while one was open for 34% of the time, Pallas kernels for 13%

profile of v6, /device:TPU:9, one launch (start us, length us, event | category | flops | bytes accessed | tf_op | source)
XLA Modules:
  0.0 576.9 jit_solution(12965481818028051367)
XLA Ops:
  31.0 5.3 fusion.8
  36.4 14.0 %collective-permute-done.6 = f32[512]{0:T(512)S(1)} collective-permute-done((f32[512]{0:T(512)S(1)}, f32[512]{0:T(512)S(1)}, u32[]{:S(2)}, u32[]{:S(2)}) %collective-permute-start.6) | collective-permute-done | bytes 2080 | tf_op jit(solution)/shard_map/ppermute | solution.py:45
  62.8 14.2 %collective-permute-done.10.refs_1_ = bf16[128,2048]{1,0:T(8,128)(2,1)} collective-permute-done((bf16[128,2048]{1,0:T(8,128)(2,1)}, bf16[128,2048]{1,0:T(8,128)(2,1)}, u32[]{:S(2)}, u32[]{:S(2)}) %collective-permute-start.10) | collective-permute-done | bytes 524320 | tf_op jit(solution)/shard_map/ppermute | solution.py:94
  78.5 4.3 collective-permute-start.19
  85.9 4.4 collective-permute-done.15.refs_6_
  93.1 4.0 shard_map.330.attended_ref
  103.3 5.3 fusion.6.own_ref
  109.5 16.8 %shard_map.331 = (bf16[512,1024]{1,0:T(8,128)(2,1)}, f32[512,1]{1,0:T(8,128)}, f32[512,1536]{1,0:T(8,128)}, f32[512,768]{1,0:T(8,128)}, bf16[1024,768]{1,0:T(8,128)(2,1)}) custom-call(f32[512,1536]{1,0:T(8,128)} %fusion.6.own_ref, bf16[512,1536]{1,0:T(8,128)(2,1)} %collective-permute-done.17.other_ref, f32[512,1]{1,0:T(8,128)} %copy.81.factor_ref, ...), custom_call_target="tpu_custom_call" | custom-call | flops 100000000 | bytes 1000000 | tf_op jit(solution)/shard_map/pallas_call | solution.py:613
  130.7 3.1 shard_map.332
  140.6 2.8 fusion.31
  146.7 6.6 %collective-permute-done.27.refs_7_ = bf16[128,2048]{1,0:T(8,128)(2,1)S(1)} collective-permute-done((bf16[128,2048]{1,0:T(8,128)(2,1)}, bf16[128,2048]{1,0:T(8,128)(2,1)S(1)}, u32[]{:S(2)}, u32[]{:S(2)}) %collective-permute-start.27) | collective-permute-done | bytes 524320 | tf_op jit(solution)/shard_map/ppermute | solution.py:94
  153.3 4.7 collective-permute-done.29
  164.7 7.2 %collective-permute-done.30 = bf16[512,512]{1,0:T(8,128)(2,1)} collective-permute-done((bf16[512,512]{1,0:T(8,128)(2,1)}, bf16[512,512]{1,0:T(8,128)(2,1)}, u32[]{:S(2)}, u32[]{:S(2)}) %collective-permute-start.30) | collective-permute-done | bytes 524320 | tf_op jit(solution)/shard_map/ppermute | solution.py:45
  175.2 3.5 convert_add_fusion
  178.7 4.5 shard_map.333
  191.8 3.7 multiply_convert_fusion.2
  216.4 13.8 %collective-permute-done.43.sent_ref = bf16[512,1024]{1,0:T(8,128)(2,1)S(1)} collective-permute-done((bf16[512,1024]{1,0:T(8,128)(2,1)S(1)}, bf16[512,1024]{1,0:T(8,128)(2,1)S(1)}, u32[]{:S(2)}, u32[]{:S(2)}) %collective-permute-start.43) | collective-permute-done | bytes 1048608 | tf_op jit(solution)/shard_map/ppermute | solution.py:94
  236.1 9.3 %shard_map.334 = bf16[4,2,256,1024]{3,2,1,0:T(8,128)(2,1)} custom-call(bf16[512,1024]{1,0:T(8,128)(2,1)} %pad_maximum_fusion.6.own_ref, bf16[512,1024]{1,0:T(8,128)(2,1)} %pad_maximum_fusion.7.far_ref, bf16[512,1024]{1,0:T(8,128)(2,1)} %pad_maximum_fusion.12.near_ref, bf16[512,1024]{1,0:T(8,128)(2,1)} %pad_maximum_fusion.13.far_near_ref, ...), custom_call_target="tpu_custom_call" | custom-call | flops 1000000 | bytes 1000000 | tf_op jit(solution)/shard_map/pallas_call | solution.py:613
  261.0 2.9 fusion.29
  270.0 7.6 %shard_map.335 = (bf16[512,256]{1,0:T(8,128)(2,1)}, bf16[512,256]{1,0:T(8,128)(2,1)}, f32[512,1]{1,0:T(8,128)}) custom-call(f32[512,256]{1,0:T(8,128)} %fusion.57.query_ref, f32[512,256]{1,0:T(8,128)} %get-tuple-element.484.pair_ref, f32[512,128]{1,0:T(8,128)} %get-tuple-element.518.cosine_ref, f32[512,128]{1,0:T(8,128)} %get-tuple-element.519.sine_ref, ...), custom_call_target="tpu_custom_call" | custom-call | flops 100000000 | bytes 1000000 | tf_op jit(solution)/shard_map/pallas_call | solution.py:613
  282.9 29.1 %shard_map.336 = (bf16[512,1792]{1,0:T(8,128)(2,1)}, bf16[512,512]{1,0:T(8,128)(2,1)}, bf16[512,128]{1,0:T(8,128)(2,1)}, f32[4,768]{1,0:T(4,128)}, f32[4,512]{1,...) custom-call(f32[512,1536]{1,0:T(8,128)} %get-tuple-element.242.mix_ref, ...), custom_call_target="tpu_custom_call" | custom-call | flops 100000000 | bytes 1000000 | tf_op jit(solution)/shard_map/pallas_call | solution.py:613
  323.7 3.3 fusion.63
  330.3 12.9 %collective-permute-done.55 = bf16[512,896]{1,0:T(8,128)(2,1)S(1)} collective-permute-done((bf16[512,896]{1,0:T(8,128)(2,1)S(1)}, bf16[512,896]{1,0:T(8,128)(2,1)S(1)}, u32[]{:S(2)}, u32[]{:S(2)}) %collective-permute-start.55) | collective-permute-done | bytes 917536 | tf_op jit(solution)/shard_map/ppermute | solution.py:94
  362.4 6.1 %collective-permute-done.59 = bf16[512,384]{1,0:T(8,128)(2,1)S(1)} collective-permute-done((bf16[512,384]{1,0:T(8,128)(2,1)S(1)}, bf16[512,384]{1,0:T(8,128)(2,1)S(1)}, u32[]{:S(2)}, u32[]{:S(2)}) %collective-permute-start.59) | collective-permute-done | bytes 393248 | tf_op jit(solution)/shard_map/ppermute | solution.py:94
  375.1 3.5 broadcast_select_fusion.5
  393.1 59.7 %collective-permute-done.63 = bf16[2,2,128,896]{3,2,1,0:T(8,128)(2,1)} collective-permute-done((bf16[2,2,128,896]{3,2,1,0:T(8,128)(2,1)}, bf16[2,2,128,896]{3,2,1,0:T(8,128)(2,1)}, u32[]{:S(2)}, u32[]{:S(2)}) %collective-permute-start.63) | collective-permute-done | bytes 917536 | tf_op jit(solution)/shard_map/ppermute | solution.py:94
  455.1 5.5 collective-permute-start.69
  472.9 3.7 collective-permute-start.67
  488.3 30.3 %collective-permute-done.70 = bf16[512,1792]{1,0:T(8,128)(2,1)} collective-permute-done((bf16[512,1792]{1,0:T(8,128)(2,1)}, bf16[512,1792]{1,0:T(8,128)(2,1)}, u32[]{:S(2)}, u32[]{:S(2)}) %collective-permute-start.70) | collective-permute-done | bytes 1835040 | tf_op jit(solution)/shard_map/ppermute | solution.py:45
  524.0 3.4 fusion
  540.6 7.7 %reduce-scatter.8.cloned.1.call-done = bf16[256,1024]{1,0:T(8,128)(2,1)} async-done(((bf16[1024,1024]{1,0:T(8,128)(2,1)}), bf16[256,1024]{1,0:T(8,128)(2,1)}) %reduce-scatter.8.cloned.1.call-update) | async-done | bytes 524304 | tf_op jit(solution)/shard_map/reduce_scatter | solution.py:147
  554.7 3.9 collective-permute-done.83
  (597 shorter events, 254.0 us)
Async XLA Ops:
  7.2 367.9 %reduce-scatter.4.cloned.1.call-start = ((), (), s32[]{:S(2)}) async-start(), calls=%async_computation.3 | async-start | bytes 5242880 | tf_op jit(solution)/shard_map/reduce_scatter | solution.py:147
  22.6 31.3 %collective-permute-start.4 = (bf16[512,896]{1,0:T(8,128)(2,1)}, bf16[512,896]{1,0:T(8,128)(2,1)}, u32[]{:S(2)}, u32[]{:S(2)}) collective-permute-start(bf16[512,896]{1,0:T(8,128)(2,1)} %fusion.91), channel_id=1, source_target_pairs={{0,2},{2,0},{1,3},{3,1},{4,6},{6,4},{5,7},{7,5},{8,10},{10,8},{9,1... | collective-permute-start | bytes 2752520 | tf_op jit(solution)/shard_map/ppermute | solution.py:45
  25.8 25.8 %collective-permute-start.3 = (bf16[512,512]{1,0:T(8,128)(2,1)S(1)}, bf16[512,512]{1,0:T(8,128)(2,1)}, u32[]{:S(2)}, u32[]{:S(2)}) collective-permute-start(bf16[512,512]{1,0:T(8,128)(2,1)S(1)} %copy-done.25), channel_id=1, source_target_pairs={{0,4},{4,0},{8,12},{12,8},{16,20},{20,16},{24,28},{28,24},{1,5},{5... | collective-permute-start | bytes 1572872 | tf_op jit(solution)/shard_map/ppermute | solution.py:94
  27.1 23.3 %collective-permute-start.6 = (f32[512]{0:T(512)S(1)}, f32[512]{0:T(512)S(1)}, u32[]{:S(2)}, u32[]{:S(2)}) collective-permute-start(f32[512]{0:T(512)S(1)} %add.372), channel_id=1, source_target_pairs={{0,2},{2,0},{1,3},{3,1},{4,6},{6,4},{5,7},{7,5},{8,10},{10,8},{9,1... | collective-permute-start | bytes 6152 | tf_op jit(solution)/shard_map/ppermute | solution.py:45
  27.3 30.1 %collective-permute-start.7 = (bf16[128,1024]{1,0:T(8,128)(2,1)}, bf16[128,1024]{1,0:T(8,128)(2,1)S(1)}, u32[]{:S(2)}, u32[]{:S(2)}) collective-permute-start(bf16[128,1024]{1,0:T(8,128)(2,1)} %collective-permute-done.1.refs_0_), channel_id=1, source_target_pairs={{0,16},{4,20},{8,24},{12,28},{16,0},{20,4},{24,8},{28,12},{1,17},{... | collective-permute-start | bytes 786440 | tf_op jit(solution)/shard_map/ppermute | solution.py:94
  30.8 26.8 %collective-permute-start.8 = (bf16[128,1024]{1,0:T(8,128)(2,1)}, bf16[128,1024]{1,0:T(8,128)(2,1)S(1)}, u32[]{:S(2)}, u32[]{:S(2)}) collective-permute-start(bf16[128,1024]{1,0:T(8,128)(2,1)} %collective-permute-done.1.refs_0_), channel_id=1, source_target_pairs={{0,8},{4,12},{8,0},{12,4},{16,24},{20,28},{24,16},{28,20},{1,9},{5... | collective-permute-start | bytes 786440 | tf_op jit(solution)/shard_map/ppermute | solution.py:94
  51.6 25.4 %collective-permute-start.10 = (bf16[128,2048]{1,0:T(8,128)(2,1)}, bf16[128,2048]{1,0:T(8,128)(2,1)}, u32[]{:S(2)}, u32[]{:S(2)}) collective-permute-start(bf16[128,2048]{1,0:T(8,128)(2,1)} %collective-permute-done.2.refs_0_), channel_id=1, source_target_pairs={{0,16},{4,20},{8,24},{12,28},{16,0},{20,4},{24,8},{28,12},{1,17},{... | collective-permute-start | bytes 1572872 | tf_op jit(solution)/shard_map/ppermute | solution.py:94
  53.9 44.4 %collective-permute-start.17 = (bf16[512,1536]{1,0:T(8,128)(2,1)}, bf16[512,1536]{1,0:T(8,128)(2,1)}, u32[]{:S(2)}, u32[]{:S(2)}) collective-permute-start(bf16[512,1536]{1,0:T(8,128)(2,1)} %fusion.8), channel_id=1, source_target_pairs={{0,2},{2,0},{1,3},{3,1},{4,6},{6,4},{5,7},{7,5},{8,10},{10,8},{9,1... | collective-permute-start | bytes 4718600 | tf_op jit(solution)/shard_map/ppermute | solution.py:45
  59.2 26.6 %collective-permute-start.13 = (bf16[128,1024]{1,0:T(8,128)(2,1)}, bf16[128,1024]{1,0:T(8,128)(2,1)S(1)}, u32[]{:S(2)}, u32[]{:S(2)}) collective-permute-start(bf16[128,1024]{1,0:T(8,128)(2,1)} %copy-done.74), channel_id=1, source_target_pairs={{0,8},{4,12},{8,0},{12,4},{16,24},{20,28},{24,16},{28,20},{1,9},{5... | collective-permute-start | bytes 786440 | tf_op jit(solution)/shard_map/ppermute | solution.py:94
  98.3 28.0 %collective-permute-start.20 = (bf16[512,1024]{1,0:T(8,128)(2,1)}, bf16[512,1024]{1,0:T(8,128)(2,1)}, u32[]{:S(2)}, u32[]{:S(2)}) collective-permute-start(bf16[512,1024]{1,0:T(8,128)(2,1)} %fusion.46), channel_id=1, source_target_pairs={{0,2},{2,0},{1,3},{3,1},{4,6},{6,4},{5,7},{7,5},{8,10},{10,8},{9,1... | collective-permute-start | bytes 3145736 | tf_op jit(solution)/shard_map/ppermute | solution.py:45
  99.7 34.1 %collective-permute-start.22 = (bf16[128,2048]{1,0:T(8,128)(2,1)}, bf16[128,2048]{1,0:T(8,128)(2,1)}, u32[]{:S(2)}, u32[]{:S(2)}) collective-permute-start(bf16[128,2048]{1,0:T(8,128)(2,1)} %collective-permute-done.10.refs_1_), channel_id=1, source_target_pairs={{0,8},{4,12},{8,0},{12,4},{16,24},{20,28},{24,16},{28,20},{1,9},{5... | collective-permute-start | bytes 1572872 | tf_op jit(solution)/shard_map/ppermute | solution.py:94
  99.7 34.1 %collective-permute-start.23 = (bf16[128,2048]{1,0:T(8,128)(2,1)}, bf16[128,2048]{1,0:T(8,128)(2,1)}, u32[]{:S(2)}, u32[]{:S(2)}) collective-permute-start(bf16[128,2048]{1,0:T(8,128)(2,1)} %collective-permute-done.10.refs_1_), channel_id=1, source_target_pairs={{0,4},{4,0},{8,12},{12,8},{16,20},{20,16},{24,28},{28,24},{1,5},{5... | collective-permute-start | bytes 1572872 | tf_op jit(solution)/shard_map/ppermute | solution.py:94
  100.6 33.2 %collective-permute-start.24 = (bf16[128,2048]{1,0:T(8,128)(2,1)}, bf16[128,2048]{1,0:T(8,128)(2,1)}, u32[]{:S(2)}, u32[]{:S(2)}) collective-permute-start(bf16[128,2048]{1,0:T(8,128)(2,1)} %collective-permute-done.11.refs_2_), channel_id=1, source_target_pairs={{0,4},{4,0},{8,12},{12,8},{16,20},{20,16},{24,28},{28,24},{1,5},{5... | collective-permute-start | bytes 1572872 | tf_op jit(solution)/shard_map/ppermute | solution.py:94
  184.3 23.9 %collective-permute-start.41 = (bf16[512,512]{1,0:T(8,128)(2,1)S(1)}, bf16[512,512]{1,0:T(8,128)(2,1)S(1)}, u32[]{:S(2)}, u32[]{:S(2)}) collective-permute-start(bf16[512,512]{1,0:T(8,128)(2,1)S(1)} %copy-done.35), channel_id=1, source_target_pairs={{0,4},{4,0},{8,12},{12,8},{16,20},{20,16},{24,28},{28,24},{1,5},{5... | collective-permute-start | bytes 1572872 | tf_op jit(solution)/shard_map/ppermute | solution.py:94
  203.7 75.2 %collective-permute-start.65 = (bf16[512,512]{1,0:T(8,128)(2,1)}, bf16[512,512]{1,0:T(8,128)(2,1)}, u32[]{:S(2)}, u32[]{:S(2)}) collective-permute-start(bf16[512,512]{1,0:T(8,128)(2,1)} %collective-permute-done.3), channel_id=1, source_target_pairs={{0,1},{1,0},{2,3},{3,2},{4,5},{5,4},{6,7},{7,6},{8,9},{9,8},{10,11... | collective-permute-start | bytes 1572872 | tf_op jit(solution)/shard_map/ppermute | solution.py:45
  205.7 24.5 %collective-permute-start.43 = (bf16[512,1024]{1,0:T(8,128)(2,1)S(1)}, bf16[512,1024]{1,0:T(8,128)(2,1)S(1)}, u32[]{:S(2)}, u32[]{:S(2)}) collective-permute-start(bf16[512,1024]{1,0:T(8,128)(2,1)S(1)} %get-tuple-element.437), channel_id=1, source_target_pairs={{0,4},{4,0},{8,12},{12,8},{16,20},{20,16},{24,28},{28,24},{1,5},{5... | collective-permute-start | bytes 3145736 | tf_op jit(solution)/shard_map/ppermute | solution.py:94
  249.2 291.3 %reduce-scatter.6.cloned.1.call-start = ((), (), s32[]{:S(2)}) async-start(), calls=%async_computation.4 | async-start | bytes 2621440 | tf_op jit(solution)/shard_map/reduce_scatter | solution.py:147
  260.1 55.9 %collective-permute-start.54 = (bf16[512,2048]{1,0:T(8,128)(2,1)}, bf16[512,2048]{1,0:T(8,128)(2,1)}, u32[]{:S(2)}, u32[]{:S(2)}) collective-permute-start(bf16[512,2048]{1,0:T(8,128)(2,1)} %constant_dynamic-update-slice_fusion), channel_id=1, source_target_pairs={{0,4},{4,0},{8,12},{12,8},{16,20},{20,16},{24,28},{28,24},{1,5},{5... | collective-permute-start | bytes 6291464 | tf_op jit(solution)/shard_map/ppermute | solution.py:94
  277.6 38.4 %collective-permute-start.53 = (bf16[512,512]{1,0:T(8,128)(2,1)}, bf16[512,512]{1,0:T(8,128)(2,1)}, u32[]{:S(2)}, u32[]{:S(2)}) collective-permute-start(bf16[512,512]{1,0:T(8,128)(2,1)} %pad_maximum_fusion.17), channel_id=1, source_target_pairs={{0,2},{2,0},{1,3},{3,1},{4,6},{6,4},{5,7},{7,5},{8,10},{10,8},{9,1... | collective-permute-start | bytes 1572872 | tf_op jit(solution)/shard_map/ppermute | solution.py:45
  329.7 45.4 %collective-permute-start.61 = (bf16[512,512]{1,0:T(8,128)(2,1)}, bf16[512,512]{1,0:T(8,128)(2,1)}, u32[]{:S(2)}, u32[]{:S(2)}) collective-permute-start(bf16[512,512]{1,0:T(8,128)(2,1)} %get-tuple-element.433), channel_id=1, source_target_pairs={{0,1},{1,0},{2,3},{3,2},{4,5},{5,4},{6,7},{7,6},{8,9},{9,8},{10,11... | collective-permute-start | bytes 1572872 | tf_op jit(solution)/shard_map/ppermute | solution.py:45
  330.3 44.8 %collective-permute-start.62 = (bf16[512,512]{1,0:T(8,128)(2,1)}, bf16[512,512]{1,0:T(8,128)(2,1)}, u32[]{:S(2)}, u32[]{:S(2)}) collective-permute-start(bf16[512,512]{1,0:T(8,128)(2,1)} %get-tuple-element.432), channel_id=1, source_target_pairs={{0,1},{1,0},{2,3},{3,2},{4,5},{5,4},{6,7},{7,6},{8,9},{9,8},{10,11... | collective-permute-start | bytes 1572872 | tf_op jit(solution)/shard_map/ppermute | solution.py:45
  344.5 30.6 %collective-permute-start.60 = (bf16[512,1024]{1,0:T(8,128)(2,1)}, bf16[512,1024]{1,0:T(8,128)(2,1)}, u32[]{:S(2)}, u32[]{:S(2)}) collective-permute-start(bf16[512,1024]{1,0:T(8,128)(2,1)} %pad_maximum_fusion.14), channel_id=1, source_target_pairs={{0,2},{2,0},{1,3},{3,1},{4,6},{6,4},{5,7},{7,5},{8,10},{10,8},{9,1... | collective-permute-start | bytes 3145736 | tf_op jit(solution)/shard_map/ppermute | solution.py:45
  373.7 102.9 %collective-permute-start.68 = (bf16[2,2,128,1280]{3,2,1,0:T(8,128)(2,1)}, bf16[2,2,128,1280]{3,2,1,0:T(8,128)(2,1)}, u32[]{:S(2)}, u32[]{:S(2)}) collective-permute-start(bf16[2,2,128,1280]{3,2,1,0:T(8,128)(2,1)} %get-tuple-element.418), channel_id=1, source_target_pairs={{0,8},{4,12},{8,0},{12,4},{16,24},{20,28},{24,16},{28,20},{1,9},{5... | collective-permute-start | bytes 3932168 | tf_op jit(solution)/shard_map/ppermute | solution.py:94
  383.7 69.1 %collective-permute-start.63 = (bf16[2,2,128,896]{3,2,1,0:T(8,128)(2,1)}, bf16[2,2,128,896]{3,2,1,0:T(8,128)(2,1)}, u32[]{:S(2)}, u32[]{:S(2)}) collective-permute-start(bf16[2,2,128,896]{3,2,1,0:T(8,128)(2,1)} %dynamic-slice_bitcast_fusion.2), channel_id=1, source_target_pairs={{0,8},{4,12},{8,0},{12,4},{16,24},{20,28},{24,16},{28,20},{1,9},{5... | collective-permute-start | bytes 2752520 | tf_op jit(solution)/shard_map/ppermute | solution.py:94
  383.8 76.8 %collective-permute-start.64 = (bf16[512,1024]{1,0:T(8,128)(2,1)}, bf16[512,1024]{1,0:T(8,128)(2,1)}, u32[]{:S(2)}, u32[]{:S(2)}) collective-permute-start(bf16[512,1024]{1,0:T(8,128)(2,1)} %get-tuple-element.273), channel_id=1, source_target_pairs={{0,2},{2,0},{1,3},{3,1},{4,6},{6,4},{5,7},{7,5},{8,10},{10,8},{9,1... | collective-permute-start | bytes 3145736 | tf_op jit(solution)/shard_map/ppermute | solution.py:45
  387.8 160.5 %reduce-scatter.8.cloned.1.call-start = ((), (), s32[]{:S(2)}) async-start(), calls=%async_computation.5 | async-start | bytes 2621440 | tf_op jit(solution)/shard_map/reduce_scatter | solution.py:147
  391.2 77.6 %collective-permute-start.66 = (bf16[2,128,1024]{2,1,0:T(8,128)(2,1)}, bf16[2,128,1024]{2,1,0:T(8,128)(2,1)}, u32[]{:S(2)}, u32[]{:S(2)}) collective-permute-start(bf16[2,128,1024]{2,1,0:T(8,128)(2,1)} %dynamic-slice_bitcast_fusion.4), channel_id=1, source_target_pairs={{0,4},{4,0},{8,12},{12,8},{16,20},{20,16},{24,28},{28,24},{1,5},{5... | collective-permute-start | bytes 1572872 | tf_op jit(solution)/shard_map/ppermute | solution.py:94
  455.1 28.4 %collective-permute-start.69 = (bf16[2,128,896]{2,1,0:T(8,128)(2,1)}, bf16[2,128,896]{2,1,0:T(8,128)(2,1)}, u32[]{:S(2)}, u32[]{:S(2)}) collective-permute-start(bf16[2,128,896]{2,1,0:T(8,128)(2,1)} %dynamic-slice_bitcast_fusion.5), channel_id=1, source_target_pairs={{0,16},{4,20},{8,24},{12,28},{16,0},{20,4},{24,8},{28,12},{1,17},{... | collective-permute-start | bytes 1376264 | tf_op jit(solution)/shard_map/ppermute | solution.py:94
  476.6 42.0 %collective-permute-start.70 = (bf16[512,1792]{1,0:T(8,128)(2,1)}, bf16[512,1792]{1,0:T(8,128)(2,1)}, u32[]{:S(2)}, u32[]{:S(2)}) collective-permute-start(bf16[512,1792]{1,0:T(8,128)(2,1)} %get-tuple-element.287), channel_id=1, source_target_pairs={{0,2},{2,0},{1,3},{3,1},{4,6},{6,4},{5,7},{7,5},{8,10},{10,8},{9,1... | collective-permute-start | bytes 5505032 | tf_op jit(solution)/shard_map/ppermute | solution.py:45
  479.5 53.9 %collective-permute-start.78 = (bf16[2,128,1024]{2,1,0:T(8,128)(2,1)}, bf16[2,128,1024]{2,1,0:T(8,128)(2,1)}, u32[]{:S(2)}, u32[]{:S(2)}) collective-permute-start(bf16[2,128,1024]{2,1,0:T(8,128)(2,1)} %pad_maximum_fusion.18), channel_id=1, source_target_pairs={{0,2},{2,0},{1,3},{3,1},{4,6},{6,4},{5,7},{7,5},{8,10},{10,8},{9,1... | collective-permute-start | bytes 1572872 | tf_op jit(solution)/shard_map/ppermute | solution.py:45
  483.5 64.8 %collective-permute-start.80 = (bf16[2,128,1280]{2,1,0:T(8,128)(2,1)}, bf16[2,128,1280]{2,1,0:T(8,128)(2,1)}, u32[]{:S(2)}, u32[]{:S(2)}) collective-permute-start(bf16[2,128,1280]{2,1,0:T(8,128)(2,1)} %dynamic-slice_bitcast_fusion.3), channel_id=1, source_target_pairs={{0,16},{4,20},{8,24},{12,28},{16,0},{20,4},{24,8},{28,12},{1,17},{... | collective-permute-start | bytes 1966088 | tf_op jit(solution)/shard_map/ppermute | solution.py:94
  485.0 45.1 %collective-permute-start.74 = (bf16[128,896]{1,0:T(8,128)(2,1)S(1)}, bf16[128,896]{1,0:T(8,128)(2,1)S(1)}, u32[]{:S(2)}, u32[]{:S(2)}) collective-permute-start(bf16[128,896]{1,0:T(8,128)(2,1)S(1)} %dynamic-slice_bitcast_fusion.7), channel_id=1, source_target_pairs={{0,4},{4,0},{8,12},{12,8},{16,20},{20,16},{24,28},{28,24},{1,5},{5... | collective-permute-start | bytes 688136 | tf_op jit(solution)/shard_map/ppermute | solution.py:94
  (167 other events, 1407.2 us)
Sparse Core Ops, SparseCore 0:
  249.4 77.2 reduce-scatter.3
  387.9 69.8 reduce-scatter.5
  483.7 64.5 reduce-scatter.7
